TPU v7x, 32 devices: a whole 2x2x4 slice. The times are simulated.
32 devices in a mesh: batch: 4 (over z), seq: 4 (over y, x), head: 2 (over core).
Axes of the slice: x: 2, y: 2, z: 4, core: 2. Of those that a mesh axis runs over, the one named last changes fastest.
Arguments:
- hidden: bfloat16 [8, 1024, 2048], P('batch', 'seq'), may hold values from -6 to 6
- norm_gain: float32 [2048], replicated, may hold values from 0.5 to 1.5
- gate_input_weight: bfloat16 [2048, 2, 4096], P(None, None, 'head'), may hold values from -0.125 to 0.125
- w_bc: bfloat16 [2048, 256], replicated, may hold values from -0.125 to 0.125
- w_dt: bfloat16 [2048, 64], P(None, 'head'), may hold values from -0.125 to 0.125
- conv_x: float32 [5, 4096], P(None, 'head'), may hold values from -3 to 3
- conv_bc: float32 [5, 256], replicated, may hold values from -3 to 3
- head_params: float32 [3, 64], P(None, 'head'), as said below
- gate_gain: float32 [4096], P('head'), may hold values from 0.5 to 1.5
- w_out: bfloat16 [4096, 2048], P('head'), may hold values from -0.09375 to 0.09375
- lengths: int32 [8], P('batch'), may hold values from 256 to 1024, as said below
- cotangent: bfloat16 [8, 1024, 2048], P('batch', 'seq'), may hold values from -6 to 6
Outputs:
- mixed_out: bfloat16 [8, 1024, 2048], P('batch', 'seq')
- grad_hidden: float32 [8, 1024, 2048], P('batch', 'seq')
- grad_norm_gain: float32 [2048], replicated
- gradient_gate_input_weight: float32 [2048, 2, 4096], P(('batch', 'seq'), None, 'head')
- grad_w_bc: float32 [2048, 256], P(('batch', 'seq'))
- grad_w_dt: float32 [2048, 64], P(('batch', 'seq'), 'head')
- grad_conv_x: float32 [5, 4096], P(None, 'head')
- grad_conv_bc: float32 [5, 256], replicated
- grad_head_params: float32 [3, 64], P(None, 'head')
- grad_gate_gain: float32 [4096], P('head')
- grad_w_out: float32 [4096, 2048], P('head', ('batch', 'seq'))
Inputs may be any that keep to these rules, and one draw needn't show every extreme that they name: `lengths`: in each aligned group of 2 sequences (those of one index of batch) exactly one sequence, chosen at random, has length 1024; the others are uniform between the bounds. Slots at or past a sequence's length are padding. `head_params`: row 1 is the logarithm of a positive decay rate; rows 0 and 2 are real numbers of order one.
All inputs are finite; a program needn't handle non-finite values.
Results may differ from a plain program's by a relative error of at most 0.0081.
Values sent between devices are 32-bit elements; how exact they have to be, the bound alone decides.
A program may use at most 192 MiB of HBM per device.

v0:
```python
import jax
import jax.numpy as jnp
from jax import lax
from jax.sharding import PartitionSpec as P

CONV = 4
SPAN = 256


TOP_PRECISION = lax.Precision.HIGHEST
EPSILON = 1e-05


def shifted(value, axis, steps):
    count = lax.axis_size(axis)
    initial, last = (max(0, -steps), min(count, count - steps))
    return lax.ppermute(value, axis, [(source, source + steps) for source in range(initial, last)])


def entering_2(part, axis, combine, identity, reverse):
    count = lax.axis_size(axis)
    place = lax.axis_index(axis)
    ahead = count - 1 - place if reverse else place
    gathered = jax.tree.map(lambda a: lax.all_gather(a, axis), part)
    state = jax.tree.map(lambda a, e: jnp.zeros_like(a) + jnp.asarray(e, a.dtype), part, identity)

    def one(turn, state):
        source = count - 1 - turn if reverse else turn
        return combine(
            state, jax.tree.map(lambda a: lax.dynamic_index_in_dim(a, source, 0, False), gathered)
        )

    return lax.fori_loop(0, ahead, one, state)


def state_space(x_act, step_dt, decay_a, b_act, c_act, state_in):
    batch, slots = (x_act.shape[0], x_act.shape[1])
    blocks = slots // SPAN

    def cut_blocks(value):
        return jnp.moveaxis(value.reshape((batch, blocks, SPAN) + value.shape[2:]), 1, 0)

    causal = jnp.arange(SPAN)[:, None] >= jnp.arange(SPAN)[None, :]

    def block_step(state, pieces):
        x_blk, dt_blk, b_blk, c_blk = pieces
        cumul = jnp.cumsum(dt_blk * decay_a, axis=1)
        spread = cumul[:, :, None, :] - cumul[:, None, :, :]
        mask_ij = causal[None, :, :, None]
        decay = jnp.where(mask_ij, jnp.exp(jnp.where(mask_ij, spread, 0.0)), 0.0)
        scores = jnp.einsum("bin,bjn->bij", c_blk, b_blk, precision=TOP_PRECISION)
        weights = scores[..., None] * decay * dt_blk[:, None, :, :]
        result = jnp.einsum("bijh,bjhp->bihp", weights, x_blk, precision=TOP_PRECISION)
        result = (
            result
            + jnp.einsum("bin,bhpn->bihp", c_blk, state, precision=TOP_PRECISION)
            * jnp.exp(cumul)[..., None]
        )
        last = cumul[:, -1, :]
        tail = jnp.exp(last[:, None, :] - cumul) * dt_blk
        state = jnp.exp(last)[:, :, None, None] * state + jnp.einsum(
            "bjh,bjhp,bjn->bhpn", tail, x_blk, b_blk, precision=TOP_PRECISION
        )
        return (state, result)

    state_out, results = lax.scan(
        jax.checkpoint(block_step),
        state_in,
        (cut_blocks(x_act), cut_blocks(step_dt), cut_blocks(b_act), cut_blocks(c_act)),
    )
    return (jnp.moveaxis(results, 0, 1).reshape(x_act.shape), state_out)


def chain_combine(earlier, later):
    return (earlier[0] * later[0], later[0][:, :, None, None] * earlier[1] + later[1])


def silu_slope(value):
    sig = jax.nn.sigmoid(value)
    return sig * (1.0 + value * (1.0 - sig))


def per_device(
    hidden,
    norm_gain,
    gate_input_weight,
    w_bc,
    w_dt,
    conv_x,
    conv_bc,
    head_params,
    gate_gain,
    w_out,
    lengths,
    cotangent,
):
    seqs, slots, model = hidden.shape
    inner_dev = gate_input_weight.shape[2]
    heads_dev = w_dt.shape[1]
    width = inner_dev // heads_dev
    state_size = w_bc.shape[1] // 2
    inner_all = inner_dev * lax.axis_size("head")
    positions = lax.axis_index("seq") * slots + jnp.arange(slots)
    mask = (positions[None, :] < lengths[:, None]).astype(jnp.float32)
    hidden_f = hidden.astype(jnp.float32)
    inv_rms = lax.rsqrt(jnp.mean(hidden_f * hidden_f, axis=-1, keepdims=True) + EPSILON)
    normalized_rows = (hidden_f * inv_rms * norm_gain).astype(jnp.bfloat16)
    projected_gate_input = jnp.einsum(
        "eqg,gjn->eqjn", normalized_rows, gate_input_weight, preferred_element_type=jnp.float32
    )
    proj_bc = jnp.einsum("btd,dc->btc", normalized_rows, w_bc, preferred_element_type=jnp.float32)
    proj_dt = jnp.einsum("btd,dh->bth", normalized_rows, w_dt, preferred_element_type=jnp.float32)
    gate_z = projected_gate_input[:, :, 0]
    pre_conv = jnp.concatenate([projected_gate_input[:, :, 1], proj_bc], axis=-1)
    conv_all = jnp.concatenate([conv_x, conv_bc], axis=1)
    edge_rows = shifted(pre_conv[:, slots - (CONV - 1) :], "seq", 1)
    extended = jnp.concatenate([edge_rows, pre_conv], axis=1)
    summed = conv_all[CONV] + extended[:, 0:slots] * conv_all[0]
    for tap in range(1, CONV):
        summed = summed + extended[:, tap : tap + slots] * conv_all[tap]
    active = jax.nn.silu(summed)
    x_act = active[..., :inner_dev].reshape(seqs, slots, heads_dev, width)
    b_act = active[..., inner_dev : inner_dev + state_size]
    c_act = active[..., inner_dev + state_size :]
    step_arg = proj_dt + head_params[0]
    step_dt = jax.nn.softplus(step_arg)
    decay_a = -jnp.exp(head_params[1])
    zero_state = jnp.zeros((seqs, heads_dev, width, state_size), jnp.float32)
    local_out, local_state = state_space(x_act, step_dt, decay_a, b_act, c_act, zero_state)
    cumul_all = jnp.cumsum(step_dt * decay_a, axis=1)
    total_decay = jnp.exp(cumul_all[:, -1, :])
    identity = (jnp.ones_like(total_decay), jnp.zeros_like(local_state))
    entering = entering_2((total_decay, local_state), "seq", chain_combine, identity, False)[1]
    growth = jnp.exp(cumul_all)
    ssm_out = (
        local_out
        + jnp.einsum("btn,bhpn->bthp", c_act, entering, precision=TOP_PRECISION) * growth[..., None]
    )
    ssm_out = ssm_out + head_params[2][:, None] * x_act
    ssm_flat = ssm_out.reshape(seqs, slots, inner_dev)
    gate_silu = jax.nn.silu(gate_z)
    gated = ssm_flat * gate_silu
    squares = lax.psum(jnp.sum(gated * gated, axis=-1), "head")
    gate_rms = lax.rsqrt(squares / inner_all + EPSILON)[..., None]
    gate_normed = gated * gate_rms
    gate_out = (gate_normed * gate_gain).astype(jnp.bfloat16)
    mixed_part = jnp.einsum("bti,id->btd", gate_out, w_out, preferred_element_type=jnp.float32)
    mixed = lax.psum(mixed_part, "head")
    mixed_out = (mask[..., None] * (hidden_f + mixed)).astype(jnp.bfloat16)
    grad_mix = (cotangent.astype(jnp.float32) * mask[..., None]).astype(jnp.bfloat16)
    grad_w_out = jnp.einsum("bti,btd->id", gate_out, grad_mix, preferred_element_type=jnp.float32)
    grad_gate_out = jnp.einsum("btd,id->bti", grad_mix, w_out, preferred_element_type=jnp.float32)
    grad_gate_gain = jnp.sum(grad_gate_out * gate_normed, axis=(0, 1))
    grad_normed_gate = grad_gate_out * gate_gain
    gate_dot = lax.psum(jnp.sum(grad_normed_gate * gate_normed, axis=-1), "head")
    grad_gated = gate_rms * (grad_normed_gate - gate_normed * (gate_dot / inner_all)[..., None])
    grad_ssm = (grad_gated * gate_silu).reshape(seqs, slots, heads_dev, width)
    grad_z = grad_gated * ssm_flat * silu_slope(gate_z)
    grad_skip = jnp.sum(grad_ssm * x_act, axis=(0, 1, 3))
    leaving = jnp.einsum("bth,bthp,btn->bhpn", growth, grad_ssm, c_act, precision=TOP_PRECISION)
    coming = entering_2((total_decay, leaving), "seq", chain_combine, identity, True)[1]

    def local_chain(x_in, dt_in, decay_in, b_in, c_in):
        return state_space(x_in, dt_in, decay_in, b_in, c_in, entering)

    unused, pullback = jax.vjp(local_chain, x_act, step_dt, decay_a, b_act, c_act)
    grad_x, grad_dt, grad_decay, grad_b, grad_c = pullback((grad_ssm, coming))
    grad_x = grad_x + grad_ssm * head_params[2][:, None]
    grad_b, grad_c = lax.psum((grad_b, grad_c), "head")
    grad_step = grad_dt * jax.nn.sigmoid(step_arg)
    grad_head = jnp.stack(
        [jnp.sum(grad_step, axis=(0, 1)), grad_decay * decay_a, grad_skip], axis=0
    )
    grad_active = jnp.concatenate([grad_x.reshape(seqs, slots, inner_dev), grad_b, grad_c], axis=-1)
    grad_summed = grad_active * silu_slope(summed)
    conv_rows = [
        jnp.sum(grad_summed * extended[:, tap : tap + slots], axis=(0, 1)) for tap in range(CONV)
    ]
    conv_rows.append(jnp.sum(grad_summed, axis=(0, 1)))
    grad_conv = jnp.stack(conv_rows, axis=0)
    grad_extended = jnp.pad(grad_summed * conv_all[0], ((0, 0), (0, CONV - 1), (0, 0)))
    for tap in range(1, CONV):
        grad_extended = grad_extended + jnp.pad(
            grad_summed * conv_all[tap], ((0, 0), (tap, CONV - 1 - tap), (0, 0))
        )
    from_next = shifted(grad_extended[:, : CONV - 1], "seq", -1)
    grad_pre = grad_extended[:, CONV - 1 :] + jnp.pad(
        from_next, ((0, 0), (slots - (CONV - 1), 0), (0, 0))
    )
    gradient_gate_input = jnp.stack([grad_z, grad_pre[..., :inner_dev]], axis=2).astype(
        jnp.bfloat16
    )
    grad_bc = grad_pre[..., inner_dev:].astype(jnp.bfloat16)
    grad_dtr = grad_step.astype(jnp.bfloat16)
    gradient_gate_input_weight = jnp.einsum(
        "ewl,ewhx->lhx", normalized_rows, gradient_gate_input, preferred_element_type=jnp.float32
    )
    grad_w_bc = jnp.einsum(
        "btd,btc->dc", normalized_rows, grad_bc, preferred_element_type=jnp.float32
    )
    grad_w_dt = jnp.einsum(
        "btd,bth->dh", normalized_rows, grad_dtr, preferred_element_type=jnp.float32
    )
    head_portion = jnp.einsum(
        "xhkr,ykr->xhy", gradient_gate_input, gate_input_weight, preferred_element_type=jnp.float32
    )
    head_portion = head_portion + jnp.einsum(
        "bth,dh->btd", grad_dtr, w_dt, preferred_element_type=jnp.float32
    )
    grad_normed = lax.psum(head_portion, "head")
    grad_normed = grad_normed + jnp.einsum(
        "btc,dc->btd", grad_bc, w_bc, preferred_element_type=jnp.float32
    )
    scaled_input = hidden_f * inv_rms
    grad_norm_gain = jnp.sum(grad_normed * scaled_input, axis=(0, 1))
    grad_scaled = grad_normed * norm_gain
    input_dot = jnp.mean(grad_scaled * scaled_input, axis=-1, keepdims=True)
    grad_hidden = grad_mix.astype(jnp.float32) + inv_rms * (grad_scaled - scaled_input * input_dot)
    gradient_gate_input_weight, grad_w_bc, grad_w_dt, grad_w_out = (
        lax.psum_scatter(
            gradient_gate_input_weight, ("batch", "seq"), scatter_dimension=0, tiled=True
        ),
        lax.psum_scatter(grad_w_bc, ("batch", "seq"), scatter_dimension=0, tiled=True),
        lax.psum_scatter(grad_w_dt, ("batch", "seq"), scatter_dimension=0, tiled=True),
        lax.psum_scatter(grad_w_out, ("batch", "seq"), scatter_dimension=1, tiled=True),
    )
    grad_conv, grad_head, grad_gate_gain, grad_norm_gain = lax.psum(
        (grad_conv, grad_head, grad_gate_gain, grad_norm_gain), ("batch", "seq")
    )
    grad_conv_x = grad_conv[:, :inner_dev]
    grad_conv_bc = grad_conv[:, inner_dev:]
    return (
        mixed_out,
        grad_hidden,
        grad_norm_gain,
        gradient_gate_input_weight,
        grad_w_bc,
        grad_w_dt,
        grad_conv_x,
        grad_conv_bc,
        grad_head,
        grad_gate_gain,
        grad_w_out,
    )


def solution(mesh):
    placed = (
        P("batch", "seq", None),
        P(),
        P(None, None, "head"),
        P(),
        P(None, "head"),
        P(None, "head"),
        P(),
        P(None, "head"),
        P("head"),
        P("head", None),
        P("batch"),
        P("batch", "seq", None),
    )
    return jax.shard_map(
        per_device,
        mesh=mesh,
        in_specs=placed,
        out_specs=(
            P("batch", "seq", None),
            P("batch", "seq", None),
            P(),
            P(("batch", "seq"), None, "head"),
            P(("batch", "seq"), None),
            P(("batch", "seq"), "head"),
            P(None, "head"),
            P(),
            P(None, "head"),
            P("head"),
            P("head", ("batch", "seq")),
        ),
        check_vma=False,
    )
```

profile of v0, /device:TPU:0, one launch (start us, length us, event | category | flops | bytes accessed | tf_op | source)
XLA Modules:
  0.0 1794.8 jit_solution(1038446950340171429)
XLA Ops:
  9.4 13.8 fusion.3
  23.3 2.9 fusion.147
  30.0 5.2 collective-permute-start
  43.7 4.2 fusion.41
  52.6 5.3 copy.170
  57.9 7.3 fusion.86
  65.4 5.4 copy.181
  71.6 8.4 all-gather
  83.2 5.9 fusion.99
  89.1 64.2 %all-gather.6.cloned.1.call-done = f32[8,32,64,128]{3,2,1,0:T(8,128)} async-done(((f32[2,32,64,128]{3,2,1,0:T(8,128)}), f32[8,32,64,128]{3,2,1,0:T(8,128)}) %all-gather.6.cloned.1.call-update) | async-done | bytes 8388624 | tf_op jit(solution)/shard_map/all_gather | solution.py:24
  153.6 4.6 fusion.108
  158.3 23.7 %multiply_reduce_fusion.10 = (f32[2,256]{1,0:T(2,128)S(1)}, f32[2,256,32,64]{1,3,2,0:T(8,128)}) fusion(f32[2,256,32,64]{1,3,2,0:T(8,128)} %bitcast.265, f32[2,256,32,64]{1,3,2,0:T(8,128)S(1)} %bitcast.257, f32[32]{0:T(128)S(1)} %copy-done.61, f32[2,256,32,64]{1,3,2,0:T(8,128)S(1)} %fusion.108, f32[2,256,32,64]{1,3,2,0:T(8,128)} %fusion.99, ...), kind=kOutput, calls=%fused_computation.112 | convolution fusion | flops 3255827968 | bytes 21760128 | tf_op jit(solution)/shard_map/while/body/eval_jaxpr/checkpoint/bijh,bjhp->bihp/dot_general | solution.py:53
  182.0 13.1 psum.70
  195.1 5.4 copy.180
  200.5 15.5 multiply_reduce_fusion.6
  218.4 11.8 multiply_reduce_fusion.7
  230.2 5.4 copy.183
  235.5 7.3 fusion.67
  244.9 11.2 fusion.22
  256.1 80.6 %all-gather.8.cloned.1.call-done = f32[8,32,64,128]{3,2,1,0:T(8,128)} async-done(((f32[2,32,64,128]{3,2,1,0:T(8,128)}), f32[8,32,64,128]{3,2,1,0:T(8,128)}) %all-gather.8.cloned.1.call-update) | async-done | bytes 8388624 | tf_op jit(solution)/shard_map/all_gather | solution.py:24
  338.2 11.4 while.17
  338.2 3.8 bitcast_add_fusion.9
  342.0 3.8 bitcast_add_fusion.9
  345.8 3.8 bitcast_add_fusion.9
  358.9 5.8 multiply_reduce_fusion.8
  365.6 5.0 multiply_reduce_fusion.5
  370.6 27.8 %fusion.18 = (f32[2,256,32]{1,2,0:T(8,128)}, f32[2,256,32]{1,2,0:T(8,128)}, f32[2,256,32]{1,2,0:T(8,128)}, f32[2,256,256]{2,1,0:T(8,128)}) fusion(f32[2,256,32]{1,2,0:T(8,128)S(1)} %copy-done.41, f32[2,256,32]{1,2,0:T(8,128)S(1)} %copy-done.43, f32[2,256,256]{2,1,0:T(8,128)S(1)} %fusion.149, pred[256,256]{1,0:T(8,128)(4,1)S(1)} %copy-done.48, ...), kind=kOutput, calls=%fused_computation.27 | convolution fusion | flops 3283959808 | bytes 9830400 | tf_op jit(solution)/shard_map/transpose(jvp())/while/body/eval_jaxpr/checkpoint/bijh,bjhp->bihp/dot_general | solution.py:53
  410.9 5.0 reduce-window.36
  423.7 8.9 fusion.92
  433.8 9.3 fusion.89
  446.2 17.9 bitcast_add_fusion.3
  464.1 5.5 copy.190
  469.7 6.8 multiply_add_fusion.1
  479.7 7.9 all-reduce.14.cloned.1.call-done
  487.7 12.8 fusion.143
  500.5 7.6 broadcast_multiply_fusion.3
  519.5 24.8 %bitcast_add_fusion.2 = f32[2,256,2048]{2,1,0:T(8,128)} fusion(f32[2,256,2048]{2,1,0:T(8,128)S(1)} %copy-done.18, bf16[2048,2,2048,1]{2,1,0,3:T(2,128)(2,1)} %bitcast.278, bf16[2,256,1,2048]{3,1,0,2:T(8,128)(2,1)} %slice_bitcast_fusion.1, bf16[2,256,1,2048]{3,1,0,2:T(8,128)(2,1)} %get-tuple-element.379), kind=kOutput, calls=%fused_computation.79 | convolution fusion | flops 8593080320 | bytes 29360128 | tf_op jit(solution)/shard_map/xhkr,ykr->xhy/dot_general | solution.py:204
  545.9 21.0 %convolution_bitcast_fusion = f32[2048,2,2048]{2,0,1:T(8,128)} fusion(bf16[2,256,1,2048]{3,1,0,2:T(8,128)(2,1)} %slice_bitcast_fusion.1, bf16[2,256,1,2048]{3,1,0,2:T(8,128)(2,1)} %get-tuple-element.379, bf16[2,256,2048]{2,1,0:T(8,128)(2,1)S(1)} %copy-done.14, f32[2048]{0:T(1024)S(1)} %copy-done.40, f32[2,256]{1,0:T(2,128)S(1)} %copy-done.52), kind=kOutput, calls=%fused_computation.26 | convolution fusion | flops 8602517504 | bytes 39856128 | tf_op jit(solution)/shard_map/ewl,ewhx->lhx/dot_general | solution.py:195
  568.5 3.3 convolution_bitcast_fusion.2
  571.9 14.6 convolution_bitcast_fusion.1
  588.3 5.7 fusion.47
  594.0 89.5 %all-reduce.6 = (f32[2048]{0:T(1024)}, f32[5,2304]{1,0:T(8,128)S(1)}, f32[3,32]{1,0:T(4,128)}, f32[2048]{0:T(1024)}) all-reduce(f32[2048]{0:T(1024)S(1)} %get-tuple-element.327, f32[5,2304]{1,0:T(8,128)S(1)} %stack.48, f32[3,32]{1,0:T(4,128)S(1)} %pad_maximum_fusion.4, ...), channel_id=1, replica_groups=mesh['batch'=4,'seq'=4,'head'=2] {'batch','seq'}, use_global_device_ids=true, to_apply=%region_28.29 | all-reduce | flops 15712 | bytes 125696 | tf_op jit(solution)/shard_map/psum | solution.py:227
  684.7 6.8 fusion.46
  691.4 585.4 %reduce-scatter.5.cloned.1.call-done = f32[128,2,2048]{2,0,1:T(8,128)} async-done(((f32[2048,2,2048]{2,0,1:T(8,128)}), f32[128,2,2048]{2,0,1:T(8,128)}) %reduce-scatter.5.cloned.1.call-update) | async-done | bytes 2097168 | tf_op jit(solution)/shard_map/reduce_scatter | solution.py:220
  1276.8 4.5 copy.208
  1281.4 79.9 %reduce-scatter.9.cloned.1.call-done = f32[128,32]{0,1:T(8,128)} async-done(((f32[2048,32]{0,1:T(8,128)}), f32[128,32]{0,1:T(8,128)}) %reduce-scatter.9.cloned.1.call-update) | async-done | bytes 16400 | tf_op jit(solution)/shard_map/reduce_scatter | solution.py:224
  1361.3 79.7 %reduce-scatter.7.cloned.1.call-done = f32[128,256]{1,0:T(8,128)} async-done(((f32[2048,256]{1,0:T(8,128)}), f32[128,256]{1,0:T(8,128)}) %reduce-scatter.7.cloned.1.call-update) | async-done | bytes 131088 | tf_op jit(solution)/shard_map/reduce_scatter | solution.py:223
  1441.0 346.5 %reduce-scatter.11.cloned.1.call-done = f32[2048,128]{1,0:T(8,128)} async-done(((f32[2048,2048]{1,0:T(8,128)}), f32[2048,128]{1,0:T(8,128)}) %reduce-scatter.11.cloned.1.call-update) | async-done | bytes 1048592 | tf_op jit(solution)/shard_map/reduce_scatter | solution.py:225
  (251 shorter events, 85.1 us)
Async XLA Ops:
  7.2 20.9 %copy-start = (bf16[2048,256]{1,0:T(8,128)(2,1)S(1)}, bf16[2048,256]{1,0:T(8,128)(2,1)}, u32[]{:S(2)}) copy-start(bf16[2048,256]{1,0:T(8,128)(2,1)} %param.19) | copy-start | bytes 3145732
  7.2 146.1 %all-gather.6.cloned.1.call-start = ((), (), s32[]{:S(2)}) async-start(), calls=%async_computation.8 | async-start | bytes 10485760 | tf_op jit(solution)/shard_map/all_gather | solution.py:24
  9.4 26.3 %copy-start.51 = (f32[2,256]{1,0:T(2,128)}, f32[2,256]{1,0:T(2,128)S(1)}, u32[]{:S(2)}) copy-start(f32[2,256]{1,0:T(2,128)S(1)} %add_rsqrt_fusion.1) | copy-start | bytes 6148
  28.1 7.1 copy-start.63
  28.1 7.6 copy-start.29
  28.9 14.2 copy-start.16
  28.9 10.2 copy-start.46
  30.0 10.0 copy-start.58
  30.0 10.3 collective-permute-start
  36.7 6.4 copy-start.19
  65.2 271.4 %all-gather.8.cloned.1.call-start = ((), (), s32[]{:S(2)}) async-start(), calls=%async_computation.9 | async-start | bytes 10485760 | tf_op jit(solution)/shard_map/all_gather | solution.py:24
  65.4 15.3 copy-start.64
  80.8 119.7 %copy-start.55 = (f32[2,256]{1,0:T(2,128)}, f32[2,256]{1,0:T(2,128)S(1)}, u32[]{:S(2)}) copy-start(f32[2,256]{1,0:T(2,128)S(1)} %compare_convert_fusion) | copy-start | bytes 6148
  195.1 5.4 copy-start.53
  235.5 7.3 copy-start.62
  242.8 244.8 %all-reduce.14.cloned.1.call-start = ((), (), s32[]{:S(2)}) async-start(), calls=%async_computation.11 | async-start | bytes 1048576 | tf_op jit(solution)/shard_map/psum | solution.py:169
  356.4 8.2 copy-start.2
  358.9 11.7 copy-start.26
  358.9 6.7 copy-start.7
  358.9 6.7 copy-start.22
  365.6 5.0 copy-start.5
  365.6 5.0 copy-start.41
  365.6 5.0 copy-start.43
  365.6 5.0 copy-start.48
  432.6 10.5 copy-start.23
  432.6 10.5 copy-start.24
  432.6 11.9 copy-start.21
  433.7 12.5 copy-start.27
  433.7 12.5 copy-start.42
  433.8 12.4 copy-start.44
  433.8 12.4 copy-start.49
  469.6 6.9 copy-start.20
  469.6 6.9 copy-start.25
  469.6 6.8 copy-start.60
  469.6 7.3 copy-start.30
  469.6 118.6 %all-reduce.12.cloned.1.call-start = ((), (), s32[]{:S(2)}) async-start(), calls=%async_computation.10 | async-start | bytes 16777216 | tf_op jit(solution)/shard_map/psum | solution.py:148
  476.5 11.2 copy-start.17
  487.6 12.8 copy-start.32
  487.6 12.8 copy-start.34
  487.6 12.8 copy-start.36
  487.6 12.8 copy-start.38
  508.1 5.3 copy-start.11
  509.2 6.8 collective-permute-start.1
  544.3 732.5 %reduce-scatter.5.cloned.1.call-start = ((), (), s32[]{:S(2)}) async-start(), calls=%async_computation.4 | async-start | bytes 35651584 | tf_op jit(solution)/shard_map/reduce_scatter | solution.py:220
  566.9 794.3 %reduce-scatter.9.cloned.1.call-start = ((), (), s32[]{:S(2)}) async-start(), calls=%async_computation.6 | async-start | bytes 278528 | tf_op jit(solution)/shard_map/reduce_scatter | solution.py:224
  568.4 872.5 %reduce-scatter.7.cloned.1.call-start = ((), (), s32[]{:S(2)}) async-start(), calls=%async_computation.5 | async-start | bytes 2228224 | tf_op jit(solution)/shard_map/reduce_scatter | solution.py:223
  571.8 1215.7 %reduce-scatter.11.cloned.1.call-start = ((), (), s32[]{:S(2)}) async-start(), calls=%async_computation.7 | async-start | bytes 17825792 | tf_op jit(solution)/shard_map/reduce_scatter | solution.py:225
  588.3 5.7 copy-start.57
  (27 other events, 91.6 us)
Sparse Core Ops, SparseCore 0:
  65.3 87.9 all-gather.5
  242.9 93.6 all-gather.7
  469.7 17.8 all-reduce.13
  544.4 40.0 all-reduce.11
  586.9 689.9 reduce-scatter.4
  1279.6 81.6 reduce-scatter.8
  1364.1 76.8 reduce-scatter.6
  1443.8 343.6 reduce-scatter.10
where the time goes:
time: 1800 us; the launch traced here: 1790 us
  waiting for transfers between devices  1250 us (69%)
  matrix products  246 us (14%)
  blocking collectives  113 us (6%)
  other arithmetic  91.9 us (5%)
  local copies, waits for them, and re-layouts  75.4 us (4%)
    reduce_scatter x1, waiting for transfers between devices, per_device(): lax.psum_scatter(gradient_gate_input_weight, ('batch', 'seq'), scatter_di...  585 us
    reduce_scatter x1, waiting for transfers between devices, per_device(): lax.psum_scatter(grad_w_out, ('batch', 'seq'), scatter_dimension=1, tiled...  347 us
    all_gather x2, waiting for transfers between devices, entering_2(): gathered = jax.tree.map(lambda a: lax.all_gather(a, axis), part)  145 us
    psum x1, blocking collectives, per_device(): lax.psum((grad_conv, grad_head, grad_gate_gain, grad_norm_gain), ('batch'...  89.5 us
    reduce_scatter x1, waiting for transfers between devices, per_device(): lax.psum_scatter(grad_w_dt, ('batch', 'seq'), scatter_dimension=0, tiled=...  79.9 us
    reduce_scatter x1, waiting for transfers between devices, per_device(): lax.psum_scatter(grad_w_bc, ('batch', 'seq'), scatter_dimension=0, tiled=...  79.7 us
    dot_general x3, matrix products, block_step(): jnp.einsum('bijh,bjhp->bihp', weights, x_blk, precision=TOP_PRECISION)  69.4 us
  transfers between devices with their start and end apart: 10, of which 8 were waited for; matrix products, arithmetic and copies ran while one was open for 6% of the time, Pallas kernels for 0%

commit v1 on v0

v1 whole, which is shorter than its diff:
```python
import functools

import jax
import jax.numpy as jnp
from jax import lax
from jax.experimental import pallas as pl
from jax.experimental.pallas import tpu as pltpu
from jax.sharding import PartitionSpec as P

CONV = 4
EDGE = 8
LANES = 256
EPSILON = 1e-05
HIGHEST = lax.Precision.HIGHEST
F32 = jnp.float32
BF16 = jnp.bfloat16
VMEM_LIMIT = 48 * 1024 * 1024


def mm(a, b, dims=((1,), (0,)), precision=None):
    return lax.dot_general(a, b, (dims, ((), ())), precision=precision, preferred_element_type=F32)


def widen(columns, width):
    slots, heads = columns.shape
    lane = lax.broadcasted_iota(jnp.int32, (slots, heads * width), 1) // width
    result = jnp.broadcast_to(columns[:, 0:1], (slots, heads * width))
    for head in range(1, heads):
        result = jnp.where(lane == head, columns[:, head : head + 1], result)
    return result


def head_sums(value, heads):
    lanes = value.shape[1]
    row = lax.broadcasted_iota(jnp.int32, (lanes, heads), 0) // (lanes // heads)
    pick = (row == lax.broadcasted_iota(jnp.int32, (lanes, heads), 1)).astype(BF16)
    high = value.astype(BF16)
    low = (value - high.astype(F32)).astype(BF16)
    return mm(high, pick) + mm(low, pick)


def triangle(slots):
    row = lax.broadcasted_iota(jnp.int32, (slots, slots), 0)
    column = lax.broadcasted_iota(jnp.int32, (slots, slots), 1)
    return (row >= column).astype(F32)


def softplus(value):
    return jnp.maximum(value, 0.0) + jnp.log1p(jnp.exp(-jnp.abs(value)))


def slope(value, sig):
    return sig * (1.0 + value * (1.0 - sig))


def convolved(extended, taps, slots):
    total = taps[CONV : CONV + 1] + extended[EDGE : EDGE + slots] * taps[CONV - 1 : CONV]
    for tap in range(CONV - 1):
        start = EDGE - (CONV - 1) + tap
        total = total + extended[start : start + slots] * taps[tap : tap + 1]
    return total


def convolved_back(grad, extended, taps):
    slots, lanes = grad.shape
    padded = jnp.concatenate([grad, jnp.zeros((EDGE, lanes), F32)], axis=0)
    back = grad * taps[CONV - 1 : CONV]
    rows = []
    for tap in range(CONV):
        start = EDGE - (CONV - 1) + tap
        rows.append(jnp.sum(grad * extended[start : start + slots], axis=0, keepdims=True))
        if tap < CONV - 1:
            ahead = CONV - 1 - tap
            back = back + padded[ahead : ahead + slots] * taps[tap : tap + 1]
    rows.append(jnp.sum(grad, axis=0, keepdims=True))
    rows.append(jnp.zeros((8 - len(rows), lanes), F32))
    return back, jnp.concatenate(rows, axis=0)


def of_head(value, head, heads):
    lane = lax.broadcasted_iota(jnp.int32, value.shape, 1) // (value.shape[1] // heads)
    return jnp.where(lane == head, value, jnp.zeros_like(value))


def local_kernel(
    heads, width, pre_x, edge_x, taps_x, pre_bc, edge_bc, taps_bc, dtraw, params,
    local_out, local_state, total_decay, b_out, c_out, steps_out, scores,
):
    slots = pre_x.shape[1]
    state = b_out.shape[2]
    tri = triangle(slots)

    @pl.when(pl.program_id(1) == 0)
    def _():
        ext = jnp.concatenate([edge_bc[0], pre_bc[0]], axis=0)
        u = convolved(ext, taps_bc[...], slots)
        act = u * jax.nn.sigmoid(u)
        b_out[0] = act[:, :state]
        c_out[0] = act[:, state:]
        scores[...] = mm(act[:, state:], act[:, :state], ((1,), (1,)), HIGHEST) * tri

    ext = jnp.concatenate([edge_x[0], pre_x[0]], axis=0)
    u = convolved(ext, taps_x[...], slots)
    x = u * jax.nn.sigmoid(u)
    par = params[0]
    step = softplus(dtraw[0, 0] + par[0:1])
    rate = step * -jnp.exp(par[1:2])
    cumul = mm(tri, rate, precision=HIGHEST)
    cumul_t = mm(rate, tri, ((0,), (1,)), precision=HIGHEST)
    steps_out[0, 0] = jnp.concatenate([step, cumul], axis=1)
    last = cumul[slots - 1 : slots]
    total_decay[0] = widen(jnp.exp(last), width)
    xd = (widen(step, width) * x).astype(BF16)
    tail = (widen(jnp.exp(last - cumul), width) * xd.astype(F32)).astype(BF16)
    local_state[0] = mm(b_out[0].astype(BF16), tail, ((0,), (0,)))
    out = widen(par[2:3], width) * x
    for head in range(heads):
        decay = jnp.exp(jnp.minimum(cumul[:, head : head + 1] - cumul_t[head : head + 1], 0.0))
        weights = (scores[...] * decay).astype(BF16)
        out = out + mm(weights, of_head(xd, head, heads))
    local_out[0] = out


def gate_kernel(heads, width, local_out, entering, c_act, steps, z, grad_out, gain, y_out, sums):
    cumul = steps[0, 0][:, heads:]
    inter = mm(c_act[0].astype(BF16), entering[0].astype(BF16))
    y = local_out[0] + widen(jnp.exp(cumul), width) * inter
    y_out[0] = y
    zv = z[0]
    g = y * (zv * jax.nn.sigmoid(zv))
    squares = jnp.sum(g * g, axis=1, keepdims=True)
    dots = jnp.sum(grad_out[0] * gain[...] * g, axis=1, keepdims=True)
    both = jnp.concatenate([squares, dots], axis=1)

    @pl.when(pl.program_id(1) == 0)
    def _():
        sums[0] = both

    @pl.when(pl.program_id(1) > 0)
    def _():
        sums[0] += both


def gate_back_kernel(
    heads, width, inner_all, y, z, grad_out, gain, sums, c_act, steps,
    gated_out, grad_y, grad_z, gain_grad, leaving,
):
    inv = lax.rsqrt(sums[0][:, 0:1] / inner_all + EPSILON)
    mean = inv * sums[0][:, 1:2] / inner_all
    zv, yv = z[0], y[0]
    sig = jax.nn.sigmoid(zv)
    silu = zv * sig
    normed = yv * silu * inv
    gated_out[0] = (normed * gain[...]).astype(BF16)
    gain_grad[0] = jnp.sum(grad_out[0] * normed, axis=0, keepdims=True)
    dg = inv * (grad_out[0] * gain[...] - normed * mean)
    dy = dg * silu
    grad_y[0] = dy
    grad_z[0] = (dg * yv * slope(zv, sig)).astype(BF16)
    growth = widen(jnp.exp(steps[0, 0][:, heads:]), width)
    leaving[0] = mm(c_act[0].astype(BF16), (growth * dy).astype(BF16), ((0,), (0,)))


def scan_back_kernel(
    heads, width, pre_x, edge_x, taps_x, dtraw, params, steps, b_act, c_act, y, grad_y, entering, coming,
    grad_pre, tail_rows, head_rows, taps_grad, grad_dt, params_grad, grad_bc, grad_scores, scores,
):
    slots = pre_x.shape[1]
    state = b_act.shape[2]
    tri = triangle(slots)
    first = pl.program_id(1) == 0

    @pl.when(first)
    def _():
        scores[...] = mm(c_act[0], b_act[0], ((1,), (1,)), HIGHEST) * tri
        grad_scores[...] = jnp.zeros_like(grad_scores)
        grad_bc[...] = jnp.zeros_like(grad_bc)

    ext = jnp.concatenate([edge_x[0], pre_x[0]], axis=0)
    u = convolved(ext, taps_x[...], slots)
    sig = jax.nn.sigmoid(u)
    x = u * sig
    par = params[0]
    decay_a = -jnp.exp(par[1:2])
    step = steps[0, 0][:, :heads]
    cumul = steps[0, 0][:, heads:]
    cumul_t = mm(step * decay_a, tri, ((0,), (1,)), precision=HIGHEST)
    last = cumul[slots - 1 : slots]
    step_wide = widen(step, width)
    tail_wide = widen(jnp.exp(last - cumul), width)
    growth = widen(jnp.exp(cumul), width)
    skip = widen(par[2:3], width)
    xd = (step_wide * x).astype(BF16)
    xd_f = xd.astype(F32)
    dy = grad_y[0]
    dy_b = dy.astype(BF16)
    coming_b = coming[0].astype(BF16)
    from_next = tail_wide * mm(b_act[0].astype(BF16), coming_b)
    grad_xd = from_next
    total = jnp.zeros((slots, slots), F32)
    for head in range(heads):
        decay = jnp.exp(jnp.minimum(cumul[:, head : head + 1] - cumul_t[head : head + 1], 0.0))
        weights = (scores[...] * decay).astype(BF16)
        mine = of_head(dy_b, head, heads)
        grad_xd = grad_xd + mm(weights, mine, ((0,), (0,)))
        total = total + mm(mine, xd, ((1,), (1,))) * decay
    grad_scores[...] += total
    grad_c = mm((growth * dy).astype(BF16), entering[0].astype(BF16), ((1,), (1,)))
    grad_b = mm((tail_wide * xd_f).astype(BF16), coming_b, ((1,), (1,)))
    grad_bc[0] += jnp.concatenate([grad_b, grad_c], axis=1)

    direct = head_sums(x * grad_xd, heads)
    ys = y[0] - skip * x
    moved = head_sums(dy_b.astype(F32) * ys - xd_f * grad_xd, heads)
    ends = jnp.exp(widen(last, width)) * jnp.sum(coming[0] * entering[0], axis=0, keepdims=True)
    ends = ends + jnp.sum(xd_f * from_next, axis=0, keepdims=True)
    skips = jnp.sum(dy * x, axis=0, keepdims=True)
    rows = head_sums(jnp.concatenate([ends, skips, jnp.zeros((6, ends.shape[1]), F32)], axis=0), heads)
    later = mm(tri, moved, ((0,), (0,)), precision=HIGHEST) + rows[0:1]
    grad_step = (direct + decay_a * later) * jax.nn.sigmoid(dtraw[0, 0] + par[0:1])
    grad_dt[0, 0] = grad_step
    params_grad[0, 0] = jnp.concatenate(
        [
            jnp.sum(grad_step, axis=0, keepdims=True),
            jnp.sum(step * later, axis=0, keepdims=True) * decay_a,
            rows[1:2],
        ],
        axis=0,
    )
    du = (step_wide * grad_xd + skip * dy) * slope(u, sig)
    back, rows8 = convolved_back(du, ext, taps_x[...])
    grad_pre[0] = back.astype(BF16)
    tail_rows[0] = back[slots - EDGE :]
    head_rows[0] = du[:EDGE]
    taps_grad[0] = rows8

    @pl.when(pl.program_id(1) == pl.num_programs(1) - 1)
    def _():
        causal = grad_scores[...] * tri
        from_c = mm(causal, c_act[0], ((0,), (0,)), HIGHEST)
        grad_bc[0] += jnp.concatenate([from_c, mm(causal, b_act[0], precision=HIGHEST)], axis=1)


def conv_back_kernel(pre, edge, taps, grad_act, grad_pre, tail_rows, head_rows, taps_grad):
    slots = pre.shape[1]
    ext = jnp.concatenate([edge[0], pre[0]], axis=0)
    u = convolved(ext, taps[...], slots)
    du = grad_act[0] * slope(u, jax.nn.sigmoid(u))
    back, rows8 = convolved_back(du, ext, taps[...])
    grad_pre[0] = back.astype(BF16)
    tail_rows[0] = back[slots - EDGE :]
    head_rows[0] = du[:EDGE]
    taps_grad[0] = rows8


def narrow_kernel(value, result):
    result[...] = value[...].astype(BF16)


def narrow(value):
    rows, columns = value.shape
    block = pl.BlockSpec((rows // 2, columns), lambda i: (i, 0))
    return pl.pallas_call(
        narrow_kernel,
        grid=(2,),
        in_specs=[block],
        out_specs=block,
        out_shape=jax.ShapeDtypeStruct(value.shape, BF16),
        name="narrow",
    )(value)


def swapped(value, axis, bit):
    count = lax.axis_size(axis)
    return lax.ppermute(value, axis, [(i, i ^ bit) for i in range(count)])


def shifted(value, axis, steps):
    count = lax.axis_size(axis)
    initial, last = (max(0, -steps), min(count, count - steps))
    return lax.ppermute(value, axis, [(source, source + steps) for source in range(initial, last)])


def head_sum(value):
    if lax.axis_size("head") == 2:
        return value + swapped(value, "head", 1)
    return lax.psum(value, "head")


def passed_on(decay, part, reverse):
    count = lax.axis_size("seq")
    place = lax.axis_index("seq")
    both = jnp.concatenate([part, jnp.broadcast_to(decay, (decay.shape[0], 8, decay.shape[2]))], axis=1)
    gathered = lax.all_gather(both, "seq")
    rows = part.shape[1]
    state = jnp.zeros_like(part)
    for turn in range(count - 1):
        source = count - 1 - turn if reverse else turn
        ahead = source > place if reverse else source < place
        later = gathered[source, :, rows : rows + 1] * state + gathered[source, :, :rows]
        state = jnp.where(ahead, later, state)
    return state


def halves(value, axis, which):
    size = value.shape[axis] // 2
    return lax.dynamic_slice_in_dim(value, which * size, size, axis)


def pair_rows(rows):
    side = lax.axis_index("head")
    mine = swapped(halves(rows, 1, side).astype(F32), "batch", 1)
    theirs = narrow(swapped(mine, "head", 1))
    mine = narrow(mine)
    low = jnp.where(side == 0, mine, theirs)
    high = jnp.where(side == 0, theirs, mine)
    return jnp.concatenate([rows, jnp.concatenate([low, high], axis=1)], axis=0)


def pair_columns(columns):
    parity = lax.axis_index("batch") % 2
    sent = halves(columns, 1, 1 - parity).astype(F32)
    got = narrow(swapped(sent, "batch", 1))
    return jnp.concatenate([halves(columns, 1, parity), got], axis=0)


def pair_grad(rows, columns):
    z, s = lax.axis_index("batch"), lax.axis_index("seq")
    parity, upper = z % 2, z // 2
    sx, sy = s % 2, s // 2
    block = rows.shape[1] // 16
    part = mm(rows, columns, ((0,), (0,)))
    part = part.reshape(4, 2, 2, block, columns.shape[1])
    half = columns.shape[1] // 2

    def pick(value, axis, index):
        return lax.dynamic_index_in_dim(value, index, axis, False)

    a, b = part[..., :half], part[..., half:]
    a = pick(a, 2, sx) + swapped(pick(a, 2, 1 - sx), "seq", 1)
    b = pick(b, 1, sy) + swapped(pick(b, 1, 1 - sy), "seq", 2)
    a = pick(a, 1, sy) + swapped(pick(a, 1, 1 - sy), "seq", 2)
    b = pick(b, 1, sx) + swapped(pick(b, 1, 1 - sx), "seq", 1)
    both = jnp.concatenate([a, b], axis=-1).reshape(2, 2, block, columns.shape[1])
    both = pick(both, 0, upper) + swapped(pick(both, 0, 1 - upper), "batch", 2)
    own = pick(both, 0, parity)
    other = swapped(pick(both, 0, 1 - parity), "batch", 1)
    low = jnp.where(parity == 0, own, other)
    high = jnp.where(parity == 0, other, own)
    return jnp.concatenate([low, high], axis=1)


def everywhere_sum(values):
    if lax.axis_size("batch") != 4 or lax.axis_size("seq") != 4:
        return lax.psum(values, ("batch", "seq"))
    for axis in ("seq", "batch"):
        for bit in (1, 2):
            values = values + swapped(values, axis, bit)
    return values


def per_device(
    hidden,
    norm_gain,
    gate_input_weight,
    w_bc,
    w_dt,
    conv_x,
    conv_bc,
    head_params,
    gate_gain,
    w_out,
    lengths,
    cotangent,
):
    seqs, slots, model = hidden.shape
    rows = seqs * slots
    inner = gate_input_weight.shape[2]
    heads_dev = w_dt.shape[1]
    width = inner // heads_dev
    state = w_bc.shape[1] // 2
    inner_all = inner * lax.axis_size("head")
    heads = LANES // width
    groups = inner // LANES
    side = lax.axis_index("head")
    paired = lax.axis_size("batch") == 4 and lax.axis_size("seq") == 4 and lax.axis_size("head") == 2

    positions = lax.axis_index("seq") * slots + jnp.arange(slots)
    mask = (positions[None, :] < lengths[:, None]).astype(F32).reshape(rows, 1)
    hidden_f = hidden.reshape(rows, model).astype(F32)
    inv_rms = lax.rsqrt(jnp.mean(hidden_f * hidden_f, axis=-1, keepdims=True) + EPSILON)
    normed = (hidden_f * inv_rms * norm_gain).astype(BF16)
    grad_mix = (cotangent.reshape(rows, model).astype(F32) * mask).astype(BF16)
    w_z, w_x = gate_input_weight[:, 0], gate_input_weight[:, 1]

    pre_x = mm(normed, w_x).reshape(seqs, slots, inner)
    pre_bc = mm(normed, w_bc).reshape(seqs, slots, 2 * state)
    proj_dt = mm(normed, w_dt)
    edges = jnp.concatenate([pre_x[:, slots - EDGE :], pre_bc[:, slots - EDGE :]], axis=2)
    edges = shifted(edges, "seq", 1)
    edge_x, edge_bc = edges[..., :inner], edges[..., inner:]
    dtraw = proj_dt.reshape(seqs, slots, groups, heads).transpose(0, 2, 1, 3)
    params = head_params.reshape(3, groups, heads).transpose(1, 0, 2)
    gain = gate_gain.reshape(1, inner)

    grid = (seqs, groups)
    S = jax.ShapeDtypeStruct
    wide = pl.BlockSpec((1, slots, LANES), lambda b, g: (b, 0, g))
    edge = pl.BlockSpec((1, EDGE, LANES), lambda b, g: (b, 0, g))
    states = pl.BlockSpec((1, state, LANES), lambda b, g: (b, 0, g))
    line = pl.BlockSpec((1, 1, LANES), lambda b, g: (b, 0, g))
    taps = pl.BlockSpec((CONV + 1, LANES), lambda b, g: (0, g))
    gain_spec = pl.BlockSpec((1, LANES), lambda b, g: (0, g))
    per_seq = lambda *shape: pl.BlockSpec((1,) + shape, lambda b, g: (b,) + (0,) * len(shape))
    fixed = lambda *shape: pl.BlockSpec(shape, lambda b, g: (0,) * len(shape))
    by_head = lambda k: pl.BlockSpec((1, 1, slots, k), lambda b, g: (b, g, 0, 0))
    par_spec = pl.BlockSpec((1, 3, heads), lambda b, g: (g, 0, 0))
    wide_s = S((seqs, slots, inner), F32)
    wide_b = S((seqs, slots, inner), BF16)
    state_s = S((seqs, state, inner), F32)
    bc_b = S((seqs, slots, state), F32)
    settings = pltpu.CompilerParams(vmem_limit_bytes=VMEM_LIMIT)

    local_out, local_state, total_decay, b_act, c_act, steps = pl.pallas_call(
        functools.partial(local_kernel, heads, width),
        grid=grid,
        in_specs=[
            wide, edge, taps, per_seq(slots, 2 * state), per_seq(EDGE, 2 * state),
            fixed(CONV + 1, 2 * state), by_head(heads), par_spec,
        ],
        out_specs=[wide, states, line, per_seq(slots, state), per_seq(slots, state), by_head(2 * heads)],
        out_shape=[
            wide_s, state_s, S((seqs, 1, inner), F32), bc_b, bc_b,
            S((seqs, groups, slots, 2 * heads), F32),
        ],
        scratch_shapes=[pltpu.VMEM((slots, slots), F32)],
        compiler_params=settings,
        name="scan_local",
    )(pre_x, edge_x, conv_x, pre_bc, edge_bc, conv_bc, dtraw, params)

    entering = passed_on(total_decay, local_state, False)
    gate_z = mm(normed, w_z).reshape(seqs, slots, inner)
    grad_out = mm(grad_mix, w_out, ((1,), (1,))).reshape(seqs, slots, inner)

    y, sums = pl.pallas_call(
        functools.partial(gate_kernel, heads, width),
        grid=grid,
        in_specs=[wide, states, per_seq(slots, state), by_head(2 * heads), wide, wide, gain_spec],
        out_specs=[wide, per_seq(slots, 2)],
        out_shape=[wide_s, S((seqs, slots, 2), F32)],
        compiler_params=settings,
        name="gate",
    )(local_out, entering, c_act, steps, gate_z, grad_out, gain)
    sums = head_sum(sums)

    gated, grad_y, grad_z, gain_grad, leaving = pl.pallas_call(
        functools.partial(gate_back_kernel, heads, width, inner_all),
        grid=grid,
        in_specs=[wide, wide, wide, gain_spec, per_seq(slots, 2), per_seq(slots, state), by_head(2 * heads)],
        out_specs=[wide, wide, wide, line, states],
        out_shape=[wide_b, wide_s, wide_b, S((seqs, 1, inner), F32), state_s],
        compiler_params=settings,
        name="gate_back",
    )(y, gate_z, grad_out, gain, sums, c_act, steps)
    gated = gated.reshape(rows, inner)
    grad_z = grad_z.reshape(rows, inner)

    coming = passed_on(total_decay, leaving, True)

    if paired:
        mix_rows = pair_rows(grad_mix)
        normed_rows = pair_rows(normed)
        grad_w_out = pair_grad(mix_rows, pair_columns(gated)).T
        grad_w_z = pair_grad(normed_rows, pair_columns(grad_z))

    mixed = head_sum(mm(gated, w_out))
    mixed_out = (mask * (hidden_f + mixed)).astype(BF16).reshape(seqs, slots, model)

    (
        grad_pre, tail_x, first_x, taps_grad_x, grad_dt, params_grad, grad_bc,
    ) = pl.pallas_call(
        functools.partial(scan_back_kernel, heads, width),
        grid=grid,
        in_specs=[
            wide, edge, taps, by_head(heads), par_spec, by_head(2 * heads), per_seq(slots, state),
            per_seq(slots, state), wide, wide, states, states,
        ],
        out_specs=[
            wide, edge, edge, edge, by_head(heads),
            pl.BlockSpec((1, 1, 3, heads), lambda b, g: (b, g, 0, 0)), per_seq(slots, 2 * state),
        ],
        out_shape=[
            wide_b, S((seqs, EDGE, inner), F32), S((seqs, EDGE, inner), F32), S((seqs, EDGE, inner), F32),
            S((seqs, groups, slots, heads), F32), S((seqs, groups, 3, heads), F32),
            S((seqs, slots, 2 * state), F32),
        ],
        scratch_shapes=[pltpu.VMEM((slots, slots), F32), pltpu.VMEM((slots, slots), F32)],
        compiler_params=settings,
        name="scan_back",
    )(pre_x, edge_x, conv_x, dtraw, params, steps, b_act, c_act, y, grad_y, entering, coming)
    grad_bc = head_sum(grad_bc)

    one = lambda *shape: pl.BlockSpec((1,) + shape, lambda b: (b, 0, 0))
    rows8 = S((seqs, EDGE, 2 * state), F32)
    grad_pre_bc, tail_bc, first_bc, taps_grad_bc = pl.pallas_call(
        conv_back_kernel,
        grid=(seqs,),
        in_specs=[
            one(slots, 2 * state), one(EDGE, 2 * state),
            pl.BlockSpec((CONV + 1, 2 * state), lambda b: (0, 0)), one(slots, 2 * state),
        ],
        out_specs=[one(slots, 2 * state), one(EDGE, 2 * state), one(EDGE, 2 * state), one(EDGE, 2 * state)],
        out_shape=[S((seqs, slots, 2 * state), BF16), rows8, rows8, rows8],
        compiler_params=settings,
        name="conv_back",
    )(pre_bc, edge_bc, conv_bc, grad_bc)

    def mended(value, tail, first, weights):
        later = shifted(first, "seq", -1)
        add = jnp.zeros_like(tail)
        for tap in range(CONV - 1):
            ahead = CONV - 1 - tap
            moved = jnp.pad(later[:, :ahead], ((0, 0), (EDGE - ahead, 0), (0, 0)))
            add = add + moved * weights[tap]
        return lax.dynamic_update_slice(value, (tail + add).astype(BF16), (0, slots - EDGE, 0))

    grad_pre = mended(grad_pre, tail_x, first_x, conv_x).reshape(rows, inner)
    grad_pre_bc = mended(grad_pre_bc, tail_bc, first_bc, conv_bc).reshape(rows, 2 * state)
    grad_dtr = grad_dt.transpose(0, 2, 1, 3).reshape(rows, heads_dev).astype(BF16)

    portion = mm(grad_z, w_z, ((1,), (1,))) + mm(grad_pre, w_x, ((1,), (1,)))
    portion = portion + mm(grad_dtr, w_dt, ((1,), (1,)))
    grad_normed = head_sum(portion) + mm(grad_pre_bc, w_bc, ((1,), (1,)))
    scaled_input = hidden_f * inv_rms
    grad_norm_gain = jnp.sum(grad_normed * scaled_input, axis=0)
    grad_scaled = grad_normed * norm_gain
    input_dot = jnp.mean(grad_scaled * scaled_input, axis=-1, keepdims=True)
    grad_hidden = grad_mix.astype(F32) + inv_rms * (grad_scaled - scaled_input * input_dot)
    grad_hidden = grad_hidden.reshape(seqs, slots, model)

    if paired:
        bc_half = halves(grad_pre_bc, 1, side)
        fill = jnp.zeros((rows, state - heads_dev), BF16)
        half = inner // 2
        columns = jnp.concatenate(
            [grad_pre[:, :half], bc_half, grad_pre[:, half:], grad_dtr, fill], axis=1
        )
        grad_w_x = pair_grad(normed_rows, pair_columns(columns))
        bc_mine = grad_w_x[:, half : half + state]
        bc_other = swapped(bc_mine, "head", 1)
        grad_w_bc = jnp.concatenate(
            [jnp.where(side == 0, bc_mine, bc_other), jnp.where(side == 0, bc_other, bc_mine)], axis=1
        )
        grad_w_dt = grad_w_x[:, inner + state : inner + state + heads_dev]
        grad_w_x = jnp.concatenate([grad_w_x[:, :half], grad_w_x[:, half + state : inner + state]], axis=1)
        grad_weight = jnp.stack([grad_w_z, grad_w_x], axis=1)
    else:
        scatter = functools.partial(lax.psum_scatter, axis_name=("batch", "seq"), tiled=True)
        over_slots = ((0,), (0,))
        grad_weight = scatter(
            jnp.stack([mm(normed, grad_z, over_slots), mm(normed, grad_pre, over_slots)], axis=1),
            scatter_dimension=0,
        )
        grad_w_bc = scatter(mm(normed, grad_pre_bc, over_slots), scatter_dimension=0)
        grad_w_dt = scatter(mm(normed, grad_dtr, over_slots), scatter_dimension=0)
        grad_w_out = scatter(mm(gated, grad_mix, over_slots), scatter_dimension=1)

    head_grad = params_grad.sum(axis=0).transpose(1, 0, 2).reshape(3, heads_dev)
    taps_sum = jnp.concatenate([taps_grad_x.sum(axis=0), taps_grad_bc.sum(axis=0)], axis=1)[: CONV + 1]
    pieces = [taps_sum, head_grad, gain_grad.sum(axis=0), grad_norm_gain]
    flat = jnp.concatenate([piece.reshape(-1) for piece in pieces])
    flat = everywhere_sum(flat)
    parted, start = [], 0
    for piece in pieces:
        parted.append(flat[start : start + piece.size].reshape(piece.shape))
        start += piece.size
    grad_conv, grad_head, grad_gate_gain, grad_norm_gain = parted
    return (
        mixed_out,
        grad_hidden,
        grad_norm_gain,
        grad_weight,
        grad_w_bc,
        grad_w_dt,
        grad_conv[:, :inner],
        grad_conv[:, inner:],
        grad_head,
        grad_gate_gain.reshape(inner),
        grad_w_out,
    )


def solution(mesh):
    placed = (
        P("batch", "seq", None),
        P(),
        P(None, None, "head"),
        P(),
        P(None, "head"),
        P(None, "head"),
        P(),
        P(None, "head"),
        P("head"),
        P("head", None),
        P("batch"),
        P("batch", "seq", None),
    )
    return jax.shard_map(
        per_device,
        mesh=mesh,
        in_specs=placed,
        out_specs=(
            P("batch", "seq", None),
            P("batch", "seq", None),
            P(),
            P(("batch", "seq"), None, "head"),
            P(("batch", "seq"), None),
            P(("batch", "seq"), "head"),
            P(None, "head"),
            P(),
            P(None, "head"),
            P("head"),
            P("head", ("batch", "seq")),
        ),
        check_vma=False,
    )
```

time: 1800 us -> 1130 us (0.63)
  waiting for transfers between devices: 1250 us -> 619 us
  matrix products: 246 us -> 123 us
  Pallas kernels: 0 us -> 122 us
  blocking collectives: 113 us -> 0 us
  local copies, waits for them, and re-layouts: 75.4 us -> 125 us
  starting transfers between devices: 7.06 us -> 51.7 us
  other arithmetic: 91.9 us -> 62.6 us
    reduce_scatter x4 -> x0, waiting for transfers between devices: 1090 us -> none  [the longest x1 585 us: per_device(): lax.psum_scatter(gradient_gate_input_weight, ('batch', 'seq'), scatter_di...]
    ppermute x0 -> x34, waiting for transfers between devices: none -> 471 us  [swapped(): return lax.ppermute(value, axis, [(i, i ^ bit) for i in range(count)])]
    dot_general x27 -> x13, matrix products: 246 us -> 123 us  [mm(): lax.dot_general(a, b, (dims, ((), ())), precision=precision, preferred_el...]
    pallas_call x0 -> x12, Pallas kernels: none -> 122 us  [the longest x1 47.8 us: per_device(): pl.pallas_call(functools.partial(scan_back_kernel, heads, width), grid=gr...]
    psum x3 -> x0, blocking collectives: 105 us -> none  [the longest x1 89.5 us: per_device(): lax.psum((grad_conv, grad_head, grad_gate_gain, grad_norm_gain), ('batch'...]
    slice x8 -> x27, local copies, waits for them, and re-layouts: 19.3 us -> 52.5 us  [the longest x1 32.8 us: per_device(): w_z, w_x = (gate_input_weight[:, 0], gate_input_weight[:, 1])]
    ppermute x0 -> x34, starting transfers between devices: none -> 31.8 us  [swapped(): return lax.ppermute(value, axis, [(i, i ^ bit) for i in range(count)])]
    reduce_sum x7 -> x4, other arithmetic: 30.3 us -> 0.06 us  [the longest x1 0.03 us: per_device(): pieces = [taps_sum, head_grad, gain_grad.sum(axis=0), grad_norm_gain]]
  transfers between devices with their start and end apart: 10 -> 39, of which waited for: 8 -> 20; matrix products, arithmetic and copies ran while one was open for 6% -> 16% of each run, Pallas kernels for 0% -> 2%
where the time goes in v1:
time: 1130 us; the launch traced here: 1120 us
  waiting for transfers between devices  619 us (55%)
  local copies, waits for them, and re-layouts  125 us (11%)
  matrix products  123 us (11%)
  Pallas kernels  122 us (11%)
  other arithmetic  62.6 us (6%)
  starting transfers between devices  51.7 us (5%)
  between operations  15.6 us (1%)
    ppermute x34, waiting for transfers between devices, swapped(): return lax.ppermute(value, axis, [(i, i ^ bit) for i in range(count)])  471 us
    all_gather x2, waiting for transfers between devices, passed_on(): gathered = lax.all_gather(both, 'seq')  141 us
    dot_general x13, matrix products, mm(): lax.dot_general(a, b, (dims, ((), ())), precision=precision, preferred_el...  123 us
    pallas_call x1, Pallas kernels, per_device(): pl.pallas_call(functools.partial(scan_back_kernel, heads, width), grid=gr...  47.8 us
    slice x1, local copies, waits for them, and re-layouts, per_device(): w_z, w_x = (gate_input_weight[:, 0], gate_input_weight[:, 1])  32.8 us
    ppermute x34, starting transfers between devices, swapped(): return lax.ppermute(value, axis, [(i, i ^ bit) for i in range(count)])  31.8 us
    unnamed x184, local copies, waits for them, and re-layouts  29.3 us
    dynamic_slice x11, local copies, waits for them, and re-layouts, pick(): return lax.dynamic_index_in_dim(value, index, axis, False)  28.1 us
  transfers between devices with their start and end apart: 39, of which 20 were waited for; matrix products, arithmetic and copies ran while one was open for 16% of the time, Pallas kernels for 2%

profile of v1, /device:TPU:0, one launch (start us, length us, event | category | flops | bytes accessed | tf_op | source)
XLA Modules:
  0.0 1119.4 jit_solution(17301611414046664332)
XLA Ops:
  10.0 32.8 %fusion.82 = (bf16[2048,1,2048]{2,1,0:T(2,128)(2,1)}, bf16[2048,1,2048]{2,1,0:T(2,128)(2,1)}) fusion(bf16[2048,2,2048]{2,1,0:T(2,128)(2,1)} %param.14), kind=kLoop, calls=%fused_computation.179 | loop fusion | bytes 33554432 | tf_op jit(solution)/shard_map/slice | solution.py:394
  42.8 11.3 %fusion.6.pre_x = f32[2,256,2048]{2,1,0:T(8,128)S(1)} fusion(bf16[2048,1,2048]{2,1,0:T(2,128)(2,1)} %get-tuple-element.120, bf16[2,256,2048]{2,1,0:T(8,128)(2,1)S(1)} %copy-done.33, f32[2048]{0:T(1024)S(1)} %copy-done.73, f32[2,256]{1,0:T(2,128)S(1)} %get-tuple-element.174), kind=kOutput, calls=%fused_computation.6 | convolution fusion | flops 4299161600 | bytes 14690304 | tf_op jit(solution)/shard_map/dot_general | solution.py:21
  56.9 5.5 collective-permute-start
  62.5 4.4 fusion.64.dtraw
  71.2 24.4 %scan_local.1 = (f32[2,256,2048]{2,1,0:T(8,128)}, f32[2,128,2048]{2,1,0:T(8,128)S(1)}, f32[2,1,2048]{2,1,0:T(1,128)S(1)}, f32[2,256,128]{2,1,0:T(8,128)S(1)}, f3...) custom-call(f32[2,256,2048]{2,1,0:T(8,128)} %copy-done.36, f32[2,8,2048]{2,1,0:T(8,128)S(1)} %slice.209.edge_x, ...), custom_call_target="tpu_custom_call" | custom-call | tf_op jit(solution)/shard_map/scan_local/pallas_call | solution.py:424
  98.8 11.6 %all-gather.7.cloned.1.call-start = ((), (), s32[]{:S(2)}) async-start(), calls=%async_computation.1 | async-start | bytes 11141120 | tf_op jit(solution)/shard_map/all_gather | solution.py:294
  111.8 10.7 fusion.grad_out
  122.5 18.3 %fusion.2.z = f32[2,256,2048]{2,1,0:T(8,128)} fusion(bf16[2048,1,2048]{2,1,0:T(2,128)(2,1)} %get-tuple-element.119, bf16[2,256,2048]{2,1,0:T(8,128)(2,1)S(1)} %copy-done.34, f32[2048]{0:T(1024)S(1)} %copy-done.74, f32[2,256]{1,0:T(2,128)S(1)} %copy-done.84), kind=kOutput, calls=%fused_computation.2 | convolution fusion | flops 4299161600 | bytes 14690304 | tf_op jit(solution)/shard_map/dot_general | solution.py:21
  140.7 50.4 %all-gather.5.cloned.1.call-done = f32[8,136,2048]{2,1,0:T(8,128)} async-done(((f32[2,136,2048]{2,1,0:T(8,128)}), f32[8,136,2048]{2,1,0:T(8,128)}) %all-gather.5.cloned.1.call-update) | async-done | bytes 8912912 | tf_op jit(solution)/shard_map/all_gather | solution.py:294
  192.3 3.6 fusion.49.entering
  195.9 15.2 %gate.1 = (f32[2,256,2048]{2,1,0:T(8,128)}, f32[2,256,2]{2,1,0:T(8,128)S(1)}) custom-call(f32[2,256,2048]{2,1,0:T(8,128)} %get-tuple-element.35.local_out, f32[2,128,2048]{2,1,0:T(8,128)S(1)} %fusion.49.entering, f32[2,256,128]{2,1,0:T(8,128)S(1)} %get-tuple-element.38.c_act, f32[2,8,256,8]{3,2,1,0:T(8,128)S(1)} %get-tuple-element.39.steps, ...), custom_call_target="tpu_custom_call" | custom-call | tf_op jit(solution)/shard_map/gate/pallas_call | solution.py:445
  212.6 16.7 %gate_back.1 = (bf16[2,256,2048]{2,1,0:T(8,128)(2,1)S(1)}, f32[2,256,2048]{2,1,0:T(8,128)}, bf16[2,256,2048]{2,1,0:T(8,128)(2,1)S(1)}, f32[2,1,2048]{2,1,0:T(1,128)S(1)}, f32[2,128,2048]{2,1,0:T(8,128)}) custom-call(f32[2,256,2048]{2,1,0:T(8,128)} %get-tuple-element.40.y, f32[2,256,2048]{2,1,0:T(8,128)} %fusion.2.z, f32[2,256,2048]{2,1,0:T(8,128)} %fusion.grad_out, ...), custom_call_target="tpu_custom_call" | custom-call | tf_op jit(solution)/shard_map/gate_back/pallas_call | solution.py:456
  231.3 3.3 pad_maximum_fusion
  236.1 90.5 %all-gather.7.cloned.1.call-done = f32[8,136,2048]{2,1,0:T(8,128)} async-done(((f32[2,136,2048]{2,1,0:T(8,128)}), f32[8,136,2048]{2,1,0:T(8,128)}) %all-gather.7.cloned.1.call-update) | async-done | bytes 8912912 | tf_op jit(solution)/shard_map/all_gather | solution.py:294
  327.8 5.1 fusion.43.coming
  332.9 47.8 %scan_back.1 = (bf16[2,256,2048]{2,1,0:T(8,128)(2,1)S(1)}, f32[2,8,2048]{2,1,0:T(8,128)S(1)}, f32[2,8,2048]{2,1,0:T(8,128)S(1)}, f32[2,8,2048]{2,1,0:T(8,128)S(1...) custom-call(f32[2,256,2048]{2,1,0:T(8,128)} %copy-done.36, ...), custom_call_target="tpu_custom_call" | custom-call | tf_op jit(solution)/shard_map/scan_back/pallas_call | solution.py:481
  392.4 3.0 collective-permute-done.3
  395.6 15.0 %fusion.8 = f32[512,2048]{1,0:T(8,128)} fusion(bf16[512,2048]{1,0:T(8,128)(2,1)S(1)} %bitcast.266, bf16[2048,1,2048]{2,1,0:T(2,128)(2,1)} %get-tuple-element.120), kind=kOutput, calls=%fused_computation.8 | convolution fusion | flops 4294967296 | bytes 14680064 | tf_op jit(solution)/shard_map/dot_general | solution.py:21
  410.6 20.0 %add_add_fusion.1 = f32[512,2048]{1,0:T(8,128)} fusion(f32[512,2048]{1,0:T(8,128)} %fusion.93, f32[512,2048]{1,0:T(8,128)} %fusion.8, bf16[512,2048]{1,0:T(8,128)(2,1)S(1)} %bitcast.265, bf16[2048,1,2048]{2,1,0:T(2,128)(2,1)} %get-tuple-element.119), kind=kOutput, calls=%fused_computation.39 | convolution fusion | flops 4297064448 | bytes 23068672 | tf_op jit(solution)/shard_map/dot_general | solution.py:21
  430.6 9.5 fusion.92
  440.7 7.0 collective-permute-done.5
  450.3 4.5 collective-permute-done.6
  454.9 6.4 fusion.25
  461.3 6.8 fusion.24
  472.6 3.5 constant_dynamic-slice_fusion.13
  483.7 4.4 concatenate.70
  493.8 26.3 %collective-permute-done.11.value = f32[512,1024]{1,0:T(8,128)} collective-permute-done((f32[512,1024]{1,0:T(8,128)}, f32[512,1024]{1,0:T(8,128)}, u32[]{:S(2)}, u32[]{:S(2)}) %collective-permute-start.11) | collective-permute-done | bytes 2097184 | tf_op jit(solution)/shard_map/ppermute | solution.py:275
  520.1 44.9 %collective-permute-done.13.value = f32[512,1024]{1,0:T(8,128)} collective-permute-done((f32[512,1024]{1,0:T(8,128)}, f32[512,1024]{1,0:T(8,128)}, u32[]{:S(2)}, u32[]{:S(2)}) %collective-permute-start.13) | collective-permute-done | bytes 2097184 | tf_op jit(solution)/shard_map/ppermute | solution.py:275
  567.4 42.5 %collective-permute-done.30.value = f32[512,1024]{1,0:T(8,128)} collective-permute-done((f32[512,1024]{1,0:T(8,128)}, f32[512,1024]{1,0:T(8,128)}, u32[]{:S(2)}, u32[]{:S(2)}) %collective-permute-start.30) | collective-permute-done | bytes 2097184 | tf_op jit(solution)/shard_map/ppermute | solution.py:275
  612.5 42.4 %collective-permute-done.28.value = f32[512,1024]{1,0:T(8,128)} collective-permute-done((f32[512,1024]{1,0:T(8,128)}, f32[512,1024]{1,0:T(8,128)}, u32[]{:S(2)}, u32[]{:S(2)}) %collective-permute-start.28) | collective-permute-done | bytes 2097184 | tf_op jit(solution)/shard_map/ppermute | solution.py:275
  654.9 48.8 %collective-permute-done.20.value = f32[512,1152]{1,0:T(8,128)} collective-permute-done((f32[512,1152]{1,0:T(8,128)}, f32[512,1152]{1,0:T(8,128)}, u32[]{:S(2)}, u32[]{:S(2)}) %collective-permute-start.20) | collective-permute-done | bytes 2359328 | tf_op jit(solution)/shard_map/ppermute | solution.py:275
  720.0 4.6 fusion.54
  737.2 4.7 fusion.10
  752.3 15.1 %fusion.38 = f32[2048,1152]{1,0:T(8,128)} fusion(bf16[512,1152]{1,0:T(8,128)(2,1)S(1)} %copy-done.57, bf16[512,1152]{1,0:T(8,128)(2,1)S(1)} %copy-done.60, bf16[512,1024]{1,0:T(8,128)(2,1)S(1)} %copy-done.65, bf16[512,1024]{1,0:T(8,128)(2,1)S(1)} %copy-done.63, bf16[512,2048]{1,0:T(8,128)(2,1)S(1)} %copy-done.48), kind=kOutput, calls=%fused_computation.47 | convolution fusion | flops 4849139712 | bytes 15990784 | tf_op jit(solution)/shard_map/dot_general | solution.py:21
  767.3 8.2 fusion.83
  778.2 3.2 copy.101
  783.7 5.4 constant_dynamic-slice_fusion.8
  789.0 3.2 copy.128
  792.2 3.3 copy.127
  803.0 20.9 %collective-permute-done.33 = f32[4,2,128,512]{3,2,0,1:T(8,128)} collective-permute-done((f32[4,2,128,512]{3,2,0,1:T(8,128)}, f32[4,2,128,512]{3,2,0,1:T(8,128)}, u32[]{:S(2)}, u32[]{:S(2)}) %collective-permute-start.33) | collective-permute-done | bytes 2097184 | tf_op jit(solution)/shard_map/ppermute | solution.py:275
  829.6 44.8 %collective-permute-done.23 = f32[4,2,128,576]{2,3,1,0:T(8,128)} collective-permute-done((f32[4,2,128,576]{2,3,1,0:T(8,128)}, f32[4,2,128,576]{2,3,1,0:T(8,128)}, u32[]{:S(2)}, u32[]{:S(2)}) %collective-permute-start.23) | collective-permute-done | bytes 2359328 | tf_op jit(solution)/shard_map/ppermute | solution.py:275
  878.3 20.0 %collective-permute-done.17 = f32[4,128,512]{2,1,0:T(8,128)S(1)} collective-permute-done((f32[4,128,512]{2,1,0:T(8,128)S(1)}, f32[4,128,512]{2,1,0:T(8,128)S(1)}, u32[]{:S(2)}, u32[]{:S(2)}) %collective-permute-start.17) | collective-permute-done | bytes 1048608 | tf_op jit(solution)/shard_map/ppermute | solution.py:275
  902.1 18.7 %collective-permute-done.34 = f32[4,128,512]{2,1,0:T(8,128)S(1)} collective-permute-done((f32[4,128,512]{2,1,0:T(8,128)S(1)}, f32[4,128,512]{2,1,0:T(8,128)S(1)}, u32[]{:S(2)}, u32[]{:S(2)}) %collective-permute-start.34) | collective-permute-done | bytes 1048608 | tf_op jit(solution)/shard_map/ppermute | solution.py:275
  925.5 17.4 %collective-permute-done.24 = f32[4,128,576]{1,2,0:T(8,128)S(1)} collective-permute-done((f32[4,128,576]{1,2,0:T(8,128)S(1)}, f32[4,128,576]{1,2,0:T(8,128)S(1)}, u32[]{:S(2)}, u32[]{:S(2)}) %collective-permute-start.24) | collective-permute-done | bytes 1179680 | tf_op jit(solution)/shard_map/ppermute | solution.py:275
  951.5 38.1 %collective-permute-done.9 = f32[15712]{0:T(1024)S(1)} collective-permute-done((f32[15712]{0:T(1024)S(1)}, f32[15712]{0:T(1024)S(1)}, u32[]{:S(2)}, u32[]{:S(2)}) %collective-permute-start.9) | collective-permute-done | bytes 62880 | tf_op jit(solution)/shard_map/ppermute | solution.py:275
  992.1 69.3 %collective-permute-done.10 = f32[15712]{0:T(1024)S(1)} collective-permute-done((f32[15712]{0:T(1024)S(1)}, f32[15712]{0:T(1024)S(1)}, u32[]{:S(2)}, u32[]{:S(2)}) %collective-permute-start.10) | collective-permute-done | bytes 62880 | tf_op jit(solution)/shard_map/ppermute | solution.py:275
  1075.5 20.0 %collective-permute-done.36 = f32[128,1024]{1,0:T(8,128)S(1)} collective-permute-done((f32[128,1024]{1,0:T(8,128)S(1)}, f32[128,1024]{1,0:T(8,128)S(1)}, u32[]{:S(2)}, u32[]{:S(2)}) %collective-permute-start.36) | collective-permute-done | bytes 524320 | tf_op jit(solution)/shard_map/ppermute | solution.py:275
  1098.3 8.1 collective-permute-done.26
  (367 shorter events, 162.3 us)
Async XLA Ops:
  7.2 46.9 %copy-start = (bf16[2048,256]{1,0:T(8,128)(2,1)S(1)}, bf16[2048,256]{1,0:T(8,128)(2,1)}, u32[]{:S(2)}) copy-start(bf16[2048,256]{1,0:T(8,128)(2,1)} %param.15) | copy-start | bytes 3145732
  7.2 183.9 %all-gather.5.cloned.1.call-start = ((), (), s32[]{:S(2)}) async-start(), calls=%async_computation | async-start | bytes 11141120 | tf_op jit(solution)/shard_map/all_gather | solution.py:294
  10.0 44.1 %copy-start.83 = (f32[2,256]{1,0:T(2,128)}, f32[2,256]{1,0:T(2,128)S(1)}, u32[]{:S(2)}) copy-start(f32[2,256]{1,0:T(2,128)S(1)} %get-tuple-element.174) | copy-start | bytes 6148
  10.0 32.8 %copy-start.33 = (bf16[2,256,2048]{2,1,0:T(8,128)(2,1)S(1)}, bf16[2,256,2048]{2,1,0:T(8,128)(2,1)}, u32[]{:S(2)}) copy-start(bf16[2,256,2048]{2,1,0:T(8,128)(2,1)} %param.12) | copy-start | bytes 6291460
  10.0 32.8 %copy-start.73 = (f32[2048]{0:T(1024)S(1)}, f32[2048]{0:T(1024)}, u32[]{:S(2)}) copy-start(f32[2048]{0:T(1024)} %param.13) | copy-start | bytes 24580
  56.9 10.1 collective-permute-start
  96.4 99.5 %copy-start.2 = (f32[2,8,256,8]{3,2,1,0:T(8,128)}, f32[2,8,256,8]{3,2,1,0:T(8,128)S(1)}, u32[]{:S(2)}) copy-start(f32[2,8,256,8]{3,2,1,0:T(8,128)S(1)} %get-tuple-element.39.steps) | copy-start | bytes 393220
  98.8 227.9 %all-gather.7.cloned.1.call-start = ((), (), s32[]{:S(2)}) async-start(), calls=%async_computation.1 | async-start | bytes 11141120 | tf_op jit(solution)/shard_map/all_gather | solution.py:294
  211.1 1.5 collective-permute-start.1
  388.3 7.1 collective-permute-start.3
  430.6 24.3 %collective-permute-start.4 = (f32[512,2048]{1,0:T(8,128)}, f32[512,2048]{1,0:T(8,128)}, u32[]{:S(2)}, u32[]{:S(2)}) collective-permute-start(f32[512,2048]{1,0:T(8,128)} %add_add_fusion.1), channel_id=1, source_target_pairs={{0,1},{1,0},{2,3},{3,2},{4,5},{5,4},{6,7},{7,6},{8,9},{9,8},{10,11... | collective-permute-start | bytes 12582920 | tf_op jit(solution)/shard_map/ppermute | solution.py:275
  440.2 21.1 %collective-permute-start.2 = (f32[512,2048]{1,0:T(8,128)}, f32[512,2048]{1,0:T(8,128)}, u32[]{:S(2)}, u32[]{:S(2)}) collective-permute-start(f32[512,2048]{1,0:T(8,128)} %fusion.92), channel_id=1, source_target_pairs={{0,1},{1,0},{2,3},{3,2},{4,5},{5,4},{6,7},{7,6},{8,9},{9,8},{10,11... | collective-permute-start | bytes 12582920 | tf_op jit(solution)/shard_map/ppermute | solution.py:275
  440.7 7.1 collective-permute-start.5
  448.8 6.0 collective-permute-start.6
  471.1 48.9 %collective-permute-start.11 = (f32[512,1024]{1,0:T(8,128)}, f32[512,1024]{1,0:T(8,128)}, u32[]{:S(2)}, u32[]{:S(2)}) collective-permute-start(f32[512,1024]{1,0:T(8,128)} %dynamic-slice_convert_fusion.4), channel_id=1, source_target_pairs={{0,8},{8,0},{16,24},{24,16},{1,9},{9,1},{17,25},{25,17},{2,10},{10... | collective-permute-start | bytes 6291464 | tf_op jit(solution)/shard_map/ppermute | solution.py:275
  476.1 88.9 %collective-permute-start.13 = (f32[512,1024]{1,0:T(8,128)}, f32[512,1024]{1,0:T(8,128)}, u32[]{:S(2)}, u32[]{:S(2)}) collective-permute-start(f32[512,1024]{1,0:T(8,128)} %get-tuple-element.152), channel_id=1, source_target_pairs={{0,8},{8,0},{16,24},{24,16},{1,9},{9,1},{17,25},{25,17},{2,10},{10... | collective-permute-start | bytes 6291464 | tf_op jit(solution)/shard_map/ppermute | solution.py:275
  478.7 131.2 %collective-permute-start.30 = (f32[512,1024]{1,0:T(8,128)}, f32[512,1024]{1,0:T(8,128)}, u32[]{:S(2)}, u32[]{:S(2)}) collective-permute-start(f32[512,1024]{1,0:T(8,128)} %get-tuple-element.148), channel_id=1, source_target_pairs={{0,8},{8,0},{16,24},{24,16},{1,9},{9,1},{17,25},{25,17},{2,10},{10... | collective-permute-start | bytes 6291464 | tf_op jit(solution)/shard_map/ppermute | solution.py:275
  489.7 165.1 %collective-permute-start.28 = (f32[512,1024]{1,0:T(8,128)}, f32[512,1024]{1,0:T(8,128)}, u32[]{:S(2)}, u32[]{:S(2)}) collective-permute-start(f32[512,1024]{1,0:T(8,128)} %dynamic-slice_convert_fusion.2), channel_id=1, source_target_pairs={{0,8},{8,0},{16,24},{24,16},{1,9},{9,1},{17,25},{25,17},{2,10},{10... | collective-permute-start | bytes 6291464 | tf_op jit(solution)/shard_map/ppermute | solution.py:275
  492.5 211.2 %collective-permute-start.20 = (f32[512,1152]{1,0:T(8,128)}, f32[512,1152]{1,0:T(8,128)}, u32[]{:S(2)}, u32[]{:S(2)}) collective-permute-start(f32[512,1152]{1,0:T(8,128)} %get-tuple-element.144), channel_id=1, source_target_pairs={{0,8},{8,0},{16,24},{24,16},{1,9},{9,1},{17,25},{25,17},{2,10},{10... | collective-permute-start | bytes 7077896 | tf_op jit(solution)/shard_map/ppermute | solution.py:275
  520.0 193.7 %collective-permute-start.12 = (f32[512,1024]{1,0:T(8,128)}, f32[512,1024]{1,0:T(8,128)S(1)}, u32[]{:S(2)}, u32[]{:S(2)}) collective-permute-start(f32[512,1024]{1,0:T(8,128)} %collective-permute-done.11.value), channel_id=1, source_target_pairs={{0,1},{1,0},{2,3},{3,2},{4,5},{5,4},{6,7},{7,6},{8,9},{9,8},{10,11... | collective-permute-start | bytes 6291464 | tf_op jit(solution)/shard_map/ppermute | solution.py:275
  567.4 44.9 %copy-start.21 = (f32[2,8,2048]{2,1,0:T(8,128)S(1)}, f32[2,8,2048]{2,1,0:T(8,128)}, u32[]{:S(2)}) copy-start(f32[2,8,2048]{2,1,0:T(8,128)} %copy-done.20) | copy-start | bytes 393220
  567.4 44.9 %copy-start.28 = (f32[2,8,3,4]{3,2,1,0:T(4,128)S(1)}, f32[2,8,3,4]{3,2,1,0:T(4,128)}, u32[]{:S(2)}) copy-start(f32[2,8,3,4]{3,2,1,0:T(4,128)} %copy-done.27) | copy-start | bytes 2308
  612.3 93.9 %copy-start.76 = (f32[2048]{0:T(1024)S(1)}, f32[2048]{0:T(1024)}, u32[]{:S(2)}) copy-start(f32[2048]{0:T(1024)} %get-tuple-element.114) | copy-start | bytes 24580
  654.9 77.3 %collective-permute-start.29 = (f32[512,1024]{1,0:T(8,128)}, f32[512,1024]{1,0:T(8,128)}, u32[]{:S(2)}, u32[]{:S(2)}) collective-permute-start(f32[512,1024]{1,0:T(8,128)} %collective-permute-done.28.value), channel_id=1, source_target_pairs={{0,1},{1,0},{2,3},{3,2},{4,5},{5,4},{6,7},{7,6},{8,9},{9,8},{10,11... | collective-permute-start | bytes 6291464 | tf_op jit(solution)/shard_map/ppermute | solution.py:275
  706.3 75.2 %collective-permute-start.7 = (f32[15712]{0:T(1024)S(1)}, f32[15712]{0:T(1024)S(1)}, u32[]{:S(2)}, u32[]{:S(2)}) collective-permute-start(f32[15712]{0:T(1024)S(1)} %concatenate.64), channel_id=1, source_target_pairs={{0,2},{2,0},{4,6},{6,4},{1,3},{3,1},{5,7},{7,5},{8,10},{10,8},{12,... | collective-permute-start | bytes 188552 | tf_op jit(solution)/shard_map/ppermute | solution.py:275
  730.0 65.5 %collective-permute-start.16 = (f32[4,2,128,512]{3,2,0,1:T(8,128)}, f32[4,2,128,512]{3,2,0,1:T(8,128)}, u32[]{:S(2)}, u32[]{:S(2)}) collective-permute-start(f32[4,2,128,512]{3,2,0,1:T(8,128)} %bitcast.255), channel_id=1, source_target_pairs={{0,4},{2,6},{4,0},{6,2},{1,5},{3,7},{5,1},{7,3},{8,12},{10,14},{12... | collective-permute-start | bytes 6291464 | tf_op jit(solution)/shard_map/ppermute | solution.py:275
  731.6 68.1 %collective-permute-start.14 = (f32[4,2,128,512]{3,2,1,0:T(8,128)}, f32[4,2,128,512]{3,2,1,0:T(8,128)}, u32[]{:S(2)}, u32[]{:S(2)}) collective-permute-start(f32[4,2,128,512]{3,2,1,0:T(8,128)} %dynamic-slice_bitcast_fusion.1), channel_id=1, source_target_pairs={{0,2},{2,0},{4,6},{6,4},{1,3},{3,1},{5,7},{7,5},{8,10},{10,8},{12,... | collective-permute-start | bytes 6291464 | tf_op jit(solution)/shard_map/ppermute | solution.py:275
  747.2 76.6 %collective-permute-start.33 = (f32[4,2,128,512]{3,2,0,1:T(8,128)}, f32[4,2,128,512]{3,2,0,1:T(8,128)}, u32[]{:S(2)}, u32[]{:S(2)}) collective-permute-start(f32[4,2,128,512]{3,2,0,1:T(8,128)} %bitcast.254), channel_id=1, source_target_pairs={{0,4},{2,6},{4,0},{6,2},{1,5},{3,7},{5,1},{7,3},{8,12},{10,14},{12... | collective-permute-start | bytes 6291464 | tf_op jit(solution)/shard_map/ppermute | solution.py:275
  750.3 75.9 %collective-permute-start.31 = (f32[4,2,128,512]{3,2,1,0:T(8,128)}, f32[4,2,128,512]{3,2,1,0:T(8,128)}, u32[]{:S(2)}, u32[]{:S(2)}) collective-permute-start(f32[4,2,128,512]{3,2,1,0:T(8,128)} %dynamic-slice_bitcast_fusion), channel_id=1, source_target_pairs={{0,2},{2,0},{4,6},{6,4},{1,3},{3,1},{5,7},{7,5},{8,10},{10,8},{12,... | collective-permute-start | bytes 6291464 | tf_op jit(solution)/shard_map/ppermute | solution.py:275
  781.5 92.9 %collective-permute-start.23 = (f32[4,2,128,576]{2,3,1,0:T(8,128)}, f32[4,2,128,576]{2,3,1,0:T(8,128)}, u32[]{:S(2)}, u32[]{:S(2)}) collective-permute-start(f32[4,2,128,576]{2,3,1,0:T(8,128)} %bitcast.58), channel_id=1, source_target_pairs={{0,4},{2,6},{4,0},{6,2},{1,5},{3,7},{5,1},{7,3},{8,12},{10,14},{12... | collective-permute-start | bytes 7077896 | tf_op jit(solution)/shard_map/ppermute | solution.py:275
  795.5 80.8 %collective-permute-start.21 = (f32[4,2,128,576]{2,3,1,0:T(8,128)}, f32[4,2,128,576]{2,3,1,0:T(8,128)S(1)}, u32[]{:S(2)}, u32[]{:S(2)}) collective-permute-start(f32[4,2,128,576]{2,3,1,0:T(8,128)} %bitcast.287), channel_id=1, source_target_pairs={{0,2},{2,0},{4,6},{6,4},{1,3},{3,1},{5,7},{7,5},{8,10},{10,8},{12,... | collective-permute-start | bytes 7077896 | tf_op jit(solution)/shard_map/ppermute | solution.py:275
  799.7 150.3 %collective-permute-start.8 = (f32[15712]{0:T(1024)S(1)}, f32[15712]{0:T(1024)S(1)}, u32[]{:S(2)}, u32[]{:S(2)}) collective-permute-start(f32[15712]{0:T(1024)S(1)} %add.283), channel_id=1, source_target_pairs={{0,4},{2,6},{4,0},{6,2},{1,5},{3,7},{5,1},{7,3},{8,12},{10,14},{12... | collective-permute-start | bytes 188552 | tf_op jit(solution)/shard_map/ppermute | solution.py:275
  823.8 74.5 %collective-permute-start.17 = (f32[4,128,512]{2,1,0:T(8,128)S(1)}, f32[4,128,512]{2,1,0:T(8,128)S(1)}, u32[]{:S(2)}, u32[]{:S(2)}) collective-permute-start(f32[4,128,512]{2,1,0:T(8,128)S(1)} %dynamic-slice_bitcast_fusion.8), channel_id=1, source_target_pairs={{0,2},{2,0},{4,6},{6,4},{1,3},{3,1},{5,7},{7,5},{8,10},{10,8},{12,... | collective-permute-start | bytes 3145736 | tf_op jit(solution)/shard_map/ppermute | solution.py:275
  826.2 72.9 %collective-permute-start.15 = (f32[4,128,512]{2,1,0:T(8,128)S(1)}, f32[4,128,512]{2,1,0:T(8,128)S(1)}, u32[]{:S(2)}, u32[]{:S(2)}) collective-permute-start(f32[4,128,512]{2,1,0:T(8,128)S(1)} %dynamic-slice_bitcast_fusion.9), channel_id=1, source_target_pairs={{0,4},{2,6},{4,0},{6,2},{1,5},{3,7},{5,1},{7,3},{8,12},{10,14},{12... | collective-permute-start | bytes 3145736 | tf_op jit(solution)/shard_map/ppermute | solution.py:275
  829.6 48.3 %copy-start.41 = (f32[4,2,1,128,576]{3,4,2,1,0:T(8,128)S(1)}, f32[4,2,1,128,576]{3,4,2,1,0:T(8,128)}, u32[]{:S(2)}) copy-start(f32[4,2,1,128,576]{3,4,2,1,0:T(8,128)} %copy.127) | copy-start | bytes 7077892
  874.4 46.4 %collective-permute-start.34 = (f32[4,128,512]{2,1,0:T(8,128)S(1)}, f32[4,128,512]{2,1,0:T(8,128)S(1)}, u32[]{:S(2)}, u32[]{:S(2)}) collective-permute-start(f32[4,128,512]{2,1,0:T(8,128)S(1)} %dynamic-slice_bitcast_fusion.5), channel_id=1, source_target_pairs={{0,2},{2,0},{4,6},{6,4},{1,3},{3,1},{5,7},{7,5},{8,10},{10,8},{12,... | collective-permute-start | bytes 3145736 | tf_op jit(solution)/shard_map/ppermute | solution.py:275
  876.4 47.0 %collective-permute-start.32 = (f32[4,128,512]{2,1,0:T(8,128)S(1)}, f32[4,128,512]{2,1,0:T(8,128)S(1)}, u32[]{:S(2)}, u32[]{:S(2)}) collective-permute-start(f32[4,128,512]{2,1,0:T(8,128)S(1)} %dynamic-slice_bitcast_fusion.6), channel_id=1, source_target_pairs={{0,4},{2,6},{4,0},{6,2},{1,5},{3,7},{5,1},{7,3},{8,12},{10,14},{12... | collective-permute-start | bytes 3145736 | tf_op jit(solution)/shard_map/ppermute | solution.py:275
  898.3 44.6 %collective-permute-start.24 = (f32[4,128,576]{1,2,0:T(8,128)S(1)}, f32[4,128,576]{1,2,0:T(8,128)S(1)}, u32[]{:S(2)}, u32[]{:S(2)}) collective-permute-start(f32[4,128,576]{1,2,0:T(8,128)S(1)} %dynamic-slice_bitcast_fusion.2), channel_id=1, source_target_pairs={{0,2},{2,0},{4,6},{6,4},{1,3},{3,1},{5,7},{7,5},{8,10},{10,8},{12,... | collective-permute-start | bytes 3538952 | tf_op jit(solution)/shard_map/ppermute | solution.py:275
  899.1 43.9 %collective-permute-start.22 = (f32[4,128,576]{1,2,0:T(8,128)S(1)}, f32[4,128,576]{1,2,0:T(8,128)S(1)}, u32[]{:S(2)}, u32[]{:S(2)}) collective-permute-start(f32[4,128,576]{1,2,0:T(8,128)S(1)} %dynamic-slice_bitcast_fusion.3), channel_id=1, source_target_pairs={{0,4},{2,6},{4,0},{6,2},{1,5},{3,7},{5,1},{7,3},{8,12},{10,14},{12... | collective-permute-start | bytes 3538952 | tf_op jit(solution)/shard_map/ppermute | solution.py:275
  920.8 146.0 %collective-permute-start.18 = (f32[2,128,1024]{2,1,0:T(8,128)}, f32[2,128,1024]{2,1,0:T(8,128)}, u32[]{:S(2)}, u32[]{:S(2)}) collective-permute-start(f32[2,128,1024]{2,1,0:T(8,128)} %dynamic-slice_bitcast_fusion.7), channel_id=1, source_target_pairs={{0,16},{8,24},{16,0},{24,8},{1,17},{9,25},{17,1},{25,9},{2,18},{10... | collective-permute-start | bytes 3145736 | tf_op jit(solution)/shard_map/ppermute | solution.py:275
  925.0 144.8 %collective-permute-start.35 = (f32[2,128,1024]{2,1,0:T(8,128)}, f32[2,128,1024]{2,1,0:T(8,128)}, u32[]{:S(2)}, u32[]{:S(2)}) collective-permute-start(f32[2,128,1024]{2,1,0:T(8,128)} %dynamic-slice_bitcast_fusion.4), channel_id=1, source_target_pairs={{0,16},{8,24},{16,0},{24,8},{1,17},{9,25},{17,1},{25,9},{2,18},{10... | collective-permute-start | bytes 3145736 | tf_op jit(solution)/shard_map/ppermute | solution.py:275
  947.5 125.2 %collective-permute-start.25 = (f32[2,128,1152]{2,1,0:T(8,128)}, f32[2,128,1152]{2,1,0:T(8,128)}, u32[]{:S(2)}, u32[]{:S(2)}) collective-permute-start(f32[2,128,1152]{2,1,0:T(8,128)} %bitcast.289), channel_id=1, source_target_pairs={{0,16},{8,24},{16,0},{24,8},{1,17},{9,25},{17,1},{25,9},{2,18},{10... | collective-permute-start | bytes 3538952 | tf_op jit(solution)/shard_map/ppermute | solution.py:275
  950.0 39.6 %collective-permute-start.9 = (f32[15712]{0:T(1024)S(1)}, f32[15712]{0:T(1024)S(1)}, u32[]{:S(2)}, u32[]{:S(2)}) collective-permute-start(f32[15712]{0:T(1024)S(1)} %add.284), channel_id=1, source_target_pairs={{0,8},{8,0},{16,24},{24,16},{1,9},{9,1},{17,25},{25,17},{2,10},{10... | collective-permute-start | bytes 188552 | tf_op jit(solution)/shard_map/ppermute | solution.py:275
  989.6 71.9 %collective-permute-start.10 = (f32[15712]{0:T(1024)S(1)}, f32[15712]{0:T(1024)S(1)}, u32[]{:S(2)}, u32[]{:S(2)}) collective-permute-start(f32[15712]{0:T(1024)S(1)} %add.285), channel_id=1, source_target_pairs={{0,16},{8,24},{16,0},{24,8},{1,17},{9,25},{17,1},{25,9},{2,18},{10... | collective-permute-start | bytes 188552 | tf_op jit(solution)/shard_map/ppermute | solution.py:275
  1069.2 27.8 %collective-permute-start.19 = (f32[128,1024]{1,0:T(8,128)}, f32[128,1024]{1,0:T(8,128)}, u32[]{:S(2)}, u32[]{:S(2)}) collective-permute-start(f32[128,1024]{1,0:T(8,128)} %dynamic-slice_bitcast_fusion.12), channel_id=1, source_target_pairs={{0,8},{8,0},{16,24},{24,16},{1,9},{9,1},{17,25},{25,17},{2,10},{10... | collective-permute-start | bytes 1572872 | tf_op jit(solution)/shard_map/ppermute | solution.py:275
  1071.2 24.4 %collective-permute-start.36 = (f32[128,1024]{1,0:T(8,128)S(1)}, f32[128,1024]{1,0:T(8,128)S(1)}, u32[]{:S(2)}, u32[]{:S(2)}) collective-permute-start(f32[128,1024]{1,0:T(8,128)S(1)} %dynamic-slice_bitcast_fusion.11), channel_id=1, source_target_pairs={{0,8},{8,0},{16,24},{24,16},{1,9},{9,1},{17,25},{25,17},{2,10},{10... | collective-permute-start | bytes 1572872 | tf_op jit(solution)/shard_map/ppermute | solution.py:275
  1075.0 31.4 %collective-permute-start.26 = (f32[128,1152]{1,0:T(8,128)}, f32[128,1152]{1,0:T(8,128)}, u32[]{:S(2)}, u32[]{:S(2)}) collective-permute-start(f32[128,1152]{1,0:T(8,128)} %dynamic-slice_bitcast_fusion.10), channel_id=1, source_target_pairs={{0,8},{8,0},{16,24},{24,16},{1,9},{9,1},{17,25},{25,17},{2,10},{10... | collective-permute-start | bytes 1769480 | tf_op jit(solution)/shard_map/ppermute | solution.py:275
  1107.7 4.0 collective-permute-start.27
  (76 other events, 485.3 us)
Sparse Core Ops, SparseCore 0:
  98.9 92.1 all-gather.4
  234.7 91.9 all-gather.6

commit v2 on v1

--- a/solution.py
+++ b/solution.py
@@ -15,6 +15,7 @@
 F32 = jnp.float32
 BF16 = jnp.bfloat16
 VMEM_LIMIT = 48 * 1024 * 1024
+COST = 0.25
 
 
 def mm(a, b, dims=((1,), (0,)), precision=None):
@@ -82,13 +83,39 @@
     return jnp.where(lane == head, value, jnp.zeros_like(value))
 
 
-def local_kernel(
+def call(kernel, inputs, in_specs, out_specs, out_shape, grid, name, micros, scratch=(), after=()):
+    count = len(inputs)
+
+    def body(*refs):
+        kernel(*refs[:count], *refs[count + len(after) :])
+
+    return pl.pallas_call(
+        body,
+        grid=grid,
+        in_specs=list(in_specs) + [pl.BlockSpec(memory_space=pl.ANY)] * len(after),
+        out_specs=out_specs,
+        out_shape=out_shape,
+        scratch_shapes=list(scratch),
+        compiler_params=pltpu.CompilerParams(vmem_limit_bytes=VMEM_LIMIT),
+        cost_estimate=pl.CostEstimate(
+            flops=int(micros * COST * 1.1e9), bytes_accessed=int(micros * COST * 2e6), transcendentals=0
+        ),
+        name=name,
+    )(*inputs, *after)
+
+
+def steps_of(dtraw, par, tri):
+    step = softplus(dtraw + par[0:1])
+    rate = step * -jnp.exp(par[1:2])
+    return step, rate, mm(tri, rate, precision=HIGHEST)
+
+
+def state_kernel(
     heads, width, pre_x, edge_x, taps_x, pre_bc, edge_bc, taps_bc, dtraw, params,
-    local_out, local_state, total_decay, b_out, c_out, steps_out, scores,
+    local_state, total_decay, b_out, c_out, steps_out,
 ):
     slots = pre_x.shape[1]
     state = b_out.shape[2]
-    tri = triangle(slots)
 
     @pl.when(pl.program_id(1) == 0)
     def _():
@@ -97,22 +124,34 @@
         act = u * jax.nn.sigmoid(u)
         b_out[0] = act[:, :state]
         c_out[0] = act[:, state:]
-        scores[...] = mm(act[:, state:], act[:, :state], ((1,), (1,)), HIGHEST) * tri
+
+    ext = jnp.concatenate([edge_x[0], pre_x[0]], axis=0)
+    u = convolved(ext, taps_x[...], slots)
+    x = u * jax.nn.sigmoid(u)
+    step, _, cumul = steps_of(dtraw[0, 0], params[0], triangle(slots))
+    steps_out[0, 0] = jnp.concatenate([step, cumul], axis=1)
+    last = cumul[slots - 1 : slots]
+    total_decay[0] = jnp.broadcast_to(widen(jnp.exp(last), width), (8, heads * width))
+    xd = (widen(step, width) * x).astype(BF16)
+    tail = (widen(jnp.exp(last - cumul), width) * xd.astype(F32)).astype(BF16)
+    local_state[0] = mm(b_out[0].astype(BF16), tail, ((0,), (0,)))
+
+
+def inside_kernel(heads, width, pre_x, edge_x, taps_x, steps, params, b_act, c_act, local_out, scores):
+    slots = pre_x.shape[1]
+    tri = triangle(slots)
+
+    @pl.when(pl.program_id(1) == 0)
+    def _():
+        scores[...] = mm(c_act[0], b_act[0], ((1,), (1,)), HIGHEST) * tri
 
     ext = jnp.concatenate([edge_x[0], pre_x[0]], axis=0)
     u = convolved(ext, taps_x[...], slots)
     x = u * jax.nn.sigmoid(u)
     par = params[0]
-    step = softplus(dtraw[0, 0] + par[0:1])
-    rate = step * -jnp.exp(par[1:2])
-    cumul = mm(tri, rate, precision=HIGHEST)
-    cumul_t = mm(rate, tri, ((0,), (1,)), precision=HIGHEST)
-    steps_out[0, 0] = jnp.concatenate([step, cumul], axis=1)
-    last = cumul[slots - 1 : slots]
-    total_decay[0] = widen(jnp.exp(last), width)
+    step, cumul = steps[0, 0][:, :heads], steps[0, 0][:, heads:]
+    cumul_t = mm(step * -jnp.exp(par[1:2]), tri, ((0,), (1,)), precision=HIGHEST)
     xd = (widen(step, width) * x).astype(BF16)
-    tail = (widen(jnp.exp(last - cumul), width) * xd.astype(F32)).astype(BF16)
-    local_state[0] = mm(b_out[0].astype(BF16), tail, ((0,), (0,)))
     out = widen(par[2:3], width) * x
     for head in range(heads):
         decay = jnp.exp(jnp.minimum(cumul[:, head : head + 1] - cumul_t[head : head + 1], 0.0))
@@ -161,20 +200,59 @@
     leaving[0] = mm(c_act[0].astype(BF16), (growth * dy).astype(BF16), ((0,), (0,)))
 
 
-def scan_back_kernel(
-    heads, width, pre_x, edge_x, taps_x, dtraw, params, steps, b_act, c_act, y, grad_y, entering, coming,
-    grad_pre, tail_rows, head_rows, taps_grad, grad_dt, params_grad, grad_bc, grad_scores, scores,
+def inside_back_kernel(
+    heads, width, pre_x, edge_x, taps_x, steps, params, b_act, c_act, grad_y, entering,
+    grad_xd_out, grad_bc, grad_scores, scores,
 ):
     slots = pre_x.shape[1]
-    state = b_act.shape[2]
     tri = triangle(slots)
-    first = pl.program_id(1) == 0
-
-    @pl.when(first)
+
+    @pl.when(pl.program_id(1) == 0)
     def _():
         scores[...] = mm(c_act[0], b_act[0], ((1,), (1,)), HIGHEST) * tri
         grad_scores[...] = jnp.zeros_like(grad_scores)
         grad_bc[...] = jnp.zeros_like(grad_bc)
+
+    ext = jnp.concatenate([edge_x[0], pre_x[0]], axis=0)
+    u = convolved(ext, taps_x[...], slots)
+    x = u * jax.nn.sigmoid(u)
+    par = params[0]
+    step, cumul = steps[0, 0][:, :heads], steps[0, 0][:, heads:]
+    cumul_t = mm(step * -jnp.exp(par[1:2]), tri, ((0,), (1,)), precision=HIGHEST)
+    growth = widen(jnp.exp(cumul), width)
+    xd = (widen(step, width) * x).astype(BF16)
+    dy = grad_y[0]
+    dy_b = dy.astype(BF16)
+    grad_xd = jnp.zeros_like(dy)
+    total = jnp.zeros((slots, slots), F32)
+    for head in range(heads):
+        decay = jnp.exp(jnp.minimum(cumul[:, head : head + 1] - cumul_t[head : head + 1], 0.0))
+        weights = (scores[...] * decay).astype(BF16)
+        mine = of_head(dy_b, head, heads)
+        grad_xd = grad_xd + mm(weights, mine, ((0,), (0,)))
+        total = total + mm(mine, xd, ((1,), (1,))) * decay
+    grad_xd_out[0] = grad_xd
+    grad_scores[...] += total
+    grad_c = mm((growth * dy).astype(BF16), entering[0].astype(BF16), ((1,), (1,)))
+    grad_bc[0] += jnp.concatenate([jnp.zeros_like(grad_c), grad_c], axis=1)
+
+    @pl.when(pl.program_id(1) == pl.num_programs(1) - 1)
+    def _():
+        causal = grad_scores[...] * tri
+        from_c = mm(causal, c_act[0], ((0,), (0,)), HIGHEST)
+        grad_bc[0] += jnp.concatenate([from_c, mm(causal, b_act[0], precision=HIGHEST)], axis=1)
+
+
+def scan_back_kernel(
+    heads, width, pre_x, edge_x, taps_x, dtraw, params, steps, b_act, y, grad_y, inside, entering, coming,
+    grad_pre, tail_rows, head_rows, taps_grad, grad_dt, params_grad, grad_b,
+):
+    slots = pre_x.shape[1]
+    tri = triangle(slots)
+
+    @pl.when(pl.program_id(1) == 0)
+    def _():
+        grad_b[...] = jnp.zeros_like(grad_b)
 
     ext = jnp.concatenate([edge_x[0], pre_x[0]], axis=0)
     u = convolved(ext, taps_x[...], slots)
@@ -184,34 +262,21 @@
     decay_a = -jnp.exp(par[1:2])
     step = steps[0, 0][:, :heads]
     cumul = steps[0, 0][:, heads:]
-    cumul_t = mm(step * decay_a, tri, ((0,), (1,)), precision=HIGHEST)
     last = cumul[slots - 1 : slots]
     step_wide = widen(step, width)
     tail_wide = widen(jnp.exp(last - cumul), width)
-    growth = widen(jnp.exp(cumul), width)
     skip = widen(par[2:3], width)
     xd = (step_wide * x).astype(BF16)
     xd_f = xd.astype(F32)
     dy = grad_y[0]
-    dy_b = dy.astype(BF16)
     coming_b = coming[0].astype(BF16)
     from_next = tail_wide * mm(b_act[0].astype(BF16), coming_b)
-    grad_xd = from_next
-    total = jnp.zeros((slots, slots), F32)
-    for head in range(heads):
-        decay = jnp.exp(jnp.minimum(cumul[:, head : head + 1] - cumul_t[head : head + 1], 0.0))
-        weights = (scores[...] * decay).astype(BF16)
-        mine = of_head(dy_b, head, heads)
-        grad_xd = grad_xd + mm(weights, mine, ((0,), (0,)))
-        total = total + mm(mine, xd, ((1,), (1,))) * decay
-    grad_scores[...] += total
-    grad_c = mm((growth * dy).astype(BF16), entering[0].astype(BF16), ((1,), (1,)))
-    grad_b = mm((tail_wide * xd_f).astype(BF16), coming_b, ((1,), (1,)))
-    grad_bc[0] += jnp.concatenate([grad_b, grad_c], axis=1)
+    grad_xd = inside[0] + from_next
+    grad_b[0] += mm((tail_wide * xd_f).astype(BF16), coming_b, ((1,), (1,)))
 
     direct = head_sums(x * grad_xd, heads)
     ys = y[0] - skip * x
-    moved = head_sums(dy_b.astype(F32) * ys - xd_f * grad_xd, heads)
+    moved = head_sums(dy.astype(BF16).astype(F32) * ys - xd_f * grad_xd, heads)
     ends = jnp.exp(widen(last, width)) * jnp.sum(coming[0] * entering[0], axis=0, keepdims=True)
     ends = ends + jnp.sum(xd_f * from_next, axis=0, keepdims=True)
     skips = jnp.sum(dy * x, axis=0, keepdims=True)
@@ -234,12 +299,6 @@
     head_rows[0] = du[:EDGE]
     taps_grad[0] = rows8
 
-    @pl.when(pl.program_id(1) == pl.num_programs(1) - 1)
-    def _():
-        causal = grad_scores[...] * tri
-        from_c = mm(causal, c_act[0], ((0,), (0,)), HIGHEST)
-        grad_bc[0] += jnp.concatenate([from_c, mm(causal, b_act[0], precision=HIGHEST)], axis=1)
-
 
 def conv_back_kernel(pre, edge, taps, grad_act, grad_pre, tail_rows, head_rows, taps_grad):
     slots = pre.shape[1]
@@ -253,21 +312,31 @@
     taps_grad[0] = rows8
 
 
-def narrow_kernel(value, result):
-    result[...] = value[...].astype(BF16)
-
-
-def narrow(value):
-    rows, columns = value.shape
-    block = pl.BlockSpec((rows // 2, columns), lambda i: (i, 0))
-    return pl.pallas_call(
-        narrow_kernel,
-        grid=(2,),
-        in_specs=[block],
-        out_specs=block,
-        out_shape=jax.ShapeDtypeStruct(value.shape, BF16),
-        name="narrow",
-    )(value)
+def assemble_kernel(mine, theirs, side, result):
+    first = side[0] == 0
+    half = mine.shape[2]
+    result[0, :, :half] = jnp.where(first, mine[0], theirs[0]).astype(BF16)
+    result[0, :, half:] = jnp.where(first, theirs[0], mine[0]).astype(BF16)
+
+
+def weight_kernel(parts, own_rows, far_rows, *refs):
+    result, columns = refs[-2:]
+    slots = own_rows.shape[0]
+
+    @pl.when(pl.program_id(0) == 0)
+    def _():
+        for index in range(parts):
+            columns[:, pl.ds(index * slots, slots)] = refs[index][...].T.astype(BF16)
+
+    total = mm(columns[:, :slots], own_rows[...])
+    for index in range(1, parts):
+        total = total + mm(columns[:, index * slots : (index + 1) * slots], far_rows[index - 1])
+    for tile in range(result.shape[0] * result.shape[1]):
+        piece = total[:, tile * 128 : (tile + 1) * 128]
+        if result.shape[0] == 1:
+            result[0, tile] = piece
+        else:
+            result[tile, 0] = piece
 
 
 def swapped(value, axis, bit):
@@ -287,11 +356,10 @@
     return lax.psum(value, "head")
 
 
-def passed_on(decay, part, reverse):
+def gathered_pass(decay, part, reverse):
     count = lax.axis_size("seq")
     place = lax.axis_index("seq")
-    both = jnp.concatenate([part, jnp.broadcast_to(decay, (decay.shape[0], 8, decay.shape[2]))], axis=1)
-    gathered = lax.all_gather(both, "seq")
+    gathered = lax.all_gather(jnp.concatenate([part, decay], axis=1), "seq")
     rows = part.shape[1]
     state = jnp.zeros_like(part)
     for turn in range(count - 1):
@@ -302,52 +370,156 @@
     return state
 
 
+def chosen(pieces, index):
+    low = jnp.where(index % 2 == 0, pieces[0], pieces[1])
+    high = jnp.where(index % 2 == 0, pieces[2], pieces[3])
+    return jnp.where(index < 2, low, high)
+
+
+def quarter(value, axis, index):
+    size = value.shape[axis] // 4
+    return lax.dynamic_slice_in_dim(value, index * size, size, axis)
+
+
+def tied(*values):
+    return lax.optimization_barrier(values)
+
+
+def passed_on(decay, part, reverse, first, second):
+    if lax.axis_size("seq") != 4:
+        beside_first = first()
+        return gathered_pass(decay, part, reverse), beside_first, second(beside_first)
+    place = lax.axis_index("seq")
+    rows = part.shape[1]
+    both = jnp.concatenate([part, decay], axis=1)
+    got = [quarter(both, 2, place)] + [swapped(quarter(both, 2, place ^ d), "seq", d) for d in (1, 2, 3)]
+    got, beside_first = tied(got, first())
+    order = (3, 2, 1, 0) if reverse else (0, 1, 2, 3)
+    state = jnp.zeros_like(got[0][:, :rows])
+    enters = [None] * 4
+    for source in order:
+        enters[source] = state
+        if source != order[-1]:
+            piece = chosen(got, place ^ source)
+            state = piece[:, rows : rows + 1] * state + piece[:, :rows]
+    back = [chosen(enters, place)] + [swapped(chosen(enters, place ^ d), "seq", d) for d in (1, 2, 3)]
+    back, beside_second = tied(back, second(beside_first))
+    entering = jnp.concatenate([chosen(back, place ^ index) for index in range(4)], axis=2)
+    return entering, beside_first, beside_second
+
+
 def halves(value, axis, which):
     size = value.shape[axis] // 2
     return lax.dynamic_slice_in_dim(value, which * size, size, axis)
 
 
-def pair_rows(rows):
-    side = lax.axis_index("head")
-    mine = swapped(halves(rows, 1, side).astype(F32), "batch", 1)
-    theirs = narrow(swapped(mine, "head", 1))
-    mine = narrow(mine)
-    low = jnp.where(side == 0, mine, theirs)
-    high = jnp.where(side == 0, theirs, mine)
-    return jnp.concatenate([rows, jnp.concatenate([low, high], axis=1)], axis=0)
-
-
-def pair_columns(columns):
-    parity = lax.axis_index("batch") % 2
-    sent = halves(columns, 1, 1 - parity).astype(F32)
-    got = narrow(swapped(sent, "batch", 1))
-    return jnp.concatenate([halves(columns, 1, parity), got], axis=0)
-
-
-def pair_grad(rows, columns):
+def core_half(value):
+    return halves(value.astype(F32), 1, lax.axis_index("head"))
+
+
+def rows_of_seq_first(half):
+    cut = half.shape[1] // 2
+    a, b = half[:, :cut], half[:, cut:]
+    return a, b, swapped(a, "seq", 1), swapped(b, "seq", 2)
+
+
+def rows_of_seq_second(a, b, a1, b2):
+    return a1, swapped(jnp.stack([a, a1]), "seq", 2), b2, swapped(jnp.stack([b, b2]), "seq", 1)
+
+
+def rows_of_seq_third(a1, a23, b2, b13):
+    high = jnp.stack([b13[0], b2, b13[1]])
+    return jnp.concatenate([jnp.concatenate([a1[None], a23], axis=0), high], axis=2)
+
+
+def assembled(mine):
+    side = lax.axis_index("head").reshape(1)
+    theirs = swapped(mine, "head", 1)
+    count, slots, half = mine.shape
+    block = pl.BlockSpec((1, slots, half), lambda i: (i, 0, 0))
+    return call(
+        assemble_kernel,
+        [mine, theirs, side],
+        [block, block, pl.BlockSpec(memory_space=pltpu.SMEM)],
+        pl.BlockSpec((1, slots, 2 * half), lambda i: (i, 0, 0)),
+        jax.ShapeDtypeStruct((count, slots, 2 * half), BF16),
+        (count,),
+        "assemble",
+        3 * count,
+    )
+
+
+def columns_of(value, axis, dim=1):
+    place = lax.axis_index(axis)
+    piece = lambda index: quarter(value, dim, index).astype(F32)
+    return [piece(place)] + [swapped(piece(place ^ d), axis, d) for d in (1, 2, 3)]
+
+
+def weight_part(own_rows, far_rows, columns, axis, after=()):
+    slots, model = own_rows.shape
+    size = columns[0].shape[1]
+    parts = len(columns)
+    whole = lambda a: pl.BlockSpec(a.shape, lambda i: (0,) * a.ndim)
+    if axis == "seq":
+        out_spec = pl.BlockSpec((1, 4, size, 128), lambda i: (i, 0, 0, 0))
+    else:
+        out_spec = pl.BlockSpec((4, 1, size, 128), lambda i: (0, i, 0, 0))
+    return call(
+        functools.partial(weight_kernel, parts),
+        [own_rows, far_rows, *columns],
+        [
+            pl.BlockSpec((slots, model // 4), lambda i: (0, i)),
+            pl.BlockSpec((parts - 1, slots, model // 4), lambda i: (0, 0, i)),
+            *[whole(c) for c in columns],
+        ],
+        out_spec,
+        jax.ShapeDtypeStruct((4, 4, size, 128), F32),
+        (4,),
+        "weight_part",
+        9,
+        scratch=[pltpu.VMEM((size, parts * slots), BF16)],
+        after=after,
+    )
+
+
+def scattered_over_seq(part):
+    place = lax.axis_index("seq")
+    sx, sy = place % 2, place // 2
+    part = part.reshape((2, 2) + part.shape[1:])
+    pick = lambda value, axis, index: lax.dynamic_index_in_dim(value, index, axis, False)
+    a, b = part[:, :, :2], part[:, :, 2:]
+    a = pick(a, 1, sx) + swapped(pick(a, 1, 1 - sx), "seq", 1)
+    b = pick(b, 0, sy) + swapped(pick(b, 0, 1 - sy), "seq", 2)
+    a = pick(a, 0, sy) + swapped(pick(a, 0, 1 - sy), "seq", 2)
+    b = pick(b, 0, sx) + swapped(pick(b, 0, 1 - sx), "seq", 1)
+    return jnp.concatenate([a, b], axis=0)
+
+
+def weight_done(part):
+    summed = lax.psum_scatter(part, "batch", scatter_dimension=0, tiled=True)[0]
+    place = lax.axis_index("seq")
+    take = lambda index: lax.dynamic_index_in_dim(summed, index, 0, False)
+    back = [take(place)] + [swapped(take(place ^ d), "seq", d) for d in (1, 2, 3)]
+    return jnp.stack([chosen(back, place ^ index) for index in range(4)])
+
+
+def pair_done(part):
+    z = lax.axis_index("batch")
+    parity, upper = z % 2, z // 2
+    pick = lambda value, index: lax.dynamic_index_in_dim(value, index, 0, False)
+    both = scattered_over_seq(part).reshape((2, 2) + part.shape[2:])
+    both = pick(both, upper) + swapped(pick(both, 1 - upper), "batch", 2)
+    own, other = pick(both, parity), swapped(pick(both, 1 - parity), "batch", 1)
+    return jnp.concatenate([jnp.where(parity == 0, own, other), jnp.where(parity == 0, other, own)], axis=0)
+
+
+def small_done(part):
     z, s = lax.axis_index("batch"), lax.axis_index("seq")
-    parity, upper = z % 2, z // 2
-    sx, sy = s % 2, s // 2
-    block = rows.shape[1] // 16
-    part = mm(rows, columns, ((0,), (0,)))
-    part = part.reshape(4, 2, 2, block, columns.shape[1])
-    half = columns.shape[1] // 2
-
-    def pick(value, axis, index):
-        return lax.dynamic_index_in_dim(value, index, axis, False)
-
-    a, b = part[..., :half], part[..., half:]
-    a = pick(a, 2, sx) + swapped(pick(a, 2, 1 - sx), "seq", 1)
-    b = pick(b, 1, sy) + swapped(pick(b, 1, 1 - sy), "seq", 2)
-    a = pick(a, 1, sy) + swapped(pick(a, 1, 1 - sy), "seq", 2)
-    b = pick(b, 1, sx) + swapped(pick(b, 1, 1 - sx), "seq", 1)
-    both = jnp.concatenate([a, b], axis=-1).reshape(2, 2, block, columns.shape[1])
-    both = pick(both, 0, upper) + swapped(pick(both, 0, 1 - upper), "batch", 2)
-    own = pick(both, 0, parity)
-    other = swapped(pick(both, 0, 1 - parity), "batch", 1)
-    low = jnp.where(parity == 0, own, other)
-    high = jnp.where(parity == 0, other, own)
-    return jnp.concatenate([low, high], axis=1)
+    part = part.reshape(-1, 2, 2, 2, 2, part.shape[1] // 16).transpose(4, 3, 1, 2, 0, 5)
+    for axis, bit, index in (("seq", 1, s % 2), ("seq", 2, s // 2), ("batch", 2, z // 2), ("batch", 1, z % 2)):
+        pick = lambda which: lax.dynamic_index_in_dim(part, which, 0, False)
+        part = pick(index) + swapped(pick(1 - index), axis, bit)
+    return part
 
 
 def everywhere_sum(values):
@@ -391,11 +563,15 @@
     inv_rms = lax.rsqrt(jnp.mean(hidden_f * hidden_f, axis=-1, keepdims=True) + EPSILON)
     normed = (hidden_f * inv_rms * norm_gain).astype(BF16)
     grad_mix = (cotangent.reshape(rows, model).astype(F32) * mask).astype(BF16)
-    w_z, w_x = gate_input_weight[:, 0], gate_input_weight[:, 1]
-
-    pre_x = mm(normed, w_x).reshape(seqs, slots, inner)
+    if paired:
+        seq_first = rows_of_seq_first(core_half(normed))
+        mix_far = swapped(core_half(grad_mix), "batch", 1)
+
     pre_bc = mm(normed, w_bc).reshape(seqs, slots, 2 * state)
     proj_dt = mm(normed, w_dt)
+    projected = jnp.einsum("tg,gjn->tjn", normed, gate_input_weight, preferred_element_type=F32)
+    gate_z = projected[:, 0].reshape(seqs, slots, inner)
+    pre_x = projected[:, 1].reshape(seqs, slots, inner)
     edges = jnp.concatenate([pre_x[:, slots - EDGE :], pre_bc[:, slots - EDGE :]], axis=2)
     edges = shifted(edges, "seq", 1)
     edge_x, edge_bc = edges[..., :inner], edges[..., inner:]
@@ -421,99 +597,151 @@
     bc_b = S((seqs, slots, state), F32)
     settings = pltpu.CompilerParams(vmem_limit_bytes=VMEM_LIMIT)
 
-    local_out, local_state, total_decay, b_act, c_act, steps = pl.pallas_call(
-        functools.partial(local_kernel, heads, width),
-        grid=grid,
-        in_specs=[
+    local_state, total_decay, b_act, c_act, steps = call(
+        functools.partial(state_kernel, heads, width),
+        [pre_x, edge_x, conv_x, pre_bc, edge_bc, conv_bc, dtraw, params],
+        [
             wide, edge, taps, per_seq(slots, 2 * state), per_seq(EDGE, 2 * state),
             fixed(CONV + 1, 2 * state), by_head(heads), par_spec,
         ],
-        out_specs=[wide, states, line, per_seq(slots, state), per_seq(slots, state), by_head(2 * heads)],
-        out_shape=[
-            wide_s, state_s, S((seqs, 1, inner), F32), bc_b, bc_b,
+        [states, edge, per_seq(slots, state), per_seq(slots, state), by_head(2 * heads)],
+        [
+            state_s, S((seqs, EDGE, inner), F32), bc_b, bc_b,
             S((seqs, groups, slots, 2 * heads), F32),
         ],
-        scratch_shapes=[pltpu.VMEM((slots, slots), F32)],
-        compiler_params=settings,
-        name="scan_local",
-    )(pre_x, edge_x, conv_x, pre_bc, edge_bc, conv_bc, dtraw, params)
-
-    entering = passed_on(total_decay, local_state, False)
-    gate_z = mm(normed, w_z).reshape(seqs, slots, inner)
-    grad_out = mm(grad_mix, w_out, ((1,), (1,))).reshape(seqs, slots, inner)
-
-    y, sums = pl.pallas_call(
+        grid,
+        "scan_state",
+        17,
+    )
+    if paired:
+        local_state, seq_first, grad_mix, steps = tied(local_state, seq_first, grad_mix, steps)
+
+    def mix_back():
+        return mm(grad_mix, w_out, ((1,), (1,))).reshape(seqs, slots, inner)
+
+    def scan_inside(_):
+        return call(
+            functools.partial(inside_kernel, heads, width),
+            [pre_x, edge_x, conv_x, steps, params, b_act, c_act],
+            [wide, edge, taps, by_head(2 * heads), par_spec, per_seq(slots, state), per_seq(slots, state)],
+            wide,
+            wide_s,
+            grid,
+            "scan_inside",
+            18,
+            scratch=[pltpu.VMEM((slots, slots), F32)],
+        )
+
+    entering, grad_out, local_out = passed_on(total_decay, local_state, False, mix_back, scan_inside)
+    if paired:
+        entering, mix_far, seq_first = tied(entering, mix_far, seq_first)
+        seq_second = rows_of_seq_second(*seq_first)
+
+    y, sums = call(
         functools.partial(gate_kernel, heads, width),
-        grid=grid,
-        in_specs=[wide, states, per_seq(slots, state), by_head(2 * heads), wide, wide, gain_spec],
-        out_specs=[wide, per_seq(slots, 2)],
-        out_shape=[wide_s, S((seqs, slots, 2), F32)],
-        compiler_params=settings,
-        name="gate",
-    )(local_out, entering, c_act, steps, gate_z, grad_out, gain)
+        [local_out, entering, c_act, steps, gate_z, grad_out, gain],
+        [wide, states, per_seq(slots, state), by_head(2 * heads), wide, wide, gain_spec],
+        [wide, per_seq(slots, 2)],
+        [wide_s, S((seqs, slots, 2), F32)],
+        grid,
+        "gate",
+        15,
+    )
     sums = head_sum(sums)
 
-    gated, grad_y, grad_z, gain_grad, leaving = pl.pallas_call(
+    gated, grad_y, grad_z, gain_grad, leaving = call(
         functools.partial(gate_back_kernel, heads, width, inner_all),
-        grid=grid,
-        in_specs=[wide, wide, wide, gain_spec, per_seq(slots, 2), per_seq(slots, state), by_head(2 * heads)],
-        out_specs=[wide, wide, wide, line, states],
-        out_shape=[wide_b, wide_s, wide_b, S((seqs, 1, inner), F32), state_s],
-        compiler_params=settings,
-        name="gate_back",
-    )(y, gate_z, grad_out, gain, sums, c_act, steps)
+        [y, gate_z, grad_out, gain, sums, c_act, steps],
+        [wide, wide, wide, gain_spec, per_seq(slots, 2), per_seq(slots, state), by_head(2 * heads)],
+        [wide, wide, wide, line, states],
+        [wide_b, wide_s, wide_b, S((seqs, 1, inner), F32), state_s],
+        grid,
+        "gate_back",
+        17,
+    )
     gated = gated.reshape(rows, inner)
     grad_z = grad_z.reshape(rows, inner)
 
-    coming = passed_on(total_decay, leaving, True)
+    def scan_inside_back():
+        inside, grad_bc = call(
+            functools.partial(inside_back_kernel, heads, width),
+            [pre_x, edge_x, conv_x, steps, params, b_act, c_act, grad_y, entering],
+            [
+                wide, edge, taps, by_head(2 * heads), par_spec, per_seq(slots, state), per_seq(slots, state),
+                wide, states,
+            ],
+            [wide, per_seq(slots, 2 * state)],
+            [wide_s, S((seqs, slots, 2 * state), F32)],
+            grid,
+            "scan_inside_back",
+            26,
+            scratch=[pltpu.VMEM((slots, slots), F32), pltpu.VMEM((slots, slots), F32)],
+        )
+        if not paired:
+            return inside, grad_bc
+        return inside, grad_bc, seq_second
+
+    def rows_ready(beside):
+        if not paired:
+            return ()
+        return assembled(rows_of_seq_third(*beside[2])), gated_far, mm(gated, w_out)
 
     if paired:
-        mix_rows = pair_rows(grad_mix)
-        normed_rows = pair_rows(normed)
-        grad_w_out = pair_grad(mix_rows, pair_columns(gated)).T
-        grad_w_z = pair_grad(normed_rows, pair_columns(grad_z))
-
-    mixed = head_sum(mm(gated, w_out))
+        parity = lax.axis_index("batch") % 2
+        gated_own = halves(gated, 1, parity).astype(F32)
+        gated_far = swapped(halves(gated, 1, 1 - parity).astype(F32), "batch", 1)
+
+    coming, beside, ready = passed_on(total_decay, leaving, True, scan_inside_back, rows_ready)
+    inside, grad_bc = beside[:2]
+    if paired:
+        normed_far, gated_far, mixed = ready
+        coming, grad_z_sent, ready = tied(coming, grad_z, ready)
+        z_columns = columns_of(grad_z_sent, "seq")
+    else:
+        mixed = mm(gated, w_out)
+    mixed = head_sum(mixed)
     mixed_out = (mask * (hidden_f + mixed)).astype(BF16).reshape(seqs, slots, model)
 
-    (
-        grad_pre, tail_x, first_x, taps_grad_x, grad_dt, params_grad, grad_bc,
-    ) = pl.pallas_call(
+    grad_pre, tail_x, first_x, taps_grad_x, grad_dt, params_grad, grad_b = call(
         functools.partial(scan_back_kernel, heads, width),
-        grid=grid,
-        in_specs=[
+        [pre_x, edge_x, conv_x, dtraw, params, steps, b_act, y, grad_y, inside, entering, coming],
+        [
             wide, edge, taps, by_head(heads), par_spec, by_head(2 * heads), per_seq(slots, state),
-            per_seq(slots, state), wide, wide, states, states,
+            wide, wide, wide, states, states,
         ],
-        out_specs=[
+        [
             wide, edge, edge, edge, by_head(heads),
-            pl.BlockSpec((1, 1, 3, heads), lambda b, g: (b, g, 0, 0)), per_seq(slots, 2 * state),
+            pl.BlockSpec((1, 1, 3, heads), lambda b, g: (b, g, 0, 0)), per_seq(slots, state),
         ],
-        out_shape=[
+        [
             wide_b, S((seqs, EDGE, inner), F32), S((seqs, EDGE, inner), F32), S((seqs, EDGE, inner), F32),
             S((seqs, groups, slots, heads), F32), S((seqs, groups, 3, heads), F32),
-            S((seqs, slots, 2 * state), F32),
+            S((seqs, slots, state), F32),
         ],
-        scratch_shapes=[pltpu.VMEM((slots, slots), F32), pltpu.VMEM((slots, slots), F32)],
-        compiler_params=settings,
-        name="scan_back",
-    )(pre_x, edge_x, conv_x, dtraw, params, steps, b_act, c_act, y, grad_y, entering, coming)
+        grid,
+        "scan_back",
+        34,
+    )
+    if paired:
+        grad_pre, z_columns, grad_dt, grad_b = tied(grad_pre, z_columns, grad_dt, grad_b)
+    grad_bc = grad_bc + jnp.pad(grad_b, ((0, 0), (0, 0), (0, state)))
     grad_bc = head_sum(grad_bc)
 
     one = lambda *shape: pl.BlockSpec((1,) + shape, lambda b: (b, 0, 0))
     rows8 = S((seqs, EDGE, 2 * state), F32)
-    grad_pre_bc, tail_bc, first_bc, taps_grad_bc = pl.pallas_call(
+    grad_pre_bc, tail_bc, first_bc, taps_grad_bc = call(
         conv_back_kernel,
-        grid=(seqs,),
-        in_specs=[
+        [pre_bc, edge_bc, conv_bc, grad_bc],
+        [
             one(slots, 2 * state), one(EDGE, 2 * state),
             pl.BlockSpec((CONV + 1, 2 * state), lambda b: (0, 0)), one(slots, 2 * state),
         ],
-        out_specs=[one(slots, 2 * state), one(EDGE, 2 * state), one(EDGE, 2 * state), one(EDGE, 2 * state)],
-        out_shape=[S((seqs, slots, 2 * state), BF16), rows8, rows8, rows8],
-        compiler_params=settings,
-        name="conv_back",
-    )(pre_bc, edge_bc, conv_bc, grad_bc)
+        [one(slots, 2 * state), one(EDGE, 2 * state), one(EDGE, 2 * state), one(EDGE, 2 * state)],
+        [S((seqs, slots, 2 * state), BF16), rows8, rows8, rows8],
+        (seqs,),
+        "conv_back",
+        3,
+    )
 
     def mended(value, tail, first, weights):
         later = shifted(first, "seq", -1)
@@ -528,32 +756,29 @@
     grad_pre_bc = mended(grad_pre_bc, tail_bc, first_bc, conv_bc).reshape(rows, 2 * state)
     grad_dtr = grad_dt.transpose(0, 2, 1, 3).reshape(rows, heads_dev).astype(BF16)
 
-    portion = mm(grad_z, w_z, ((1,), (1,))) + mm(grad_pre, w_x, ((1,), (1,)))
-    portion = portion + mm(grad_dtr, w_dt, ((1,), (1,)))
-    grad_normed = head_sum(portion) + mm(grad_pre_bc, w_bc, ((1,), (1,)))
-    scaled_input = hidden_f * inv_rms
-    grad_norm_gain = jnp.sum(grad_normed * scaled_input, axis=0)
-    grad_scaled = grad_normed * norm_gain
-    input_dot = jnp.mean(grad_scaled * scaled_input, axis=-1, keepdims=True)
-    grad_hidden = grad_mix.astype(F32) + inv_rms * (grad_scaled - scaled_input * input_dot)
-    grad_hidden = grad_hidden.reshape(seqs, slots, model)
-
+    grad_zx = jnp.stack([grad_z, grad_pre], axis=1)
     if paired:
-        bc_half = halves(grad_pre_bc, 1, side)
-        fill = jnp.zeros((rows, state - heads_dev), BF16)
-        half = inner // 2
-        columns = jnp.concatenate(
-            [grad_pre[:, :half], bc_half, grad_pre[:, half:], grad_dtr, fill], axis=1
-        )
-        grad_w_x = pair_grad(normed_rows, pair_columns(columns))
-        bc_mine = grad_w_x[:, half : half + state]
+        x_columns = columns_of(grad_pre, "seq")
+        part_z = weight_part(normed, normed_far, z_columns, "seq")
+        grad_w_z = weight_done(part_z)
+        part_out = weight_part(grad_mix, assembled(mix_far[None]), [gated_own, gated_far], "batch", after=(part_z,))
+        x_columns, part_out = tied(x_columns, part_out)
+        part_x = weight_part(normed, normed_far, x_columns, "seq")
+        grad_w_x = weight_done(part_x)
+        small = jnp.concatenate([halves(grad_pre_bc, 1, side), grad_dtr], axis=1)
+        part_small = mm(small, normed, ((0,), (0,)))
+        part_x, part_small, grad_zx = tied(part_x, part_small, grad_zx)
+        grad_w_out = pair_done(part_out)
+        done_small = small_done(part_small)
+        bc_mine = done_small[:state]
         bc_other = swapped(bc_mine, "head", 1)
         grad_w_bc = jnp.concatenate(
-            [jnp.where(side == 0, bc_mine, bc_other), jnp.where(side == 0, bc_other, bc_mine)], axis=1
+            [jnp.where(side == 0, bc_mine, bc_other), jnp.where(side == 0, bc_other, bc_mine)], axis=0
+        ).T
+        grad_w_dt = done_small[state:].T
+        grad_weight = jnp.stack(
+            [grad_w_z.reshape(inner, model // 16).T, grad_w_x.reshape(inner, model // 16).T], axis=1
         )
-        grad_w_dt = grad_w_x[:, inner + state : inner + state + heads_dev]
-        grad_w_x = jnp.concatenate([grad_w_x[:, :half], grad_w_x[:, half + state : inner + state]], axis=1)
-        grad_weight = jnp.stack([grad_w_z, grad_w_x], axis=1)
     else:
         scatter = functools.partial(lax.psum_scatter, axis_name=("batch", "seq"), tiled=True)
         over_slots = ((0,), (0,))
@@ -564,6 +789,16 @@
         grad_w_bc = scatter(mm(normed, grad_pre_bc, over_slots), scatter_dimension=0)
         grad_w_dt = scatter(mm(normed, grad_dtr, over_slots), scatter_dimension=0)
         grad_w_out = scatter(mm(gated, grad_mix, over_slots), scatter_dimension=1)
+
+    portion = jnp.einsum("tjn,gjn->tg", grad_zx, gate_input_weight, preferred_element_type=F32)
+    portion = portion + mm(grad_dtr, w_dt, ((1,), (1,)))
+    grad_normed = head_sum(portion) + mm(grad_pre_bc, w_bc, ((1,), (1,)))
+    scaled_input = hidden_f * inv_rms
+    grad_norm_gain = jnp.sum(grad_normed * scaled_input, axis=0)
+    grad_scaled = grad_normed * norm_gain
+    input_dot = jnp.mean(grad_scaled * scaled_input, axis=-1, keepdims=True)
+    grad_hidden = grad_mix.astype(F32) + inv_rms * (grad_scaled - scaled_input * input_dot)
+    grad_hidden = grad_hidden.reshape(seqs, slots, model)
 
     head_grad = params_grad.sum(axis=0).transpose(1, 0, 2).reshape(3, heads_dev)
     taps_sum = jnp.concatenate([taps_grad_x.sum(axis=0), taps_grad_bc.sum(axis=0)], axis=1)[: CONV + 1]

time: 1130 us -> 635 us (0.56)
  waiting for transfers between devices: 619 us -> 162 us
  Pallas kernels: 122 us -> 169 us
  matrix products: 123 us -> 77.6 us
  local copies, waits for them, and re-layouts: 125 us -> 80.5 us
    ppermute x34 -> x51, waiting for transfers between devices: 471 us -> 137 us  [swapped(): return lax.ppermute(value, axis, [(i, i ^ bit) for i in range(count)])]
    all_gather x2 -> x0, waiting for transfers between devices: 141 us -> none  [passed_on(): gathered = lax.all_gather(both, 'seq')]
    dot_general x13 -> x7, matrix products: 123 us -> 38.8 us  [mm(): lax.dot_general(a, b, (dims, ((), ())), precision=precision, preferred_el...]
    pallas_call x12, Pallas kernels: 122 us -> 169 us  [call(): pl.pallas_call(body, grid=grid, in_specs=list(in_specs) + [pl.BlockSpec(m...]
    dot_general x0 -> x2, matrix products: none -> 38.8 us  [the longest x1 24.9 us: per_device(): jnp.einsum('tjn,gjn->tg', grad_zx, gate_input_weight, preferred_element_t...]
    slice x9, local copies, waits for them, and re-layouts: 46.7 us -> 10.2 us  [the longest x1 4.07 us: scattered_over_seq(): a, b = (part[:, :, :2], part[:, :, 2:])]
    dynamic_slice x11 -> x5, local copies, waits for them, and re-layouts: 28.1 us -> 2.86 us  [the longest x3 1.54 us: small_done(): pick = lambda which: lax.dynamic_index_in_dim(part, which, 0, False)]
    ppermute x3, waiting for transfers between devices: 7.48 us -> 24.6 us  [shifted(): lax.ppermute(value, axis, [(source, source + steps) for source in range(i...]
  transfers between devices with their start and end apart: 39 -> 56, of which waited for: 20 -> 21; matrix products, arithmetic and copies ran while one was open for 16% -> 26% of each run, Pallas kernels for 2% -> 25%
where the time goes in v2:
time: 635 us; the launch traced here: 626 us
  Pallas kernels  169 us (27%)
  waiting for transfers between devices  162 us (26%)
  local copies, waits for them, and re-layouts  80.5 us (13%)
  matrix products  77.6 us (12%)
  other arithmetic  66.7 us (11%)
  starting transfers between devices  54.9 us (9%)
  between operations  15.6 us (2%)
    pallas_call x12, Pallas kernels, call(): pl.pallas_call(body, grid=grid, in_specs=list(in_specs) + [pl.BlockSpec(m...  169 us
    ppermute x51, waiting for transfers between devices, swapped(): return lax.ppermute(value, axis, [(i, i ^ bit) for i in range(count)])  137 us
    ppermute x51, starting transfers between devices, swapped(): return lax.ppermute(value, axis, [(i, i ^ bit) for i in range(count)])  46.7 us
    dot_general x7, matrix products, mm(): lax.dot_general(a, b, (dims, ((), ())), precision=precision, preferred_el...  38.8 us
    unnamed x165, local copies, waits for them, and re-layouts  26.7 us
    dot_general x1, matrix products, per_device(): jnp.einsum('tjn,gjn->tg', grad_zx, gate_input_weight, preferred_element_t...  24.9 us
    ppermute x3, waiting for transfers between devices, shifted(): lax.ppermute(value, axis, [(source, source + steps) for source in range(i...  24.6 us
    dot_general x1, matrix products, per_device(): jnp.einsum('tg,gjn->tjn', normed, gate_input_weight, preferred_element_ty...  13.9 us
  transfers between devices with their start and end apart: 56, of which 21 were waited for; matrix products, arithmetic and copies ran while one was open for 26% of the time, Pallas kernels for 25%

profile of v2, /device:TPU:0, one launch (start us, length us, event | category | flops | bytes accessed | tf_op | source)
XLA Modules:
  0.0 625.9 jit_solution(9633512449340894822)
XLA Ops:
  11.3 13.9 %fusion.2 = f32[512,2,2048]{2,0,1:T(8,128)S(1)} fusion(bf16[2048,2,2048]{2,1,0:T(2,128)(2,1)} %param.14, bf16[512,2048]{1,0:T(8,128)(2,1)S(1)} %fusion.9.refs_0_), kind=kOutput, calls=%fused_computation.2 | convolution fusion | flops 8589934592 | bytes 27262976 | tf_op jit(solution)/shard_map/tg,gjn->tjn/dot_general | solution.py:572
  25.3 2.8 fusion.66
  30.2 5.5 collective-permute-start
  45.0 5.3 fusion.25.refs_6_.refs_3_
  53.2 17.1 %scan_state.1 = (f32[2,128,2048]{2,1,0:T(8,128)S(1)}, f32[2,8,2048]{2,1,0:T(8,128)S(1)}, f32[2,256,128]{2,1,0:T(8,128)S(1)}, f32[2,256,128]{2,1,0:T(8,128)S(1)}, f32[2,8,256,8]{3,2,1,0:T(8,128)S(1)}) custom-call(f32[2,256,2048]{2,1,0:T(8,128)} %bitcast.270, f32[2,8,2048]{2,1,0:T(8,128)S(1)} %slice.194.refs_1_, f32[5,2048]{1,0:T(8,128)S(1)} %copy-done.27, ...), custom_call_target="tpu_custom_call" | custom-call | flops 4674999808 | bytes 8500000 | tf_op jit(solution)/shard_map/scan_state/pallas_call | solution.py:92
  74.5 9.5 %fusion.72 = f32[512,2048]{1,0:T(8,128)} fusion(bf16[512,2048]{1,0:T(8,128)(2,1)S(1)} %fusion.4.refs_0_, bf16[2048,2048]{1,0:T(8,128)(2,1)} %param.21), kind=kOutput, calls=%fused_computation.196 | convolution fusion | flops 4294967296 | bytes 14680064 | tf_op jit(solution)/shard_map/dot_general | solution.py:22
  86.5 11.3 %collective-permute-done.4 = f32[2,136,512]{2,1,0:T(8,128)S(1)} collective-permute-done((f32[2,136,512]{2,1,0:T(8,128)S(1)}, f32[2,136,512]{2,1,0:T(8,128)S(1)}, u32[]{:S(2)}, u32[]{:S(2)}) %collective-permute-start.4) | collective-permute-done | bytes 557088 | tf_op jit(solution)/shard_map/ppermute | solution.py:344
  102.2 18.4 %scan_inside.1.refs_0_ = f32[2,256,2048]{2,1,0:T(8,128)} custom-call(f32[2,256,2048]{2,1,0:T(8,128)} %bitcast.271, f32[2,8,2048]{2,1,0:T(8,128)S(1)} %slice.194.refs_1_, f32[5,2048]{1,0:T(8,128)S(1)} %copy-done.27, f32[2,8,256,8]{3,2,1,0:T(8,128)S(1)} %get-tuple-element.101.refs_3_.refs_6_.refs_5_, f32[8,3,4]{2,1,0:T(4,128)S(1)} %bitcast.259, ...), custom_call_target="tpu_custom_call" | custom-call | flops 4950000128 | bytes 9000000 | tf_op jit(solution)/shard_map/scan_inside/pallas_call | solution.py:92
  122.7 3.8 pad_maximum_fusion.2
  127.6 3.0 pad_maximum_fusion.3
  131.4 14.6 %gate.1 = (f32[2,256,2048]{2,1,0:T(8,128)}, f32[2,256,2]{2,1,0:T(8,128)S(1)}) custom-call(f32[2,256,2048]{2,1,0:T(8,128)} %scan_inside.1.refs_0_, f32[2,128,2048]{2,1,0:T(8,128)S(1)} %pad_maximum_fusion.1.refs_1_.refs_8_.refs_10_, f32[2,256,128]{2,1,0:T(8,128)S(1)} %get-tuple-element.103.refs_6_.refs_2_.refs_5_, ...), custom_call_target="tpu_custom_call" | custom-call | flops 4124999936 | bytes 7500000 | tf_op jit(solution)/shard_map/gate/pallas_call | solution.py:92
  147.5 16.6 %gate_back.1 = (bf16[2,256,2048]{2,1,0:T(8,128)(2,1)S(1)}, f32[2,256,2048]{2,1,0:T(8,128)}, bf16[2,256,2048]{2,1,0:T(8,128)(2,1)S(1)}, f32[2,1,2048]{2,1,0:T(1,128)S(1)}, f32[2,128,2048]{2,1,0:T(8,128)}) custom-call(f32[2,256,2048]{2,1,0:T(8,128)} %get-tuple-element.115.refs_0_.refs_7_, f32[2,256,2048]{2,1,0:T(8,128)} %bitcast.266, ...), custom_call_target="tpu_custom_call" | custom-call | flops 4674999808 | bytes 8500000 | tf_op jit(solution)/shard_map/gate_back/pallas_call | solution.py:92
  164.8 3.3 constant_dynamic-update-slice_fusion.4
  172.7 25.7 %scan_inside_back.1 = (f32[2,256,2048]{2,1,0:T(8,128)}, f32[2,256,256]{2,1,0:T(8,128)S(1)}) custom-call(f32[2,256,2048]{2,1,0:T(8,128)} %bitcast.272, f32[2,8,2048]{2,1,0:T(8,128)S(1)} %slice.194.refs_1_, f32[5,2048]{1,0:T(8,128)S(1)} %copy-done.27, f32[2,8,256,8]{3,2,1,0:T(8,128)S(1)} %copy-done.15, f32[8,3,4]{2,1,0:T(4,128)S(1)} %bitcast.260, ...), custom_call_target="tpu_custom_call" | custom-call | flops 7150000128 | bytes 13000000 | tf_op jit(solution)/shard_map/scan_inside_back/pallas_call | solution.py:92
  201.4 4.7 maximum_maximum_fusion.refs_0_
  206.3 3.4 dynamic-slice_convert_fusion.2
  214.6 9.4 %fusion.73 = f32[512,2048]{1,0:T(8,128)} fusion(bf16[512,2048]{1,0:T(8,128)(2,1)S(1)} %bitcast.255, bf16[2048,2048]{1,0:T(8,128)(2,1)} %param.21), kind=kOutput, calls=%fused_computation.197 | convolution fusion | flops 4294967296 | bytes 14680064 | tf_op jit(solution)/shard_map/dot_general | solution.py:22
  224.0 8.2 %assemble.2.refs_1_ = bf16[3,512,2048]{2,1,0:T(8,128)(2,1)} custom-call(f32[3,512,1024]{2,1,0:T(8,128)} %maximum_maximum_fusion.refs_0_, f32[3,512,1024]{2,1,0:T(8,128)} %collective-permute-done.19.refs_1_, s32[1]{0:T(128)} %bitcast.20.refs_2_), custom_call_target="tpu_custom_call" | custom-call | flops 2475000064 | bytes 4500000 | tf_op jit(solution)/shard_map/assemble/pallas_call | solution.py:92
  232.2 25.4 %collective-permute-done.20.refs_3_ = f32[512,1024]{1,0:T(8,128)S(1)} collective-permute-done((f32[512,1024]{1,0:T(8,128)S(1)}, f32[512,1024]{1,0:T(8,128)S(1)}, u32[]{:S(2)}, u32[]{:S(2)}) %collective-permute-start.20) | collective-permute-done | bytes 2097184 | tf_op jit(solution)/shard_map/ppermute | solution.py:344
  264.8 34.0 %scan_back.1 = (bf16[2,256,2048]{2,1,0:T(8,128)(2,1)S(1)}, f32[2,8,2048]{2,1,0:T(8,128)S(1)}, f32[2,8,2048]{2,1,0:T(8,128)S(1)}, f32[2,8,2048]{2,1,0:T(8,128)S(1...) custom-call(f32[2,256,2048]{2,1,0:T(8,128)} %bitcast.273, ...), custom_call_target="tpu_custom_call" | custom-call | flops 9349999616 | bytes 17000000 | tf_op jit(solution)/shard_map/scan_back/pallas_call | solution.py:92
  303.3 6.1 collective-permute-done.23.refs_4_
  309.4 9.1 %weight_part.3.refs_4_ = f32[4,4,512,128]{3,2,1,0:T(8,128)} custom-call(bf16[512,2048]{1,0:T(8,128)(2,1)} %copy-done.38, bf16[3,512,2048]{2,1,0:T(8,128)(2,1)} %assemble.2.refs_1_, f32[512,512]{1,0:T(8,128)S(1)} %get-tuple-element.152.refs_2_, f32[512,512]{1,0:T(8,128)S(1)} %collective-permute-done.22.refs_3_, ...), custom_call_target="tpu_custom_call" | custom-call | flops 2475000064 | bytes 4500000 | tf_op jit(solution)/shard_map/weight_part/pallas_call | solution.py:92
  323.2 3.4 assemble.3.refs_1_
  338.2 3.9 dynamic-slice_convert_fusion.4
  345.8 2.7 fusion.74
  354.6 10.0 %weight_part.4 = f32[4,4,1024,128]{3,2,1,0:T(8,128)} custom-call(bf16[512,2048]{1,0:T(8,128)(2,1)S(1)} %fusion.4.refs_0_, bf16[1,512,2048]{2,1,0:T(8,128)(2,1)S(1)} %copy-done.2, f32[512,1024]{1,0:T(8,128)} %get-tuple-element.231.refs_2_, f32[512,1024]{1,0:T(8,128)} %copy-done.53, f32[4,4,512,128]{3,2,1,0:T(8,128)} %weight_part.3.refs_4_), custom_call_target="tpu_custom_call" | custom-call | flops 2475000064 | bytes 4500000 | tf_op jit(solution)/shard_map/weight_part/pallas_call | solution.py:92
  366.1 24.3 %collective-permute-done.31 = f32[2,8,256]{2,1,0:T(8,128)} collective-permute-done((f32[2,8,256]{2,1,0:T(8,128)}, f32[2,8,256]{2,1,0:T(8,128)}, u32[]{:S(2)}, u32[]{:S(2)}) %collective-permute-start.31) | collective-permute-done | bytes 16416 | tf_op jit(solution)/shard_map/ppermute | solution.py:350
  393.3 3.4 fusion.40
  396.8 10.0 %weight_part.5 = f32[4,4,512,128]{3,2,1,0:T(8,128)} custom-call(bf16[512,2048]{1,0:T(8,128)(2,1)} %copy-done.38, bf16[3,512,2048]{2,1,0:T(8,128)(2,1)} %assemble.2.refs_1_, f32[512,512]{1,0:T(8,128)S(1)} %copy-done.9, f32[512,512]{1,0:T(8,128)} %collective-permute-done.26.refs_3_, f32[512,512]{1,0:T(8,128)} %collective-permute-done.27.refs_4_, ...), custom_call_target="tpu_custom_call" | custom-call | flops 2475000064 | bytes 4500000 | tf_op jit(solution)/shard_map/weight_part/pallas_call | solution.py:92
  406.8 3.2 reshape.201
  410.0 4.2 constant_dynamic-slice_fusion.4
  414.2 2.7 collective-permute-start.43
  417.0 4.1 fusion.65
  427.4 24.9 %bitcast_add_fusion = f32[512,2048]{1,0:T(8,128)} fusion(f32[512,2048]{1,0:T(8,128)S(1)} %copy-done.49, bf16[512,2,2048]{2,0,1:T(8,128)(2,1)} %pad_maximum_fusion, bf16[2048,2,2048]{2,1,0:T(2,128)(2,1)} %param.14), kind=kOutput, calls=%fused_computation.8 | convolution fusion | flops 8590983168 | bytes 29360128 | tf_op jit(solution)/shard_map/tjn,gjn->tg/dot_general | solution.py:793
  459.4 17.2 %collective-permute-done.44 = f32[2,2,160,128]{3,1,0,2:T(2,128)} collective-permute-done((f32[2,2,160,128]{3,1,0,2:T(2,128)}, f32[2,2,160,128]{3,1,0,2:T(2,128)}, u32[]{:S(2)}, u32[]{:S(2)}) %collective-permute-start.44) | collective-permute-done | bytes 327712 | tf_op jit(solution)/shard_map/ppermute | solution.py:344
  478.0 2.7 collective-permute-start.45
  493.2 4.1 collective-permute-done.46
  498.3 9.4 %collective-permute-done.51 = f32[2,1024,128]{2,1,0:T(8,128)} collective-permute-done((f32[2,1024,128]{2,1,0:T(8,128)}, f32[2,1024,128]{2,1,0:T(8,128)}, u32[]{:S(2)}, u32[]{:S(2)}) %collective-permute-start.51) | collective-permute-done | bytes 1048608 | tf_op jit(solution)/shard_map/ppermute | solution.py:344
  517.2 7.6 %fusion.14 = (f32[2048]{0:T(1024)S(1)}, f32[512]{0:T(512)S(1)}, f32[512,2048]{1,0:T(8,128)}) fusion(bf16[2,256,2048]{2,1,0:T(8,128)(2,1)} %param.12, f32[512]{0:T(512)S(1)} %bitcast.304, f32[2048]{0:T(1024)S(1)} %copy-done.67, f32[512,2048]{1,0:T(8,128)} %bitcast_add_fusion, f32[512,2048]{1,0:T(8,128)} %collective-permute-done.32, ...), kind=kOutput, calls=%fused_computation.22 | convolution fusion | flops 546305536 | bytes 16011264 | tf_op jit(solution)/shard_map/dot_general | solution.py:22
  527.0 34.4 %collective-permute-done.52 = f32[2,1024,128]{2,1,0:T(8,128)} collective-permute-done((f32[2,1024,128]{2,1,0:T(8,128)}, f32[2,1024,128]{2,1,0:T(8,128)}, u32[]{:S(2)}, u32[]{:S(2)}) %collective-permute-start.52) | collective-permute-done | bytes 1048608 | tf_op jit(solution)/shard_map/ppermute | solution.py:344
  563.9 3.5 collective-permute-done.34
  570.4 2.9 collective-permute-done.35
  573.4 7.3 %fusion.13 = (f32[512,2048]{1,0:T(8,128)}, bf16[512,2048]{1,0:T(8,128)(2,1)}) fusion(bf16[2,256,2048]{2,1,0:T(8,128)(2,1)S(1)} %copy-done.40, bf16[512,2048]{1,0:T(8,128)(2,1)S(1)} %fusion.4.refs_0_, f32[512,2048]{1,0:T(8,128)} %get-tuple-element.208, f32[512]{0:T(512)S(1)} %broadcast_multiply_fusion, f32[2048]{0:T(1024)S(1)} %copy-done.67, ...), kind=kLoop, calls=%fused_computation.21 | loop fusion | flops 12582912 | bytes 23083008 | tf_op jit(solution)/shard_map/add | solution.py:800
  593.3 5.6 collective-permute-done.38
  598.8 2.6 collective-permute-start.42
  603.7 3.5 collective-permute-done.40
  607.2 2.8 collective-permute-done.42
  615.9 2.9 copy.63
  (374 shorter events, 155.4 us)
Async XLA Ops:
  7.2 576.3 %reduce-scatter.3.cloned.1.call-start = ((), (), s32[]{:S(2)}) async-start(), calls=%async_computation.2 | async-start | bytes 5242880 | tf_op jit(solution)/shard_map/reduce_scatter | solution.py:499
  30.2 20.2 %collective-permute-start = (f32[2,8,2304]{2,1,0:T(8,128)S(1)}, f32[2,8,2304]{2,1,0:T(8,128)}, u32[]{:S(2)}, u32[]{:S(2)}) collective-permute-start(f32[2,8,2304]{2,1,0:T(8,128)S(1)} %pad_maximum_fusion.10), channel_id=1, source_target_pairs={{0,2},{2,4},{4,6},{1,3},{3,5},{5,7},{8,10},{10,12},{12,14},{9,11},... | collective-permute-start | bytes 442376 | tf_op jit(solution)/shard_map/ppermute | solution.py:350
  38.7 31.6 %collective-permute-start.1 = (f32[512,512]{1,0:T(8,128)}, f32[512,512]{1,0:T(8,128)}, u32[]{:S(2)}, u32[]{:S(2)}) collective-permute-start(f32[512,512]{1,0:T(8,128)} %get-tuple-element.122), channel_id=1, source_target_pairs={{0,2},{2,0},{4,6},{6,4},{1,3},{3,1},{5,7},{7,5},{8,10},{10,8},{12,... | collective-permute-start | bytes 3145736 | tf_op jit(solution)/shard_map/ppermute | solution.py:344
  39.6 30.8 %collective-permute-start.2 = (f32[512,512]{1,0:T(8,128)}, f32[512,512]{1,0:T(8,128)}, u32[]{:S(2)}, u32[]{:S(2)}) collective-permute-start(f32[512,512]{1,0:T(8,128)} %get-tuple-element.124), channel_id=1, source_target_pairs={{0,4},{2,6},{4,0},{6,2},{1,5},{3,7},{5,1},{7,3},{8,12},{10,14},{12... | collective-permute-start | bytes 3145736 | tf_op jit(solution)/shard_map/ppermute | solution.py:344
  43.3 79.4 %collective-permute-start.9 = (f32[512,1024]{1,0:T(8,128)}, f32[512,1024]{1,0:T(8,128)}, u32[]{:S(2)}, u32[]{:S(2)}) collective-permute-start(f32[512,1024]{1,0:T(8,128)} %dynamic-slice_convert_fusion), channel_id=1, source_target_pairs={{0,8},{8,0},{16,24},{24,16},{1,9},{9,1},{17,25},{25,17},{2,10},{10... | collective-permute-start | bytes 6291464 | tf_op jit(solution)/shard_map/ppermute | solution.py:344
  70.8 15.7 %collective-permute-start.3 = (f32[2,136,512]{2,1,0:T(8,128)S(1)}, f32[2,136,512]{2,1,0:T(8,128)S(1)}, u32[]{:S(2)}, u32[]{:S(2)}) collective-permute-start(f32[2,136,512]{2,1,0:T(8,128)S(1)} %get-tuple-element.227), channel_id=1, source_target_pairs={{0,2},{2,0},{4,6},{6,4},{1,3},{3,1},{5,7},{7,5},{8,10},{10,8},{12,... | collective-permute-start | bytes 1671176 | tf_op jit(solution)/shard_map/ppermute | solution.py:344
  73.0 24.9 %collective-permute-start.4 = (f32[2,136,512]{2,1,0:T(8,128)S(1)}, f32[2,136,512]{2,1,0:T(8,128)S(1)}, u32[]{:S(2)}, u32[]{:S(2)}) collective-permute-start(f32[2,136,512]{2,1,0:T(8,128)S(1)} %get-tuple-element.226), channel_id=1, source_target_pairs={{0,4},{2,6},{4,0},{6,2},{1,5},{3,7},{5,1},{7,3},{8,12},{10,14},{12... | collective-permute-start | bytes 1671176 | tf_op jit(solution)/shard_map/ppermute | solution.py:344
  74.1 23.7 %collective-permute-start.5 = (f32[2,136,512]{2,1,0:T(8,128)S(1)}, f32[2,136,512]{2,1,0:T(8,128)S(1)}, u32[]{:S(2)}, u32[]{:S(2)}) collective-permute-start(f32[2,136,512]{2,1,0:T(8,128)S(1)} %get-tuple-element.225), channel_id=1, source_target_pairs={{0,6},{2,4},{4,2},{6,0},{1,7},{3,5},{5,3},{7,1},{8,14},{10,12},{12... | collective-permute-start | bytes 1671176 | tf_op jit(solution)/shard_map/ppermute | solution.py:344
  98.7 22.0 %collective-permute-start.6 = (f32[2,128,512]{2,1,0:T(8,128)S(1)}, f32[2,128,512]{2,1,0:T(8,128)S(1)}, u32[]{:S(2)}, u32[]{:S(2)}) collective-permute-start(f32[2,128,512]{2,1,0:T(8,128)S(1)} %get-tuple-element.265), channel_id=1, source_target_pairs={{0,2},{2,0},{4,6},{6,4},{1,3},{3,1},{5,7},{7,5},{8,10},{10,8},{12,... | collective-permute-start | bytes 1572872 | tf_op jit(solution)/shard_map/ppermute | solution.py:344
  99.6 22.5 %collective-permute-start.7 = (f32[2,128,512]{2,1,0:T(8,128)S(1)}, f32[2,128,512]{2,1,0:T(8,128)S(1)}, u32[]{:S(2)}, u32[]{:S(2)}) collective-permute-start(f32[2,128,512]{2,1,0:T(8,128)S(1)} %get-tuple-element.264), channel_id=1, source_target_pairs={{0,4},{2,6},{4,0},{6,2},{1,5},{3,7},{5,1},{7,3},{8,12},{10,14},{12... | collective-permute-start | bytes 1572872 | tf_op jit(solution)/shard_map/ppermute | solution.py:344
  100.7 21.4 %collective-permute-start.8 = (f32[2,128,512]{2,1,0:T(8,128)S(1)}, f32[2,128,512]{2,1,0:T(8,128)S(1)}, u32[]{:S(2)}, u32[]{:S(2)}) collective-permute-start(f32[2,128,512]{2,1,0:T(8,128)S(1)} %get-tuple-element.209), channel_id=1, source_target_pairs={{0,6},{2,4},{4,2},{6,0},{1,7},{3,5},{5,3},{7,1},{8,14},{10,12},{12... | collective-permute-start | bytes 1572872 | tf_op jit(solution)/shard_map/ppermute | solution.py:344
  126.6 71.9 %collective-permute-start.14 = (f32[2,512,512]{2,1,0:T(8,128)}, f32[2,512,512]{2,1,0:T(8,128)}, u32[]{:S(2)}, u32[]{:S(2)}) collective-permute-start(f32[2,512,512]{2,1,0:T(8,128)} %pad_maximum_fusion.2), channel_id=1, source_target_pairs={{0,4},{2,6},{4,0},{6,2},{1,5},{3,7},{5,1},{7,3},{8,12},{10,14},{12... | collective-permute-start | bytes 6291464 | tf_op jit(solution)/shard_map/ppermute | solution.py:344
  130.6 67.9 %collective-permute-start.15 = (f32[2,512,512]{2,1,0:T(8,128)}, f32[2,512,512]{2,1,0:T(8,128)}, u32[]{:S(2)}, u32[]{:S(2)}) collective-permute-start(f32[2,512,512]{2,1,0:T(8,128)} %pad_maximum_fusion.3), channel_id=1, source_target_pairs={{0,2},{2,0},{4,6},{6,4},{1,3},{3,1},{5,7},{7,5},{8,10},{10,8},{12,... | collective-permute-start | bytes 6291464 | tf_op jit(solution)/shard_map/ppermute | solution.py:344
  169.2 29.2 %collective-permute-start.11 = (f32[2,136,512]{2,1,0:T(8,128)S(1)}, f32[2,136,512]{2,1,0:T(8,128)S(1)}, u32[]{:S(2)}, u32[]{:S(2)}) collective-permute-start(f32[2,136,512]{2,1,0:T(8,128)S(1)} %get-tuple-element.220), channel_id=1, source_target_pairs={{0,2},{2,0},{4,6},{6,4},{1,3},{3,1},{5,7},{7,5},{8,10},{10,8},{12,... | collective-permute-start | bytes 1671176 | tf_op jit(solution)/shard_map/ppermute | solution.py:344
  170.5 28.0 %collective-permute-start.12 = (f32[2,136,512]{2,1,0:T(8,128)S(1)}, f32[2,136,512]{2,1,0:T(8,128)S(1)}, u32[]{:S(2)}, u32[]{:S(2)}) collective-permute-start(f32[2,136,512]{2,1,0:T(8,128)S(1)} %get-tuple-element.219), channel_id=1, source_target_pairs={{0,4},{2,6},{4,0},{6,2},{1,5},{3,7},{5,1},{7,3},{8,12},{10,14},{12... | collective-permute-start | bytes 1671176 | tf_op jit(solution)/shard_map/ppermute | solution.py:344
  171.5 26.9 %collective-permute-start.13 = (f32[2,136,512]{2,1,0:T(8,128)S(1)}, f32[2,136,512]{2,1,0:T(8,128)S(1)}, u32[]{:S(2)}, u32[]{:S(2)}) collective-permute-start(f32[2,136,512]{2,1,0:T(8,128)S(1)} %get-tuple-element.218), channel_id=1, source_target_pairs={{0,6},{2,4},{4,2},{6,0},{1,7},{3,5},{5,3},{7,1},{8,14},{10,12},{12... | collective-permute-start | bytes 1671176 | tf_op jit(solution)/shard_map/ppermute | solution.py:344
  206.1 17.9 %collective-permute-start.19 = (f32[3,512,1024]{2,1,0:T(8,128)}, f32[3,512,1024]{2,1,0:T(8,128)}, u32[]{:S(2)}, u32[]{:S(2)}) collective-permute-start(f32[3,512,1024]{2,1,0:T(8,128)} %maximum_maximum_fusion.refs_0_), channel_id=1, source_target_pairs={{0,1},{1,0},{2,3},{3,2},{4,5},{5,4},{6,7},{7,6},{8,9},{9,8},{10,11... | collective-permute-start | bytes 18874376 | tf_op jit(solution)/shard_map/ppermute | solution.py:344
  209.6 48.0 %collective-permute-start.20 = (f32[512,1024]{1,0:T(8,128)S(1)}, f32[512,1024]{1,0:T(8,128)S(1)}, u32[]{:S(2)}, u32[]{:S(2)}) collective-permute-start(f32[512,1024]{1,0:T(8,128)S(1)} %get-tuple-element.232), channel_id=1, source_target_pairs={{0,8},{8,0},{16,24},{24,16},{1,9},{9,1},{17,25},{25,17},{2,10},{10... | collective-permute-start | bytes 6291464 | tf_op jit(solution)/shard_map/ppermute | solution.py:344
  210.8 46.9 %collective-permute-start.16 = (f32[2,128,512]{2,1,0:T(8,128)S(1)}, f32[2,128,512]{2,1,0:T(8,128)S(1)}, u32[]{:S(2)}, u32[]{:S(2)}) collective-permute-start(f32[2,128,512]{2,1,0:T(8,128)S(1)} %get-tuple-element.263), channel_id=1, source_target_pairs={{0,2},{2,0},{4,6},{6,4},{1,3},{3,1},{5,7},{7,5},{8,10},{10,8},{12,... | collective-permute-start | bytes 1572872 | tf_op jit(solution)/shard_map/ppermute | solution.py:344
  212.2 45.4 %collective-permute-start.17 = (f32[2,128,512]{2,1,0:T(8,128)S(1)}, f32[2,128,512]{2,1,0:T(8,128)S(1)}, u32[]{:S(2)}, u32[]{:S(2)}) collective-permute-start(f32[2,128,512]{2,1,0:T(8,128)S(1)} %fusion.38), channel_id=1, source_target_pairs={{0,4},{2,6},{4,0},{6,2},{1,5},{3,7},{5,1},{7,3},{8,12},{10,14},{12... | collective-permute-start | bytes 1572872 | tf_op jit(solution)/shard_map/ppermute | solution.py:344
  213.5 44.2 %collective-permute-start.18 = (f32[2,128,512]{2,1,0:T(8,128)S(1)}, f32[2,128,512]{2,1,0:T(8,128)S(1)}, u32[]{:S(2)}, u32[]{:S(2)}) collective-permute-start(f32[2,128,512]{2,1,0:T(8,128)S(1)} %get-tuple-element.261), channel_id=1, source_target_pairs={{0,6},{2,4},{4,2},{6,0},{1,7},{3,5},{5,3},{7,1},{8,14},{10,12},{12... | collective-permute-start | bytes 1572872 | tf_op jit(solution)/shard_map/ppermute | solution.py:344
  261.2 42.1 %collective-permute-start.22 = (f32[512,512]{1,0:T(8,128)S(1)}, f32[512,512]{1,0:T(8,128)S(1)}, u32[]{:S(2)}, u32[]{:S(2)}) collective-permute-start(f32[512,512]{1,0:T(8,128)S(1)} %get-tuple-element.239), channel_id=1, source_target_pairs={{0,2},{2,0},{4,6},{6,4},{1,3},{3,1},{5,7},{7,5},{8,10},{10,8},{12,... | collective-permute-start | bytes 3145736 | tf_op jit(solution)/shard_map/ppermute | solution.py:344
  262.5 46.9 %collective-permute-start.23 = (f32[512,512]{1,0:T(8,128)S(1)}, f32[512,512]{1,0:T(8,128)S(1)}, u32[]{:S(2)}, u32[]{:S(2)}) collective-permute-start(f32[512,512]{1,0:T(8,128)S(1)} %get-tuple-element.238), channel_id=1, source_target_pairs={{0,4},{2,6},{4,0},{6,2},{1,5},{3,7},{5,1},{7,3},{8,12},{10,14},{12... | collective-permute-start | bytes 3145736 | tf_op jit(solution)/shard_map/ppermute | solution.py:344
  263.6 45.8 %collective-permute-start.24 = (f32[512,512]{1,0:T(8,128)S(1)}, f32[512,512]{1,0:T(8,128)S(1)}, u32[]{:S(2)}, u32[]{:S(2)}) collective-permute-start(f32[512,512]{1,0:T(8,128)S(1)} %get-tuple-element.237), channel_id=1, source_target_pairs={{0,6},{2,4},{4,2},{6,0},{1,7},{3,5},{5,3},{7,1},{8,14},{10,12},{12... | collective-permute-start | bytes 3145736 | tf_op jit(solution)/shard_map/ppermute | solution.py:344
  318.6 271.1 %reduce-scatter.5.cloned.1.call-start = ((), (), s32[]{:S(2)}) async-start(), calls=%async_computation.3 | async-start | bytes 5242880 | tf_op jit(solution)/shard_map/reduce_scatter | solution.py:499
  342.1 54.6 %collective-permute-start.26 = (f32[512,512]{1,0:T(8,128)}, f32[512,512]{1,0:T(8,128)}, u32[]{:S(2)}, u32[]{:S(2)}) collective-permute-start(f32[512,512]{1,0:T(8,128)} %get-tuple-element.235), channel_id=1, source_target_pairs={{0,2},{2,0},{4,6},{6,4},{1,3},{3,1},{5,7},{7,5},{8,10},{10,8},{12,... | collective-permute-start | bytes 3145736 | tf_op jit(solution)/shard_map/ppermute | solution.py:344
  343.8 52.9 %collective-permute-start.27 = (f32[512,512]{1,0:T(8,128)}, f32[512,512]{1,0:T(8,128)}, u32[]{:S(2)}, u32[]{:S(2)}) collective-permute-start(f32[512,512]{1,0:T(8,128)} %get-tuple-element.234), channel_id=1, source_target_pairs={{0,4},{2,6},{4,0},{6,2},{1,5},{3,7},{5,1},{7,3},{8,12},{10,14},{12... | collective-permute-start | bytes 3145736 | tf_op jit(solution)/shard_map/ppermute | solution.py:344
  345.4 51.4 %collective-permute-start.28 = (f32[512,512]{1,0:T(8,128)}, f32[512,512]{1,0:T(8,128)}, u32[]{:S(2)}, u32[]{:S(2)}) collective-permute-start(f32[512,512]{1,0:T(8,128)} %get-tuple-element.233), channel_id=1, source_target_pairs={{0,6},{2,4},{4,2},{6,0},{1,7},{3,5},{5,3},{7,1},{8,14},{10,12},{12... | collective-permute-start | bytes 3145736 | tf_op jit(solution)/shard_map/ppermute | solution.py:344
  353.3 37.1 %collective-permute-start.31 = (f32[2,8,256]{2,1,0:T(8,128)}, f32[2,8,256]{2,1,0:T(8,128)}, u32[]{:S(2)}, u32[]{:S(2)}) collective-permute-start(f32[2,8,256]{2,1,0:T(8,128)} %get-tuple-element.164), channel_id=1, source_target_pairs={{2,0},{4,2},{6,4},{3,1},{5,3},{7,5},{10,8},{12,10},{14,12},{11,9},... | collective-permute-start | bytes 49160 | tf_op jit(solution)/shard_map/ppermute | solution.py:350
  414.2 38.2 %collective-permute-start.43 = (f32[2,2,2,160,128]{4,0,2,1,3:T(2,128)}, f32[2,2,2,160,128]{4,0,2,1,3:T(2,128)}, u32[]{:S(2)}, u32[]{:S(2)}) collective-permute-start(f32[2,2,2,160,128]{4,0,2,1,3:T(2,128)} %bitcast.64), channel_id=1, source_target_pairs={{0,2},{2,0},{4,6},{6,4},{1,3},{3,1},{5,7},{7,5},{8,10},{10,8},{12,... | collective-permute-start | bytes 1966088 | tf_op jit(solution)/shard_map/ppermute | solution.py:344
  422.6 58.1 %collective-permute-start.50 = (f32[2,2,1024,128]{3,2,1,0:T(8,128)}, f32[2,2,1024,128]{3,2,1,0:T(8,128)}, u32[]{:S(2)}, u32[]{:S(2)}) collective-permute-start(f32[2,2,1024,128]{3,2,1,0:T(8,128)} %dynamic-slice_bitcast_fusion), channel_id=1, source_target_pairs={{0,4},{2,6},{4,0},{6,2},{1,5},{3,7},{5,1},{7,3},{8,12},{10,14},{12... | collective-permute-start | bytes 6291464 | tf_op jit(solution)/shard_map/ppermute | solution.py:344
  426.4 58.3 %collective-permute-start.48 = (f32[2,2,1024,128]{3,2,1,0:T(8,128)}, f32[2,2,1024,128]{3,2,1,0:T(8,128)}, u32[]{:S(2)}, u32[]{:S(2)}) collective-permute-start(f32[2,2,1024,128]{3,2,1,0:T(8,128)} %dynamic-slice_bitcast_fusion.1), channel_id=1, source_target_pairs={{0,2},{2,0},{4,6},{6,4},{1,3},{3,1},{5,7},{7,5},{8,10},{10,8},{12,... | collective-permute-start | bytes 6291464 | tf_op jit(solution)/shard_map/ppermute | solution.py:344
  452.4 64.8 %collective-permute-start.32 = (f32[512,2048]{1,0:T(8,128)}, f32[512,2048]{1,0:T(8,128)}, u32[]{:S(2)}, u32[]{:S(2)}) collective-permute-start(f32[512,2048]{1,0:T(8,128)} %bitcast_add_fusion), channel_id=1, source_target_pairs={{0,1},{1,0},{2,3},{3,2},{4,5},{5,4},{6,7},{7,6},{8,9},{9,8},{10,11... | collective-permute-start | bytes 12582920 | tf_op jit(solution)/shard_map/ppermute | solution.py:344
  455.5 21.1 %collective-permute-start.44 = (f32[2,2,160,128]{3,1,0,2:T(2,128)}, f32[2,2,160,128]{3,1,0,2:T(2,128)}, u32[]{:S(2)}, u32[]{:S(2)}) collective-permute-start(f32[2,2,160,128]{3,1,0,2:T(2,128)} %bitcast.66), channel_id=1, source_target_pairs={{0,4},{2,6},{4,0},{6,2},{1,5},{3,7},{5,1},{7,3},{8,12},{10,14},{12... | collective-permute-start | bytes 983048 | tf_op jit(solution)/shard_map/ppermute | solution.py:344
  456.3 117.1 %collective-permute-start.21 = (f32[512,2048]{1,0:T(8,128)}, f32[512,2048]{1,0:T(8,128)}, u32[]{:S(2)}, u32[]{:S(2)}) collective-permute-start(f32[512,2048]{1,0:T(8,128)} %fusion.73), channel_id=1, source_target_pairs={{0,1},{1,0},{2,3},{3,2},{4,5},{5,4},{6,7},{7,6},{8,9},{9,8},{10,11... | collective-permute-start | bytes 12582920 | tf_op jit(solution)/shard_map/ppermute | solution.py:344
  478.0 13.2 %collective-permute-start.45 = (f32[2,160,128]{2,1,0:T(8,128)S(1)}, f32[2,160,128]{2,1,0:T(8,128)S(1)}, u32[]{:S(2)}, u32[]{:S(2)}) collective-permute-start(f32[2,160,128]{2,1,0:T(8,128)S(1)} %bitcast.287), channel_id=1, source_target_pairs={{0,16},{8,24},{16,0},{24,8},{1,17},{9,25},{17,1},{25,9},{2,18},{10... | collective-permute-start | bytes 491528 | tf_op jit(solution)/shard_map/ppermute | solution.py:344
  484.4 23.3 %collective-permute-start.51 = (f32[2,1024,128]{2,1,0:T(8,128)}, f32[2,1024,128]{2,1,0:T(8,128)}, u32[]{:S(2)}, u32[]{:S(2)}) collective-permute-start(f32[2,1024,128]{2,1,0:T(8,128)} %dynamic-slice_bitcast_fusion.3), channel_id=1, source_target_pairs={{0,2},{2,0},{4,6},{6,4},{1,3},{3,1},{5,7},{7,5},{8,10},{10,8},{12,... | collective-permute-start | bytes 3145736 | tf_op jit(solution)/shard_map/ppermute | solution.py:344
  488.3 23.4 %collective-permute-start.49 = (f32[2,1024,128]{2,1,0:T(8,128)}, f32[2,1024,128]{2,1,0:T(8,128)}, u32[]{:S(2)}, u32[]{:S(2)}) collective-permute-start(f32[2,1024,128]{2,1,0:T(8,128)} %dynamic-slice_bitcast_fusion.4), channel_id=1, source_target_pairs={{0,4},{2,6},{4,0},{6,2},{1,5},{3,7},{5,1},{7,3},{8,12},{10,14},{12... | collective-permute-start | bytes 3145736 | tf_op jit(solution)/shard_map/ppermute | solution.py:344
  498.2 18.2 %collective-permute-start.47 = (f32[128,128]{1,0:T(8,128)S(1)}, f32[128,128]{1,0:T(8,128)S(1)}, u32[]{:S(2)}, u32[]{:S(2)}) collective-permute-start(f32[128,128]{1,0:T(8,128)S(1)} %slice.218), channel_id=1, source_target_pairs={{0,1},{1,0},{2,3},{3,2},{4,5},{5,4},{6,7},{7,6},{8,9},{9,8},{10,11... | collective-permute-start | bytes 196616 | tf_op jit(solution)/shard_map/ppermute | solution.py:344
  515.6 45.8 %collective-permute-start.52 = (f32[2,1024,128]{2,1,0:T(8,128)}, f32[2,1024,128]{2,1,0:T(8,128)}, u32[]{:S(2)}, u32[]{:S(2)}) collective-permute-start(f32[2,1024,128]{2,1,0:T(8,128)} %dynamic-slice_bitcast_fusion.2), channel_id=1, source_target_pairs={{0,16},{8,24},{16,0},{24,8},{1,17},{9,25},{17,1},{25,9},{2,18},{10... | collective-permute-start | bytes 3145736 | tf_op jit(solution)/shard_map/ppermute | solution.py:344
  525.6 37.5 %collective-permute-start.33 = (f32[15712]{0:T(1024)S(1)}, f32[15712]{0:T(1024)S(1)}, u32[]{:S(2)}, u32[]{:S(2)}) collective-permute-start(f32[15712]{0:T(1024)S(1)} %concatenate.48), channel_id=1, source_target_pairs={{0,2},{2,0},{4,6},{6,4},{1,3},{3,1},{5,7},{7,5},{8,10},{10,8},{12,... | collective-permute-start | bytes 188552 | tf_op jit(solution)/shard_map/ppermute | solution.py:344
  568.4 23.9 %collective-permute-start.53 = (f32[1024,128]{1,0:T(8,128)}, f32[1024,128]{1,0:T(8,128)}, u32[]{:S(2)}, u32[]{:S(2)}) collective-permute-start(f32[1024,128]{1,0:T(8,128)} %dynamic-slice_bitcast_fusion.5), channel_id=1, source_target_pairs={{0,8},{8,0},{16,24},{24,16},{1,9},{9,1},{17,25},{25,17},{2,10},{10... | collective-permute-start | bytes 1572872 | tf_op jit(solution)/shard_map/ppermute | solution.py:344
  585.5 13.3 %collective-permute-start.38 = (f32[512,128]{1,0:T(8,128)S(1)}, f32[512,128]{1,0:T(8,128)S(1)}, u32[]{:S(2)}, u32[]{:S(2)}) collective-permute-start(f32[512,128]{1,0:T(8,128)S(1)} %get-tuple-element.272), channel_id=1, source_target_pairs={{0,4},{2,6},{4,0},{6,2},{1,5},{3,7},{5,1},{7,3},{8,12},{10,14},{12... | collective-permute-start | bytes 786440 | tf_op jit(solution)/shard_map/ppermute | solution.py:344
  586.7 17.0 %collective-permute-start.39 = (f32[512,128]{1,0:T(8,128)}, f32[512,128]{1,0:T(8,128)}, u32[]{:S(2)}, u32[]{:S(2)}) collective-permute-start(f32[512,128]{1,0:T(8,128)} %get-tuple-element.271), channel_id=1, source_target_pairs={{0,6},{2,4},{4,2},{6,0},{1,7},{3,5},{5,3},{7,1},{8,14},{10,12},{12... | collective-permute-start | bytes 786440 | tf_op jit(solution)/shard_map/ppermute | solution.py:344
  589.0 14.7 %collective-permute-start.37 = (f32[512,128]{1,0:T(8,128)}, f32[512,128]{1,0:T(8,128)}, u32[]{:S(2)}, u32[]{:S(2)}) collective-permute-start(f32[512,128]{1,0:T(8,128)} %get-tuple-element.273), channel_id=1, source_target_pairs={{0,2},{2,0},{4,6},{6,4},{1,3},{3,1},{5,7},{7,5},{8,10},{10,8},{12,... | collective-permute-start | bytes 786440 | tf_op jit(solution)/shard_map/ppermute | solution.py:344
  590.8 16.4 %collective-permute-start.40 = (f32[512,128]{1,0:T(8,128)S(1)}, f32[512,128]{1,0:T(8,128)S(1)}, u32[]{:S(2)}, u32[]{:S(2)}) collective-permute-start(f32[512,128]{1,0:T(8,128)S(1)} %get-tuple-element.276), channel_id=1, source_target_pairs={{0,2},{2,0},{4,6},{6,4},{1,3},{3,1},{5,7},{7,5},{8,10},{10,8},{12,... | collective-permute-start | bytes 786440 | tf_op jit(solution)/shard_map/ppermute | solution.py:344
  592.2 15.0 %collective-permute-start.41 = (f32[512,128]{1,0:T(8,128)S(1)}, f32[512,128]{1,0:T(8,128)S(1)}, u32[]{:S(2)}, u32[]{:S(2)}) collective-permute-start(f32[512,128]{1,0:T(8,128)S(1)} %get-tuple-element.275), channel_id=1, source_target_pairs={{0,4},{2,6},{4,0},{6,2},{1,5},{3,7},{5,1},{7,3},{8,12},{10,14},{12... | collective-permute-start | bytes 786440 | tf_op jit(solution)/shard_map/ppermute | solution.py:344
  598.8 11.1 %collective-permute-start.42 = (f32[512,128]{1,0:T(8,128)S(1)}, f32[512,128]{1,0:T(8,128)S(1)}, u32[]{:S(2)}, u32[]{:S(2)}) collective-permute-start(f32[512,128]{1,0:T(8,128)S(1)} %get-tuple-element.274), channel_id=1, source_target_pairs={{0,6},{2,4},{4,2},{6,0},{1,7},{3,5},{5,3},{7,1},{8,14},{10,12},{12... | collective-permute-start | bytes 786440 | tf_op jit(solution)/shard_map/ppermute | solution.py:344
  (84 other events, 818.1 us)
Sparse Core Ops, SparseCore 0:
  318.7 75.9 reduce-scatter.2
  406.9 79.1 reduce-scatter.4

commit v3 on v2

v3 whole, which is shorter than its diff:
```python
import functools

import jax
import jax.numpy as jnp
from jax import lax
from jax.experimental import pallas as pl
from jax.experimental.pallas import tpu as pltpu
from jax.sharding import PartitionSpec as P

CONV = 4
EDGE = 8
LANES = 512
EPSILON = 1e-05
HIGHEST = lax.Precision.HIGHEST
F32 = jnp.float32
BF16 = jnp.bfloat16
VMEM_LIMIT = 48 * 1024 * 1024
COST = 0.25


def mm(a, b, dims=((1,), (0,)), precision=None):
    return lax.dot_general(a, b, (dims, ((), ())), precision=precision, preferred_element_type=F32)


def split(value, count):
    parts, rest = [], value
    for _ in range(count):
        part = rest.astype(BF16).astype(F32)
        parts.append(part)
        rest = rest - part
    return jnp.concatenate(parts, axis=0)


def of_head(rows, columns, heads):
    head = lax.broadcasted_iota(jnp.int32, (rows, columns), 0) % heads
    lane = lax.broadcasted_iota(jnp.int32, (rows, columns), 1) // (columns // heads)
    return (head == lane).astype(F32).astype(BF16)


def widen(rows, lanes):
    heads = rows.shape[0]
    return mm(split(rows, 2).astype(BF16), of_head(2 * heads, lanes, heads), ((0,), (0,)))


def head_sums(value, heads, parts=2):
    pick = of_head(heads, value.shape[1], heads)
    high = value.astype(BF16)
    total = mm(pick, high, ((1,), (1,)))
    if parts == 2:
        total = total + mm(pick, (value - high.astype(F32)).astype(BF16), ((1,), (1,)))
    return total


def row_sums(value):
    ones = jnp.ones((8, value.shape[1]), BF16)
    high = value.astype(BF16)
    return mm(ones, high, ((1,), (1,))) + mm(ones, (value - high.astype(F32)).astype(BF16), ((1,), (1,)))


def exact(rows, matrix, dims=((1,), (0,))):
    heads = rows.shape[0]
    result = mm(split(rows, 3).astype(BF16), matrix, dims)
    return result[:heads] + result[heads : 2 * heads] + result[2 * heads :]


def spreads(cumul):
    heads, slots = cumul.shape
    parts = split(cumul, 3)
    row = lax.broadcasted_iota(jnp.int32, parts.shape, 0) % heads

    def spread(head, start, size, end):
        mask = (row == head).astype(F32)
        left = jnp.concatenate([parts, mask], axis=0).astype(BF16)
        right = jnp.concatenate([mask, -parts], axis=0).astype(BF16)
        return mm(left[:, start : start + size], right[:, :end], ((0,), (0,)))

    return spread


def triangle(slots, dtype=F32):
    row = lax.broadcasted_iota(jnp.int32, (slots, slots), 0)
    column = lax.broadcasted_iota(jnp.int32, (slots, slots), 1)
    return (row >= column).astype(F32).astype(dtype)


def softplus(value):
    return jnp.maximum(value, 0.0) + jnp.log1p(jnp.exp(-jnp.abs(value)))


def slope(value, sig):
    return sig * (1.0 + value * (1.0 - sig))


def convolved(extended, taps, slots):
    total = taps[CONV : CONV + 1] + extended[EDGE : EDGE + slots] * taps[CONV - 1 : CONV]
    for tap in range(CONV - 1):
        start = EDGE - (CONV - 1) + tap
        total = total + extended[start : start + slots] * taps[tap : tap + 1]
    return total


def convolved_back(grad, pre, before, taps):
    slots, lanes = grad.shape
    padded = jnp.concatenate([grad, jnp.zeros((EDGE, lanes), F32)], axis=0)
    row = lax.broadcasted_iota(jnp.int32, (EDGE, lanes), 0)
    back = grad * taps[CONV - 1 : CONV]
    rows = []
    for tap in range(CONV - 1):
        ahead = CONV - 1 - tap
        moved = padded[ahead : ahead + slots]
        back = back + moved * taps[tap : tap + 1]
        first = jnp.where(row >= EDGE - ahead, pltpu.roll(grad[:EDGE], EDGE - ahead, 0), 0.0)
        total = jnp.sum(moved * pre, axis=0, keepdims=True)
        rows.append(total + jnp.sum(first * before, axis=0, keepdims=True))
    rows.append(jnp.sum(grad * pre, axis=0, keepdims=True))
    rows.append(jnp.sum(grad, axis=0, keepdims=True))
    rows.append(jnp.zeros((8 - len(rows), lanes), F32))
    return back, jnp.concatenate(rows, axis=0)


def pair_part_of(value, side, width):
    lane = lax.broadcasted_iota(jnp.int32, value.shape, 1) // width
    return jnp.where(lane == side, value, jnp.zeros_like(value))


def call(kernel, inputs, in_specs, out_specs, out_shape, grid, name, micros, scratch=(), index=None):
    scalars = () if index is None else (index.reshape(1),)
    return pl.pallas_call(
        kernel,
        grid_spec=pltpu.PrefetchScalarGridSpec(
            num_scalar_prefetch=len(scalars),
            grid=grid,
            in_specs=list(in_specs),
            out_specs=out_specs,
            scratch_shapes=list(scratch),
        ),
        out_shape=out_shape,
        compiler_params=pltpu.CompilerParams(vmem_limit_bytes=VMEM_LIMIT),
        cost_estimate=pl.CostEstimate(
            flops=int(micros * COST * 1.1e9), bytes_accessed=int(micros * COST * 2e6), transcendentals=0
        ),
        name=name,
    )(*scalars, *inputs)


def state_kernel(
    heads, pre_x, edge_x, taps_x, pre_bc, edge_bc, taps_bc, dtraw, params,
    local_state, total_decay, u_out, b_out, c_out, steps_out, b_turned,
):
    slots, lanes = pre_x.shape[1:]
    state = b_out.shape[2]

    @pl.when(pl.program_id(1) == 0)
    def _():
        ext = jnp.concatenate([edge_bc[0], pre_bc[0]], axis=0)
        u = convolved(ext, taps_bc[...], slots)
        act = u * jax.nn.sigmoid(u)
        b_out[0] = act[:, :state]
        c_out[0] = act[:, state:]
        b_turned[...] = act[:, :state].T.astype(BF16)

    ext = jnp.concatenate([edge_x[0], pre_x[0]], axis=0)
    u = convolved(ext, taps_x[...], slots)
    u_out[0] = u
    x = u * jax.nn.sigmoid(u)
    par = params[0]
    step = softplus(dtraw[0, 0] + par[:, 0:1])
    rate = step * -jnp.exp(par[:, 1:2])
    cumul = exact(rate, triangle(slots, BF16), ((1,), (1,)))
    steps_out[0, 0] = jnp.concatenate([step, cumul], axis=0)
    last = cumul[:, slots - 1 : slots]
    total_decay[0] = widen(jnp.broadcast_to(jnp.exp(last), (heads, 8)), lanes)
    xd = (widen(step, lanes) * x).astype(BF16)
    tail = (widen(jnp.exp(last - cumul), lanes) * xd.astype(F32)).astype(BF16)
    local_state[0] = mm(b_turned[...], tail)


def inside_kernel(heads, width, u, steps, params, b_act, c_act, local_out, scores):
    slots, lanes = u.shape[1:]

    @pl.when(pl.program_id(1) == 0)
    def _():
        scores[...] = mm(c_act[0], b_act[0], ((1,), (1,)), HIGHEST) * triangle(slots)

    uv = u[0]
    x = uv * jax.nn.sigmoid(uv)
    step, cumul = steps[0, 0][:heads], steps[0, 0][heads:]
    spread = spreads(cumul)
    xd = (widen(step, lanes) * x).astype(BF16)
    skip = widen(jnp.broadcast_to(params[0][:, 2:3], (heads, 8)), lanes)[0:1] * x
    half = slots // 2
    for pair in range(heads // 2):
        at = slice(pair * 2 * width, (pair + 1) * 2 * width)
        top, low = skip[:half, at], skip[half:, at]
        for side in range(2):
            head = 2 * pair + side
            mine = pair_part_of(xd[:, at], side, width)
            decay = jnp.exp(jnp.minimum(spread(head, 0, half, half), 0.0))
            top = top + mm((scores[:half, :half] * decay).astype(BF16), mine[:half])
            decay = jnp.exp(jnp.minimum(spread(head, half, half, slots), 0.0))
            low = low + mm((scores[half:] * decay).astype(BF16), mine)
        local_out[0, :half, at] = top
        local_out[0, half:, at] = low


def gate_kernel(heads, local_out, entering, c_act, steps, z, grad_out, gain, y_out, sums):
    lanes = z.shape[-1]
    growth = widen(jnp.exp(steps[0, 0][heads:]), lanes)
    y = local_out[0] + growth * mm(c_act[0].astype(BF16), entering[0].astype(BF16))
    y_out[0] = y
    zv = z[0]
    g = y * (zv * jax.nn.sigmoid(zv))
    squares = row_sums(g * g)
    dots = row_sums(grad_out[0] * gain[...] * g)
    row = lax.broadcasted_iota(jnp.int32, squares.shape, 0)
    both = jnp.where(row == 0, squares, jnp.where(row == 1, dots, 0.0))

    @pl.when(pl.program_id(1) == 0)
    def _():
        sums[0] = both

    @pl.when(pl.program_id(1) > 0)
    def _():
        sums[0] += both


def gate_back_kernel(
    heads, inner_all, y, z, grad_out, gain, sums, c_act, steps,
    gated_out, grad_y, grad_z, gain_grad, leaving, c_turned,
):
    lanes = z.shape[-1]

    @pl.when(pl.program_id(1) == 0)
    def _():
        c_turned[...] = c_act[0].T.astype(BF16)

    inv_row = lax.rsqrt(sums[0][0:1] / inner_all + EPSILON)
    mean_row = inv_row * sums[0][1:2] / inner_all
    rows = jnp.concatenate([split(inv_row, 2), split(mean_row, 2), jnp.zeros_like(sums[0][:4])], axis=0)
    row = lax.broadcasted_iota(jnp.int32, (8, lanes), 0)
    rows = rows.astype(BF16)
    inv = mm(rows, (row < 2).astype(F32).astype(BF16), ((0,), (0,)))
    mean = mm(rows, ((row >= 2) & (row < 4)).astype(F32).astype(BF16), ((0,), (0,)))
    zv, yv = z[0], y[0]
    sig = jax.nn.sigmoid(zv)
    silu = zv * sig
    normed = yv * silu * inv
    gated_out[0] = (normed * gain[...]).astype(BF16)
    gain_grad[0] = jnp.sum(grad_out[0] * normed, axis=0, keepdims=True)
    dg = inv * (grad_out[0] * gain[...] - normed * mean)
    dy = dg * silu
    grad_y[0] = dy
    grad_z[0] = (dg * yv * slope(zv, sig)).astype(BF16)
    growth = widen(jnp.exp(steps[0, 0][heads:]), lanes)
    leaving[0] = mm(c_turned[...], (growth * dy).astype(BF16))


def inside_back_kernel(
    heads, width, u, steps, b_act, c_act, grad_y, entering,
    grad_xd_out, grad_bc, grad_scores, scores,
):
    slots, lanes = u.shape[1:]

    @pl.when(pl.program_id(1) == 0)
    def _():
        scores[...] = mm(c_act[0], b_act[0], ((1,), (1,)), HIGHEST) * triangle(slots)
        grad_scores[...] = jnp.zeros_like(grad_scores)
        grad_bc[...] = jnp.zeros_like(grad_bc)

    uv = u[0]
    step, cumul = steps[0, 0][:heads], steps[0, 0][heads:]
    spread = spreads(cumul)
    xd = (widen(step, lanes) * (uv * jax.nn.sigmoid(uv))).astype(BF16)
    dy = grad_y[0]
    dy_b = dy.astype(BF16)
    half = slots // 2
    sum_top = jnp.zeros((half, half), F32)
    sum_low = jnp.zeros((half, slots), F32)
    for pair in range(heads // 2):
        at = slice(pair * 2 * width, (pair + 1) * 2 * width)
        xd_pair = xd[:, at]
        top, whole = None, None
        for side in range(2):
            head = 2 * pair + side
            mine = pair_part_of(dy_b[:, at], side, width)
            decay = jnp.exp(jnp.minimum(spread(head, 0, half, half), 0.0))
            weights = (scores[:half, :half] * decay).astype(BF16)
            part = mm(weights, mine[:half], ((0,), (0,)))
            top = part if top is None else top + part
            sum_top = sum_top + mm(mine[:half], xd_pair[:half], ((1,), (1,))) * decay
            decay = jnp.exp(jnp.minimum(spread(head, half, half, slots), 0.0))
            weights = (scores[half:] * decay).astype(BF16)
            part = mm(weights, mine[half:], ((0,), (0,)))
            whole = part if whole is None else whole + part
            sum_low = sum_low + mm(mine[half:], xd_pair, ((1,), (1,))) * decay
        grad_xd_out[0, :half, at] = whole[:half] + top
        grad_xd_out[0, half:, at] = whole[half:]
    grad_scores[:half, :half] += sum_top
    grad_scores[half:] += sum_low
    growth = widen(jnp.exp(cumul), lanes)
    grad_c = mm((growth * dy).astype(BF16), entering[0].astype(BF16), ((1,), (1,)))
    grad_bc[0] += jnp.concatenate([jnp.zeros_like(grad_c), grad_c], axis=1)

    @pl.when(pl.program_id(1) == pl.num_programs(1) - 1)
    def _():
        causal = grad_scores[...] * triangle(slots)
        from_c = mm(causal, c_act[0], ((0,), (0,)), HIGHEST)
        grad_bc[0] += jnp.concatenate([from_c, mm(causal, b_act[0], precision=HIGHEST)], axis=1)


def scan_back_kernel(
    heads, u, pre_x, edge_x, taps_x, dtraw, params, steps, b_act, y, grad_y, inside, entering, coming,
    grad_pre, tail_rows, head_rows, taps_grad, grad_dt, params_grad, grad_b,
):
    slots, lanes = u.shape[1:]

    @pl.when(pl.program_id(1) == 0)
    def _():
        grad_b[...] = jnp.zeros_like(grad_b)

    uv = u[0]
    sig = jax.nn.sigmoid(uv)
    x = uv * sig
    par = params[0]
    decay_a = -jnp.exp(par[:, 1:2])
    step, cumul = steps[0, 0][:heads], steps[0, 0][heads:]
    last = cumul[:, slots - 1 : slots]
    step_wide = widen(step, lanes)
    tail_wide = widen(jnp.exp(last - cumul), lanes)
    lines = widen(jnp.concatenate([jnp.exp(last)] * 4 + [par[:, 2:3]] * 4, axis=1), lanes)
    skip = lines[4:5]
    xd = (step_wide * x).astype(BF16)
    xd_f = xd.astype(F32)
    dy = grad_y[0]
    coming_b = coming[0].astype(BF16)
    from_next = tail_wide * mm(b_act[0].astype(BF16), coming_b)
    grad_xd = inside[0] + from_next
    grad_b[0] += mm((tail_wide * xd_f).astype(BF16), coming_b, ((1,), (1,)))

    direct = head_sums(x * grad_xd, heads, 1)
    ys = y[0] - skip * x
    moved = head_sums(dy.astype(BF16).astype(F32) * ys - xd_f * grad_xd, heads)
    ends = lines[0:1] * jnp.sum(coming[0] * entering[0], axis=0, keepdims=True)
    ends = ends + jnp.sum(xd_f * from_next, axis=0, keepdims=True)
    skips = jnp.sum(dy * x, axis=0, keepdims=True)
    columns = head_sums(jnp.concatenate([ends, skips, jnp.zeros((6, lanes), F32)], axis=0), heads)
    later = exact(moved, triangle(slots, BF16)) + columns[:, 0:1]
    grad_step = (direct + decay_a * later) * jax.nn.sigmoid(dtraw[0, 0] + par[:, 0:1])
    grad_dt[0, 0] = grad_step
    params_grad[0, 0] = jnp.concatenate(
        [
            jnp.sum(grad_step, axis=1, keepdims=True),
            jnp.sum(step * later, axis=1, keepdims=True) * decay_a,
            columns[:, 1:2],
        ],
        axis=1,
    )
    du = (step_wide * grad_xd + skip * dy) * slope(uv, sig)
    back, rows8 = convolved_back(du, pre_x[0], edge_x[0], taps_x[...])
    grad_pre[0] = back.astype(BF16)
    tail_rows[0] = back[slots - EDGE :]
    head_rows[0] = du[:EDGE]
    taps_grad[0] = rows8


def conv_back_kernel(pre, edge, taps, grad_act, grad_pre, tail_rows, head_rows, taps_grad):
    slots = pre.shape[1]
    ext = jnp.concatenate([edge[0], pre[0]], axis=0)
    u = convolved(ext, taps[...], slots)
    du = grad_act[0] * slope(u, jax.nn.sigmoid(u))
    back, rows8 = convolved_back(du, pre[0], edge[0], taps[...])
    grad_pre[0] = back.astype(BF16)
    tail_rows[0] = back[slots - EDGE :]
    head_rows[0] = du[:EDGE]
    taps_grad[0] = rows8


def assemble_kernel(mine, theirs, side, result):
    first = side[0] == 0
    half = mine.shape[2]
    result[0, :, :half] = jnp.where(first, mine[0], theirs[0]).astype(BF16)
    result[0, :, half:] = jnp.where(first, theirs[0], mine[0]).astype(BF16)


def weight_kernel(parts, own_rows, far_rows, *refs):
    result, columns = refs[-2:]
    slots = own_rows.shape[0]

    @pl.when(pl.program_id(0) == 0)
    def _():
        for index in range(parts):
            columns[:, pl.ds(index * slots, slots)] = refs[index][...].T.astype(BF16)

    total = mm(columns[:, :slots], own_rows[...])
    for index in range(1, parts):
        total = total + mm(columns[:, index * slots : (index + 1) * slots], far_rows[index - 1])
    for tile in range(result.shape[0] * result.shape[1]):
        piece = total[:, tile * 128 : (tile + 1) * 128]
        if result.shape[0] == 1:
            result[0, tile] = piece
        else:
            result[tile, 0] = piece


def pair_kernel(place, rows, far_rows, own, far, keep_a, send_a, keep_b, send_b, columns):
    slots = rows.shape[0]
    step = pl.program_id(0)

    @pl.when(step == 0)
    def _():
        columns[:, :slots] = own[...].T.astype(BF16)
        columns[:, slots:] = far[...].T.astype(BF16)

    total = mm(columns[:, :slots], rows[...]) + mm(columns[:, slots:], far_rows[...])
    for tile in range(4):
        piece = total[:, tile * 128 : (tile + 1) * 128]
        away = place[0] ^ tile
        for first, keep, send, bit in ((True, keep_a, send_a, away % 2), (False, keep_b, send_b, away // 2)):
            at = away // 2 if first else away % 2
            mine = step < 2 if first else step >= 2

            @pl.when(mine & (bit == 0))
            def _():
                keep[at, 0] = piece

            @pl.when(mine & (bit == 1))
            def _():
                send[at, 0] = piece


def mend_kernel(place, value, tail, later, taps, mended, *pieces):
    seqs, slots, _ = value.shape
    row = lax.broadcasted_iota(jnp.int32, (EDGE, value.shape[2]), 0)
    for seq in range(seqs):
        end = tail[seq]
        for tap in range(CONV - 1):
            ahead = CONV - 1 - tap
            moved = pltpu.roll(later[seq], EDGE - ahead, 0)
            end = end + jnp.where(row >= EDGE - ahead, moved, 0.0) * taps[tap : tap + 1]
        mended[seq] = jnp.concatenate([value[seq, : slots - 16], value[seq, slots - 16 :]], axis=0)
        last = jnp.concatenate([value[seq, slots - 16 :][: 16 - EDGE].astype(F32), end], axis=0).astype(BF16)
        mended[seq, slots - 16 :] = last
    for index, piece in enumerate(pieces):

        @pl.when(pl.program_id(0) == index)
        def _():
            for seq in range(seqs):
                piece[seq * slots : (seq + 1) * slots] = mended[seq].astype(F32)


def finish_kernel(place, *refs):
    result = refs[-1]
    for index in range(4):

        @pl.when(pl.program_id(0) == index)
        def _():
            result[:, 0] = refs[index][...].T
            result[:, 1] = refs[4 + index][...].T


def swapped(value, axis, bit):
    count = lax.axis_size(axis)
    return lax.ppermute(value, axis, [(i, i ^ bit) for i in range(count)])


def shifted(value, axis, steps):
    count = lax.axis_size(axis)
    initial, last = (max(0, -steps), min(count, count - steps))
    return lax.ppermute(value, axis, [(source, source + steps) for source in range(initial, last)])


def head_sum(value):
    if lax.axis_size("head") == 2:
        return value + swapped(value, "head", 1)
    return lax.psum(value, "head")


def gathered_pass(decay, part, reverse):
    count = lax.axis_size("seq")
    place = lax.axis_index("seq")
    gathered = lax.all_gather(jnp.concatenate([part, decay], axis=1), "seq")
    rows = part.shape[1]
    state = jnp.zeros_like(part)
    for turn in range(count - 1):
        source = count - 1 - turn if reverse else turn
        ahead = source > place if reverse else source < place
        later = gathered[source, :, rows : rows + 1] * state + gathered[source, :, :rows]
        state = jnp.where(ahead, later, state)
    return state


def chosen(pieces, index):
    low = jnp.where(index % 2 == 0, pieces[0], pieces[1])
    high = jnp.where(index % 2 == 0, pieces[2], pieces[3])
    return jnp.where(index < 2, low, high)


def quarter(value, axis, index):
    size = value.shape[axis] // 4
    return lax.dynamic_slice_in_dim(value, index * size, size, axis)


def tied(*values):
    return lax.optimization_barrier(values)


def passed_on(decay, part, reverse, first, second):
    if lax.axis_size("seq") != 4:
        beside_first = first()
        return gathered_pass(decay, part, reverse), beside_first, second(beside_first)
    place = lax.axis_index("seq")
    rows = part.shape[1]
    both = jnp.concatenate([part, decay], axis=1)
    got = [quarter(both, 2, place)] + [swapped(quarter(both, 2, place ^ d), "seq", d) for d in (1, 2, 3)]
    got, beside_first = tied(got, first())
    order = (3, 2, 1, 0) if reverse else (0, 1, 2, 3)
    state = jnp.zeros_like(got[0][:, :rows])
    enters = [None] * 4
    for source in order:
        enters[source] = state
        if source != order[-1]:
            piece = chosen(got, place ^ source)
            state = piece[:, rows : rows + 1] * state + piece[:, :rows]
    back = [chosen(enters, place)] + [swapped(chosen(enters, place ^ d), "seq", d) for d in (1, 2, 3)]
    back, beside_second = tied(back, second(beside_first))
    entering = jnp.concatenate([chosen(back, place ^ index) for index in range(4)], axis=2)
    return entering, beside_first, beside_second


def halves(value, axis, which):
    size = value.shape[axis] // 2
    return lax.dynamic_slice_in_dim(value, which * size, size, axis)


def core_half(value):
    return halves(value.astype(F32), 1, lax.axis_index("head"))


def rows_of_seq_first(half):
    cut = half.shape[1] // 2
    a, b = half[:, :cut], half[:, cut:]
    return a, b, swapped(a, "seq", 1), swapped(b, "seq", 2)


def rows_of_seq_second(a, b, a1, b2):
    return a1, swapped(jnp.stack([a, a1]), "seq", 2), b2, swapped(jnp.stack([b, b2]), "seq", 1)


def rows_of_seq_third(a1, a23, b2, b13):
    high = jnp.stack([b13[0], b2, b13[1]])
    return jnp.concatenate([jnp.concatenate([a1[None], a23], axis=0), high], axis=2)


def assembled(mine):
    side = lax.axis_index("head").reshape(1)
    theirs = swapped(mine, "head", 1)
    count, slots, half = mine.shape
    block = pl.BlockSpec((1, slots, half), lambda i: (i, 0, 0))
    return call(
        assemble_kernel,
        [mine, theirs, side],
        [block, block, pl.BlockSpec(memory_space=pltpu.SMEM)],
        pl.BlockSpec((1, slots, 2 * half), lambda i: (i, 0, 0)),
        jax.ShapeDtypeStruct((count, slots, 2 * half), BF16),
        (count,),
        "assemble",
        count,
    )


def columns_of(value, axis, dim=1):
    place = lax.axis_index(axis)
    piece = lambda index: quarter(value, dim, index).astype(F32)
    return [piece(place)] + [swapped(piece(place ^ d), axis, d) for d in (1, 2, 3)]


def weight_part(own_rows, far_rows, columns, axis):
    slots, model = own_rows.shape
    size = columns[0].shape[1]
    parts = len(columns)
    whole = lambda a: pl.BlockSpec(a.shape, lambda i: (0,) * a.ndim)
    if axis == "seq":
        out_spec = pl.BlockSpec((1, 4, size, 128), lambda i: (i, 0, 0, 0))
    else:
        out_spec = pl.BlockSpec((4, 1, size, 128), lambda i: (0, i, 0, 0))
    return call(
        functools.partial(weight_kernel, parts),
        [own_rows, far_rows, *columns],
        [
            pl.BlockSpec((slots, model // 4), lambda i: (0, i)),
            pl.BlockSpec((parts - 1, slots, model // 4), lambda i: (0, 0, i)),
            *[whole(c) for c in columns],
        ],
        out_spec,
        jax.ShapeDtypeStruct((4, 4, size, 128), F32),
        (4,),
        "weight_part",
        1,
        scratch=[pltpu.VMEM((size, parts * slots), BF16)],
    )


def over_batch(part):
    return lax.psum_scatter(part, "batch", scatter_dimension=0, tiled=True)[0]


def sent_back(summed, axis):
    place = lax.axis_index(axis)
    take = lambda index: lax.dynamic_index_in_dim(summed, index, 0, False)
    return [take(place)] + [swapped(take(place ^ d), axis, d) for d in (1, 2, 3)]


def finished(z_pieces, x_pieces):
    size, block = z_pieces[0].shape
    whole = pl.BlockSpec((size, block), lambda i, p: (0, 0))
    return call(
        finish_kernel,
        [*z_pieces, *x_pieces],
        [whole] * 8,
        pl.BlockSpec((block, 2, size), lambda i, p: (0, 0, i ^ p[0])),
        jax.ShapeDtypeStruct((block, 2, 4 * size), F32),
        (4,),
        "finish",
        4,
        index=lax.axis_index("seq"),
    )


def mended_pieces(value, tail, later, taps):
    seqs, slots, inner = value.shape
    size = inner // 4
    at = lambda *shape: pl.BlockSpec(shape + (size,), lambda i, p: (0,) * len(shape) + (i ^ p[0],))
    mended, *pieces = call(
        mend_kernel,
        [value, tail, later, taps],
        [at(seqs, slots), at(seqs, EDGE), at(seqs, EDGE), at(CONV + 1)],
        [at(seqs, slots)] + [pl.BlockSpec((seqs * slots, size), lambda i, p: (0, 0))] * 4,
        [jax.ShapeDtypeStruct(value.shape, BF16)] + [jax.ShapeDtypeStruct((seqs * slots, size), F32)] * 4,
        (4,),
        "mend",
        4,
        index=lax.axis_index("seq"),
    )
    return mended, pieces


def pair_part(rows, far_rows, own, far):
    slots, model = rows.shape
    size = own.shape[1]
    whole = lambda v: pl.BlockSpec(v.shape, lambda i, p: (0,) * v.ndim)
    part = pl.BlockSpec((slots, model // 4), lambda i, p: (0, i))
    a_spec = pl.BlockSpec((2, 1, size, 128), lambda i, p: (0, jnp.minimum(i, 1), 0, 0))
    b_spec = pl.BlockSpec((2, 1, size, 128), lambda i, p: (0, jnp.maximum(i - 2, 0), 0, 0))
    return call(
        pair_kernel,
        [rows, far_rows, own, far],
        [part, part, whole(own), whole(far)],
        [a_spec, a_spec, b_spec, b_spec],
        [jax.ShapeDtypeStruct((2, 2, size, 128), F32)] * 4,
        (4,),
        "pair_part",
        1,
        scratch=[pltpu.VMEM((size, 2 * slots), BF16)],
        index=lax.axis_index("seq"),
    )


def small_step(value, axis, bit, index):
    pick = lambda which: lax.dynamic_index_in_dim(value, which, 0, False)
    return pick(index) + swapped(pick(1 - index), axis, bit)


def first_transfers(parts, sum_z):
    keep_a, send_a, keep_b, send_b = parts
    return keep_a + swapped(send_a, "seq", 1), keep_b + swapped(send_b, "seq", 2), sent_back(sum_z, "seq")


def second_transfers(a, b, small):
    small = small.reshape(-1, 2, 2, 2, 2, small.shape[1] // 16).transpose(4, 3, 1, 2, 0, 5)
    a = a[0] + swapped(a[1], "seq", 2)
    b = b[0] + swapped(b[1], "seq", 1)
    return a, b, small_step(small, "seq", 1, lax.axis_index("seq") % 2)


def out_weight(pieces):
    even, odd = pieces[0] + pieces[2], pieces[1] + pieces[3]
    parity = lax.axis_index("batch") % 2
    return jnp.concatenate([jnp.where(parity == 0, even, odd), jnp.where(parity == 0, odd, even)], axis=0)


def added_over(values, axis):
    for bit in (1, 2):
        values = values + swapped(values, axis, bit)
    return values


def per_device(
    hidden,
    norm_gain,
    gate_input_weight,
    w_bc,
    w_dt,
    conv_x,
    conv_bc,
    head_params,
    gate_gain,
    w_out,
    lengths,
    cotangent,
):
    seqs, slots, model = hidden.shape
    rows = seqs * slots
    inner = gate_input_weight.shape[2]
    heads_dev = w_dt.shape[1]
    width = inner // heads_dev
    state = w_bc.shape[1] // 2
    inner_all = inner * lax.axis_size("head")
    heads = LANES // width
    groups = inner // LANES
    side = lax.axis_index("head")
    paired = lax.axis_size("batch") == 4 and lax.axis_size("seq") == 4 and lax.axis_size("head") == 2

    positions = lax.axis_index("seq") * slots + jnp.arange(slots)
    mask = (positions[None, :] < lengths[:, None]).astype(F32).reshape(rows, 1)
    hidden_f = hidden.reshape(rows, model).astype(F32)
    inv_rms = lax.rsqrt(jnp.mean(hidden_f * hidden_f, axis=-1, keepdims=True) + EPSILON)
    normed = (hidden_f * inv_rms * norm_gain).astype(BF16)
    grad_mix = (cotangent.reshape(rows, model).astype(F32) * mask).astype(BF16)
    if paired:
        seq_first = rows_of_seq_first(core_half(normed))
        mix_far = swapped(core_half(grad_mix), "batch", 1)

    proj = mm(normed, jnp.concatenate([w_bc, w_dt], axis=1))
    pre_bc = proj[:, : 2 * state].reshape(seqs, slots, 2 * state)
    projected = jnp.einsum("tg,gjn->tjn", normed, gate_input_weight, preferred_element_type=F32)
    gate_z = projected[:, 0].reshape(seqs, slots, inner)
    pre_x = projected[:, 1].reshape(seqs, slots, inner)
    edges = jnp.concatenate([pre_x[:, slots - EDGE :], pre_bc[:, slots - EDGE :]], axis=2)
    edges = shifted(edges, "seq", 1)
    edge_x, edge_bc = edges[..., :inner], edges[..., inner:]
    dtraw = proj[:, 2 * state :].reshape(seqs, slots, groups, heads).transpose(0, 2, 3, 1)
    params = head_params.reshape(3, groups, heads).transpose(1, 2, 0)
    gain = gate_gain.reshape(1, inner)

    grid = (seqs, groups)
    S = jax.ShapeDtypeStruct
    wide = pl.BlockSpec((1, slots, LANES), lambda b, g: (b, 0, g))
    edge = pl.BlockSpec((1, EDGE, LANES), lambda b, g: (b, 0, g))
    states = pl.BlockSpec((1, state, LANES), lambda b, g: (b, 0, g))
    line = pl.BlockSpec((1, 1, LANES), lambda b, g: (b, 0, g))
    taps = pl.BlockSpec((CONV + 1, LANES), lambda b, g: (0, g))
    gain_spec = pl.BlockSpec((1, LANES), lambda b, g: (0, g))
    per_seq = lambda *shape: pl.BlockSpec((1,) + shape, lambda b, g: (b,) + (0,) * len(shape))
    fixed = lambda *shape: pl.BlockSpec(shape, lambda b, g: (0,) * len(shape))
    by_head = lambda k: pl.BlockSpec((1, 1, k, slots), lambda b, g: (b, g, 0, 0))
    par_spec = pl.BlockSpec((1, heads, 3), lambda b, g: (g, 0, 0))
    wide_s = S((seqs, slots, inner), F32)
    wide_b = S((seqs, slots, inner), BF16)
    state_s = S((seqs, state, inner), F32)
    bc_b = S((seqs, slots, state), F32)
    settings = pltpu.CompilerParams(vmem_limit_bytes=VMEM_LIMIT)

    local_state, total_decay, u, b_act, c_act, steps = call(
        functools.partial(state_kernel, heads),
        [pre_x, edge_x, conv_x, pre_bc, edge_bc, conv_bc, dtraw, params],
        [
            wide, edge, taps, per_seq(slots, 2 * state), per_seq(EDGE, 2 * state),
            fixed(CONV + 1, 2 * state), by_head(heads), par_spec,
        ],
        [states, edge, wide, per_seq(slots, state), per_seq(slots, state), by_head(2 * heads)],
        [
            state_s, S((seqs, EDGE, inner), F32), wide_s, bc_b, bc_b,
            S((seqs, groups, 2 * heads, slots), F32),
        ],
        grid,
        "scan_state",
        17,
        scratch=[pltpu.VMEM((state, slots), BF16)],
    )
    if paired:
        local_state, seq_first, grad_mix, steps = tied(local_state, seq_first, grad_mix, steps)

    def mix_back():
        return mm(grad_mix, w_out, ((1,), (1,))).reshape(seqs, slots, inner)

    def scan_inside(_):
        return call(
            functools.partial(inside_kernel, heads, width),
            [u, steps, params, b_act, c_act],
            [wide, by_head(2 * heads), par_spec, per_seq(slots, state), per_seq(slots, state)],
            wide,
            wide_s,
            grid,
            "scan_inside",
            18,
            scratch=[pltpu.VMEM((slots, slots), F32)],
        )

    entering, grad_out, local_out = passed_on(total_decay, local_state, False, mix_back, scan_inside)
    if paired:
        entering, mix_far, seq_first = tied(entering, mix_far, seq_first)
        seq_second = rows_of_seq_second(*seq_first)

    y, sums = call(
        functools.partial(gate_kernel, heads),
        [local_out, entering, c_act, steps, gate_z, grad_out, gain],
        [wide, states, per_seq(slots, state), by_head(2 * heads), wide, wide, gain_spec],
        [wide, per_seq(8, slots)],
        [wide_s, S((seqs, 8, slots), F32)],
        grid,
        "gate",
        15,
    )
    sums = head_sum(sums)

    gated, grad_y, grad_z, gain_grad, leaving = call(
        functools.partial(gate_back_kernel, heads, inner_all),
        [y, gate_z, grad_out, gain, sums, c_act, steps],
        [wide, wide, wide, gain_spec, per_seq(8, slots), per_seq(slots, state), by_head(2 * heads)],
        [wide, wide, wide, line, states],
        [wide_b, wide_s, wide_b, S((seqs, 1, inner), F32), state_s],
        grid,
        "gate_back",
        17,
        scratch=[pltpu.VMEM((state, slots), BF16)],
    )
    gated = gated.reshape(rows, inner)
    grad_z = grad_z.reshape(rows, inner)

    def scan_inside_back():
        inside, grad_bc = call(
            functools.partial(inside_back_kernel, heads, width),
            [u, steps, b_act, c_act, grad_y, entering],
            [wide, by_head(2 * heads), per_seq(slots, state), per_seq(slots, state), wide, states],
            [wide, per_seq(slots, 2 * state)],
            [wide_s, S((seqs, slots, 2 * state), F32)],
            grid,
            "scan_inside_back",
            26,
            scratch=[pltpu.VMEM((slots, slots), F32), pltpu.VMEM((slots, slots), F32)],
        )
        if not paired:
            return inside, grad_bc
        return inside, grad_bc, seq_second

    def rows_ready(beside):
        if not paired:
            return ()
        return assembled(rows_of_seq_third(*beside[2])), mm(gated, w_out)

    coming, beside, ready = passed_on(total_decay, leaving, True, scan_inside_back, rows_ready)
    inside, grad_bc = beside[:2]
    if paired:
        coming, grad_z_sent, gated_sent, ready = tied(coming, grad_z, gated, ready)
        normed_far, mixed = ready
        z_columns = columns_of(grad_z_sent, "seq")
        parity = lax.axis_index("batch") % 2
        gated_own = halves(gated, 1, parity).astype(F32)
        gated_far = swapped(halves(gated_sent, 1, 1 - parity).astype(F32), "batch", 1)
    else:
        mixed = mm(gated, w_out)
    grad_pre, tail_x, first_x, taps_grad_x, grad_dt, params_grad, grad_b = call(
        functools.partial(scan_back_kernel, heads),
        [u, pre_x, edge_x, conv_x, dtraw, params, steps, b_act, y, grad_y, inside, entering, coming],
        [
            wide, wide, edge, taps, by_head(heads), par_spec, by_head(2 * heads), per_seq(slots, state),
            wide, wide, wide, states, states,
        ],
        [
            wide, edge, edge, edge, by_head(heads),
            pl.BlockSpec((1, 1, heads, 3), lambda b, g: (b, g, 0, 0)), per_seq(slots, state),
        ],
        [
            wide_b, S((seqs, EDGE, inner), F32), S((seqs, EDGE, inner), F32), S((seqs, EDGE, inner), F32),
            S((seqs, groups, heads, slots), F32), S((seqs, groups, heads, 3), F32),
            S((seqs, slots, state), F32),
        ],
        grid,
        "scan_back",
        34,
    )
    if paired:
        later_x = shifted(first_x, "seq", -1)
        grad_pre, z_columns, gated_far = tied(grad_pre, z_columns, gated_far)
        part_z = weight_part(normed, normed_far, z_columns, "seq")
        later_x, part_z, tail_x = tied(later_x, part_z, tail_x)
        sum_z = over_batch(part_z)
        grad_pre, pieces = mended_pieces(grad_pre, tail_x, later_x, conv_x)
        pieces, grad_b = tied(pieces, grad_b)
        x_columns = pieces[:1] + [swapped(pieces[d], "seq", d) for d in (1, 2, 3)]
    grad_bc = grad_bc + jnp.pad(grad_b, ((0, 0), (0, 0), (0, state)))
    grad_bc = head_sum(grad_bc)
    if paired:
        mix_far = assembled(mix_far[None])[0]
        parts_out = pair_part(grad_mix, mix_far, gated_own, gated_far)
        x_columns, parts_out, grad_bc = tied(x_columns, parts_out, grad_bc)
        part_x = weight_part(normed, normed_far, x_columns, "seq")
        sum_x = over_batch(part_x)
        part_x, grad_bc = tied(part_x, grad_bc)

    one = lambda *shape: pl.BlockSpec((1,) + shape, lambda b: (b, 0, 0))
    rows8 = S((seqs, EDGE, 2 * state), F32)
    grad_pre_bc, tail_bc, first_bc, taps_grad_bc = call(
        conv_back_kernel,
        [pre_bc, edge_bc, conv_bc, grad_bc],
        [
            one(slots, 2 * state), one(EDGE, 2 * state),
            pl.BlockSpec((CONV + 1, 2 * state), lambda b: (0, 0)), one(slots, 2 * state),
        ],
        [one(slots, 2 * state), one(EDGE, 2 * state), one(EDGE, 2 * state), one(EDGE, 2 * state)],
        [S((seqs, slots, 2 * state), BF16), rows8, rows8, rows8],
        (seqs,),
        "conv_back",
        3,
    )

    def mended(value, tail, first, weights):
        later = shifted(first, "seq", -1)
        add = jnp.zeros_like(tail)
        for tap in range(CONV - 1):
            ahead = CONV - 1 - tap
            moved = jnp.pad(later[:, :ahead], ((0, 0), (EDGE - ahead, 0), (0, 0)))
            add = add + moved * weights[tap]
        return lax.dynamic_update_slice(value, (tail + add).astype(BF16), (0, slots - EDGE, 0))

    if not paired:
        grad_pre = mended(grad_pre, tail_x, first_x, conv_x)
    grad_pre = grad_pre.reshape(rows, inner)
    grad_pre_bc = mended(grad_pre_bc, tail_bc, first_bc, conv_bc).reshape(rows, 2 * state)
    grad_dtr = grad_dt.transpose(0, 3, 1, 2).reshape(rows, heads_dev).astype(BF16)

    if paired:
        a, b, z_pieces = first_transfers(parts_out, sum_z)
        a, b, z_pieces, grad_pre_bc, grad_dtr, grad_pre = tied(a, b, z_pieces, grad_pre_bc, grad_dtr, grad_pre)
        small = jnp.concatenate([halves(grad_pre_bc, 1, side), grad_dtr], axis=1)
        small = mm(small, normed, ((0,), (0,)))
    grad_zx = jnp.stack([grad_z, grad_pre], axis=1)
    portion = jnp.einsum("tjn,gjn->tg", grad_zx, gate_input_weight, preferred_element_type=F32)
    portion = portion + mm(grad_dtr, w_dt, ((1,), (1,)))
    if paired:
        a, b, small = second_transfers(a, b, small)
        a, b, small, portion, mixed = tied(a, b, small, portion, mixed)
        out_pieces = sent_back(jnp.concatenate([a, b], axis=0), "batch")
        small = small_step(small, "seq", 2, lax.axis_index("seq") // 2)
    mixed = head_sum(mixed)
    mixed_out = (mask * (hidden_f + mixed)).astype(BF16).reshape(seqs, slots, model)
    grad_normed = head_sum(portion) + mm(grad_pre_bc, w_bc, ((1,), (1,)))
    scaled_input = hidden_f * inv_rms
    grad_norm_gain = jnp.sum(grad_normed * scaled_input, axis=0)
    grad_scaled = grad_normed * norm_gain
    input_dot = jnp.mean(grad_scaled * scaled_input, axis=-1, keepdims=True)
    grad_hidden = grad_mix.astype(F32) + inv_rms * (grad_scaled - scaled_input * input_dot)
    grad_hidden = grad_hidden.reshape(seqs, slots, model)

    head_grad = params_grad.sum(axis=0).transpose(2, 0, 1).reshape(3, heads_dev)
    taps_sum = jnp.concatenate([taps_grad_x.sum(axis=0), taps_grad_bc.sum(axis=0)], axis=1)[: CONV + 1]
    pieces = [taps_sum, head_grad, gain_grad.sum(axis=0), grad_norm_gain]
    flat = jnp.concatenate([piece.reshape(-1) for piece in pieces])
    if paired:
        flat = added_over(flat, "seq")
        out_pieces, sum_x, flat, small, grad_hidden, mixed_out = tied(
            out_pieces, sum_x, flat, small, grad_hidden, mixed_out
        )
        batch_place = lax.axis_index("batch")
        x_pieces = sent_back(sum_x, "seq")
        small = small_step(small, "batch", 2, batch_place // 2)
        done_small = small_step(small, "batch", 1, batch_place % 2)
        flat = added_over(flat, "batch")
        grad_weight = finished(z_pieces, x_pieces)
        grad_w_out = out_weight(out_pieces)
        bc_mine = done_small[:state]
        bc_other = swapped(bc_mine, "head", 1)
        grad_w_bc = jnp.concatenate(
            [jnp.where(side == 0, bc_mine, bc_other), jnp.where(side == 0, bc_other, bc_mine)], axis=0
        ).T
        grad_w_dt = done_small[state:].T
    else:
        scatter = functools.partial(lax.psum_scatter, axis_name=("batch", "seq"), tiled=True)
        over_slots = ((0,), (0,))
        grad_weight = scatter(
            jnp.stack([mm(normed, grad_z, over_slots), mm(normed, grad_pre, over_slots)], axis=1),
            scatter_dimension=0,
        )
        grad_w_bc = scatter(mm(normed, grad_pre_bc, over_slots), scatter_dimension=0)
        grad_w_dt = scatter(mm(normed, grad_dtr, over_slots), scatter_dimension=0)
        grad_w_out = scatter(mm(gated, grad_mix, over_slots), scatter_dimension=1)
        flat = lax.psum(flat, ("batch", "seq"))

    parted, start = [], 0
    for piece in pieces:
        parted.append(flat[start : start + piece.size].reshape(piece.shape))
        start += piece.size
    grad_conv, grad_head, grad_gate_gain, grad_norm_gain = parted
    return (
        mixed_out,
        grad_hidden,
        grad_norm_gain,
        grad_weight,
        grad_w_bc,
        grad_w_dt,
        grad_conv[:, :inner],
        grad_conv[:, inner:],
        grad_head,
        grad_gate_gain.reshape(inner),
        grad_w_out,
    )


def solution(mesh):
    placed = (
        P("batch", "seq", None),
        P(),
        P(None, None, "head"),
        P(),
        P(None, "head"),
        P(None, "head"),
        P(),
        P(None, "head"),
        P("head"),
        P("head", None),
        P("batch"),
        P("batch", "seq", None),
    )
    return jax.shard_map(
        per_device,
        mesh=mesh,
        in_specs=placed,
        out_specs=(
            P("batch", "seq", None),
            P("batch", "seq", None),
            P(),
            P(("batch", "seq"), None, "head"),
            P(("batch", "seq"), None),
            P(("batch", "seq"), "head"),
            P(None, "head"),
            P(),
            P(None, "head"),
            P("head"),
            P("head", ("batch", "seq")),
        ),
        check_vma=False,
    )
```

time: 635 us -> 567 us (0.89)
  Pallas kernels: 169 us -> 135 us
  local copies, waits for them, and re-layouts: 80.5 us -> 48 us
  starting transfers between devices: 54.9 us -> 73.9 us
  other arithmetic: 66.7 us -> 52 us
    pallas_call x12 -> x14, Pallas kernels: 169 us -> 135 us  [call(): pl.pallas_call(kernel, grid_spec=pltpu.PrefetchScalarGridSpec(num_scalar_...]
    ppermute x51 -> x52, starting transfers between devices: 46.7 us -> 66.4 us  [swapped(): return lax.ppermute(value, axis, [(i, i ^ bit) for i in range(count)])]
    reduce_scatter x2, waiting for transfers between devices: 0.01 us -> 9.75 us  [over_batch(): return lax.psum_scatter(part, 'batch', scatter_dimension=0, tiled=True)[0]]
    unnamed x165 -> x155, local copies, waits for them, and re-layouts: 26.7 us -> 19.5 us
    ppermute x51 -> x52, waiting for transfers between devices: 137 us -> 130 us  [swapped(): return lax.ppermute(value, axis, [(i, i ^ bit) for i in range(count)])]
    dot_general x7 -> x6, matrix products: 38.8 us -> 34.8 us  [mm(): lax.dot_general(a, b, (dims, ((), ())), precision=precision, preferred_el...]
    add x13 -> x12, other arithmetic: 13 us -> 10.3 us  [the longest x1 2.41 us: first_transfers(): keep_b + swapped(send_b, 'seq', 2)]
  transfers between devices with their start and end apart: 56 -> 57, of which waited for: 21 -> 24; matrix products, arithmetic and copies ran while one was open for 26% -> 22% of each run, Pallas kernels for 25% -> 24%
where the time goes in v3:
time: 567 us; the launch traced here: 559 us
  waiting for transfers between devices  162 us (29%)
  Pallas kernels  135 us (24%)
  starting transfers between devices  73.9 us (13%)
  matrix products  72.2 us (13%)
  other arithmetic  52 us (9%)
  local copies, waits for them, and re-layouts  48 us (8%)
  between operations  15.6 us (3%)
    pallas_call x14, Pallas kernels, call(): pl.pallas_call(kernel, grid_spec=pltpu.PrefetchScalarGridSpec(num_scalar_...  135 us
    ppermute x52, waiting for transfers between devices, swapped(): return lax.ppermute(value, axis, [(i, i ^ bit) for i in range(count)])  130 us
    ppermute x52, starting transfers between devices, swapped(): return lax.ppermute(value, axis, [(i, i ^ bit) for i in range(count)])  66.4 us
    dot_general x6, matrix products, mm(): lax.dot_general(a, b, (dims, ((), ())), precision=precision, preferred_el...  34.8 us
    dot_general x1, matrix products, per_device(): jnp.einsum('tjn,gjn->tg', grad_zx, gate_input_weight, preferred_element_t...  23.5 us
    ppermute x3, waiting for transfers between devices, shifted(): lax.ppermute(value, axis, [(source, source + steps) for source in range(i...  22.3 us
    unnamed x155, local copies, waits for them, and re-layouts  19.5 us
    dot_general x1, matrix products, per_device(): jnp.einsum('tg,gjn->tjn', normed, gate_input_weight, preferred_element_ty...  13.9 us
  transfers between devices with their start and end apart: 57, of which 24 were waited for; matrix products, arithmetic and copies ran while one was open for 22% of the time, Pallas kernels for 24%

profile of v3, /device:TPU:0, one launch (start us, length us, event | category | flops | bytes accessed | tf_op | source)
XLA Modules:
  0.0 559.3 jit_solution(3187654123600480209)
XLA Ops:
  11.3 13.9 %fusion.2 = f32[512,2,2048]{2,0,1:T(8,128)S(1)} fusion(bf16[2048,2,2048]{2,1,0:T(2,128)(2,1)} %param.14, bf16[512,2048]{1,0:T(8,128)(2,1)S(1)} %fusion.12.own_rows), kind=kOutput, calls=%fused_computation.2 | convolution fusion | flops 8589934592 | bytes 27262976 | tf_op jit(solution)/shard_map/tg,gjn->tjn/dot_general | solution.py:735
  25.2 3.9 fusion.41
  34.3 4.8 collective-permute-start
  47.7 11.4 %scan_state.1 = (f32[2,128,2048]{2,1,0:T(8,128)S(1)}, f32[2,8,2048]{2,1,0:T(8,128)S(1)}, f32[2,256,2048]{2,1,0:T(8,128)}, f32[2,256,128]{2,1,0:T(8,128)S(1)}, f3...) custom-call(f32[2,256,2048]{2,1,0:T(8,128)} %bitcast.200, f32[2,8,2048]{2,1,0:T(8,128)S(1)} %slice.187.edge_x, ...), custom_call_target="tpu_custom_call" | custom-call | flops 4674999808 | bytes 8500000 | tf_op jit(solution)/shard_map/scan_state/pallas_call | solution.py:128
  59.2 7.6 %collective-permute-done.1 = f32[512,512]{1,0:T(8,128)} collective-permute-done((f32[512,512]{1,0:T(8,128)}, f32[512,512]{1,0:T(8,128)}, u32[]{:S(2)}, u32[]{:S(2)}) %collective-permute-start.1) | collective-permute-done | bytes 1048608 | tf_op jit(solution)/shard_map/ppermute | solution.py:463
  71.1 9.4 %fusion.46 = f32[512,2048]{1,0:T(8,128)} fusion(bf16[512,2048]{1,0:T(8,128)(2,1)S(1)} %copy-done.40, bf16[2048,2048]{1,0:T(8,128)(2,1)} %param.21), kind=kOutput, calls=%fused_computation.158 | convolution fusion | flops 4294967296 | bytes 14680064 | tf_op jit(solution)/shard_map/dot_general | solution.py:22
  83.2 10.8 %collective-permute-done.5 = f32[2,136,512]{2,1,0:T(8,128)S(1)} collective-permute-done((f32[2,136,512]{2,1,0:T(8,128)S(1)}, f32[2,136,512]{2,1,0:T(8,128)S(1)}, u32[]{:S(2)}, u32[]{:S(2)}) %collective-permute-start.5) | collective-permute-done | bytes 557088 | tf_op jit(solution)/shard_map/ppermute | solution.py:463
  98.3 9.4 %scan_inside.1.local_out = f32[2,256,2048]{2,1,0:T(8,128)S(1)} custom-call(f32[2,256,2048]{2,1,0:T(8,128)} %get-tuple-element.137.u, f32[2,4,16,256]{3,2,1,0:T(8,128)S(1)} %get-tuple-element.140.steps, f32[4,8,3]{2,1,0:T(8,128)S(1)} %bitcast.193, f32[2,256,128]{2,1,0:T(8,128)S(1)} %get-tuple-element.141.b_act, f32[2,256,128]{2,1,0:T(8,128)S(1)} %get-tuple-element.149.c_act), custom_call_target="tpu_custom_call" | custom-call | flops 4950000128 | bytes 9000000 | tf_op jit(solution)/shard_map/scan_inside/pallas_call | solution.py:128
  109.6 8.7 %collective-permute-done.7 = f32[2,128,512]{2,1,0:T(8,128)S(1)} collective-permute-done((f32[2,128,512]{2,1,0:T(8,128)S(1)}, f32[2,128,512]{2,1,0:T(8,128)S(1)}, u32[]{:S(2)}, u32[]{:S(2)}) %collective-permute-start.7) | collective-permute-done | bytes 524320 | tf_op jit(solution)/shard_map/ppermute | solution.py:463
  118.8 3.8 pad_maximum_fusion.1
  124.0 3.0 pad_maximum_fusion.2
  127.6 11.3 %gate.1 = (f32[2,256,2048]{2,1,0:T(8,128)}, f32[2,8,256]{2,1,0:T(8,128)S(1)}) custom-call(f32[2,256,2048]{2,1,0:T(8,128)} %copy-done.28, f32[2,128,2048]{2,1,0:T(8,128)S(1)} %pad_maximum_fusion.entering, f32[2,256,128]{2,1,0:T(8,128)S(1)} %get-tuple-element.149.c_act, f32[2,4,16,256]{3,2,1,0:T(8,128)S(1)} %get-tuple-element.140.steps, ...), custom_call_target="tpu_custom_call" | custom-call | flops 4124999936 | bytes 7500000 | tf_op jit(solution)/shard_map/gate/pallas_call | solution.py:128
  140.1 11.7 %gate_back.1 = (bf16[2,256,2048]{2,1,0:T(8,128)(2,1)S(1)}, f32[2,256,2048]{2,1,0:T(8,128)}, bf16[2,256,2048]{2,1,0:T(8,128)(2,1)S(1)}, f32[2,1,2048]{2,1,0:T(1,128)S(1)}, f32[2,128,2048]{2,1,0:T(8,128)}) custom-call(f32[2,256,2048]{2,1,0:T(8,128)} %get-tuple-element.161.y, f32[2,256,2048]{2,1,0:T(8,128)} %bitcast.204, f32[2,256,2048]{2,1,0:T(8,128)} %bitcast.228, ...), custom_call_target="tpu_custom_call" | custom-call | flops 4674999808 | bytes 8500000 | tf_op jit(solution)/shard_map/gate_back/pallas_call | solution.py:128
  151.8 3.2 constant_dynamic-update-slice_fusion.3
  160.0 20.3 %scan_inside_back.1 = (f32[2,256,2048]{2,1,0:T(8,128)}, f32[2,256,256]{2,1,0:T(8,128)S(1)}) custom-call(f32[2,256,2048]{2,1,0:T(8,128)} %get-tuple-element.137.u, f32[2,4,16,256]{3,2,1,0:T(8,128)S(1)} %get-tuple-element.140.steps, f32[2,256,128]{2,1,0:T(8,128)S(1)} %get-tuple-element.141.b_act, f32[2,256,128]{2,1,0:T(8,128)S(1)} %get-tuple-element.149.c_act, ...), custom_call_target="tpu_custom_call" | custom-call | flops 7150000128 | bytes 13000000 | tf_op jit(solution)/shard_map/scan_inside_back/pallas_call | solution.py:128
  180.3 7.4 %collective-permute-done.11 = f32[2,136,512]{2,1,0:T(8,128)S(1)} collective-permute-done((f32[2,136,512]{2,1,0:T(8,128)}, f32[2,136,512]{2,1,0:T(8,128)S(1)}, u32[]{:S(2)}, u32[]{:S(2)}) %collective-permute-start.11) | collective-permute-done | bytes 557088 | tf_op jit(solution)/shard_map/ppermute | solution.py:463
  187.8 7.8 %collective-permute-done.13 = f32[2,136,512]{2,1,0:T(8,128)S(1)} collective-permute-done((f32[2,136,512]{2,1,0:T(8,128)}, f32[2,136,512]{2,1,0:T(8,128)S(1)}, u32[]{:S(2)}, u32[]{:S(2)}) %collective-permute-start.13) | collective-permute-done | bytes 557088 | tf_op jit(solution)/shard_map/ppermute | solution.py:463
  195.8 4.7 maximum_maximum_fusion.mine
  206.8 9.4 %fusion.47 = f32[512,2048]{1,0:T(8,128)} fusion(bf16[512,2048]{1,0:T(8,128)(2,1)S(1)} %bitcast.183, bf16[2048,2048]{1,0:T(8,128)(2,1)} %param.21), kind=kOutput, calls=%fused_computation.159 | convolution fusion | flops 4294967296 | bytes 14680064 | tf_op jit(solution)/shard_map/dot_general | solution.py:22
  216.2 8.2 %assemble.2.far_rows = bf16[3,512,2048]{2,1,0:T(8,128)(2,1)} custom-call(f32[3,512,1024]{2,1,0:T(8,128)} %maximum_maximum_fusion.mine, f32[3,512,1024]{2,1,0:T(8,128)} %collective-permute-done.19.theirs, s32[1]{0:T(128)} %bitcast.19.side), custom_call_target="tpu_custom_call" | custom-call | flops 825000000 | bytes 1500000 | tf_op jit(solution)/shard_map/assemble/pallas_call | solution.py:128
  224.4 3.7 collective-permute-done.17
  238.9 21.3 %scan_back.1 = (bf16[2,256,2048]{2,1,0:T(8,128)(2,1)S(1)}, f32[2,8,2048]{2,1,0:T(8,128)S(1)}, f32[2,8,2048]{2,1,0:T(8,128)S(1)}, f32[2,8,2048]{2,1,0:T(8,128)S(1...) custom-call(f32[2,256,2048]{2,1,0:T(8,128)} %get-tuple-element.137.u, ...), custom_call_target="tpu_custom_call" | custom-call | flops 9349999616 | bytes 17000000 | tf_op jit(solution)/shard_map/scan_back/pallas_call | solution.py:128
  264.1 16.9 %collective-permute-done.21.refs_2_ = f32[512,512]{1,0:T(8,128)S(1)} collective-permute-done((f32[512,512]{1,0:T(8,128)}, f32[512,512]{1,0:T(8,128)S(1)}, u32[]{:S(2)}, u32[]{:S(2)}) %collective-permute-start.21) | collective-permute-done | bytes 1048608 | tf_op jit(solution)/shard_map/ppermute | solution.py:463
  281.1 2.9 collective-permute-done.22.refs_3_
  284.0 9.1 %weight_part.2 = f32[4,4,512,128]{3,2,1,0:T(8,128)} custom-call(bf16[512,2048]{1,0:T(8,128)(2,1)} %copy-done.36, bf16[3,512,2048]{2,1,0:T(8,128)(2,1)} %assemble.2.far_rows, f32[512,512]{1,0:T(8,128)S(1)} %get-tuple-element.195.refs_0_, f32[512,512]{1,0:T(8,128)S(1)} %collective-permute-done.20.refs_1_, f32[512,512]{1,0:T(8,128)S(1)} %collective-permute-done.21.refs_2_, ...), custom_call_target="tpu_custom_call" | custom-call | flops 275000000 | bytes 500000 | tf_op jit(solution)/shard_map/weight_part/pallas_call | solution.py:128
  296.3 5.7 %mend.1 = (bf16[2,256,2048]{2,1,0:T(8,128)(2,1)}, f32[512,512]{1,0:T(8,128)S(1)}, f32[512,512]{1,0:T(8,128)}, f32[512,512]{1,0:T(8,128)}, f32[512,512]{1,0:T(8,128)}) custom-call(s32[1]{0:T(128)} %bitcast.place, bf16[2,256,2048]{2,1,0:T(8,128)(2,1)} %copy-done.31, f32[2,8,2048]{2,1,0:T(8,128)S(1)} %copy-done.33, f32[2,8,2048]{2,1,0:T(8,128)S(1)} %copy-done.24, ...), custom_call_target="tpu_custom_call" | custom-call | flops 1100000000 | bytes 2000000 | tf_op jit(solution)/shard_map/mend/pallas_call | solution.py:128
  306.4 2.8 dynamic-slice_convert_fusion.2.own
  312.5 11.3 %pair_part.1 = (f32[2,2,1024,128]{3,2,1,0:T(8,128)S(1)}, f32[2,2,1024,128]{3,2,1,0:T(8,128)}, f32[2,2,1024,128]{3,2,1,0:T(8,128)}, f32[2,2,1024,128]{3,2,1,0:T(8,128)}) custom-call(s32[1]{0:T(128)} %bitcast.place, bf16[512,2048]{1,0:T(8,128)(2,1)} %copy-done.39, bf16[512,2048]{1,0:T(8,128)(2,1)} %bitcast.177, f32[512,1024]{1,0:T(8,128)} %dynamic-slice_convert_fusion.2.own, ...), custom_call_target="tpu_custom_call" | custom-call | flops 275000000 | bytes 500000 | tf_op jit(solution)/shard_map/pair_part/pallas_call | solution.py:128
  328.4 22.9 %collective-permute-done.26.refs_2_ = f32[512,512]{1,0:T(8,128)} collective-permute-done((f32[512,512]{1,0:T(8,128)}, f32[512,512]{1,0:T(8,128)}, u32[]{:S(2)}, u32[]{:S(2)}) %collective-permute-start.26) | collective-permute-done | bytes 1048608 | tf_op jit(solution)/shard_map/ppermute | solution.py:463
  353.0 3.9 copy.57
  357.6 10.2 %weight_part.3 = f32[4,4,512,128]{3,2,1,0:T(8,128)} custom-call(bf16[512,2048]{1,0:T(8,128)(2,1)} %copy-done.36, bf16[3,512,2048]{2,1,0:T(8,128)(2,1)} %assemble.2.far_rows, f32[512,512]{1,0:T(8,128)S(1)} %get-tuple-element.224.refs_0_, f32[512,512]{1,0:T(8,128)} %collective-permute-done.25.refs_1_, f32[512,512]{1,0:T(8,128)} %collective-permute-done.26.refs_2_, ...), custom_call_target="tpu_custom_call" | custom-call | flops 275000000 | bytes 500000 | tf_op jit(solution)/shard_map/weight_part/pallas_call | solution.py:128
  375.0 2.6 collective-permute-start.32
  378.1 22.3 %collective-permute-done.35 = f32[2,8,256]{2,1,0:T(8,128)S(1)} collective-permute-done((f32[2,8,256]{2,1,0:T(8,128)S(1)}, f32[2,8,256]{2,1,0:T(8,128)S(1)}, u32[]{:S(2)}, u32[]{:S(2)}) %collective-permute-start.35) | collective-permute-done | bytes 16416 | tf_op jit(solution)/shard_map/ppermute | solution.py:469
  411.2 2.8 collective-permute-start.36
  420.7 23.5 %fusion = f32[512,2048,1]{1,0,2:T(8,128)S(1)} fusion(bf16[2048,2,2048]{2,1,0:T(2,128)(2,1)} %param.14, bf16[512,1,2048]{2,0,1:T(8,128)(2,1)} %bitcast.229, bf16[512,1,2048]{2,0,1:T(8,128)(2,1)S(1)} %bitcast.181), kind=kOutput, calls=%fused_computation | convolution fusion | flops 8592031744 | bytes 25165824 | tf_op jit(solution)/shard_map/tjn,gjn->tg/dot_general | solution.py:938
  444.2 2.7 bitcast_add_fusion
  447.0 2.7 collective-permute-done.38
  460.6 2.7 collective-permute-start.40
  463.3 2.7 collective-permute-done.45
  466.0 3.7 collective-permute-start.41
  470.6 9.6 %fusion.14 = (f32[512]{0:T(512)S(1)}, f32[2048]{0:T(1024)S(1)}, f32[512,2048]{1,0:T(8,128)}, bf16[512,2048]{1,0:T(8,128)(2,1)}) fusion(bf16[2,256,2048]{2,1,0:T(8,128)(2,1)S(1)} %copy-done.38, f32[2048]{0:T(1024)S(1)} %copy-done.62, f32[512]{0:T(512)S(1)} %bitcast.220, f32[512,2048]{1,0:T(8,128)} %bitcast_add_fusion, ...), kind=kOutput, calls=%fused_computation.20 | convolution fusion | flops 550499840 | bytes 26499072 | tf_op jit(solution)/shard_map/dot_general | solution.py:22
  481.2 3.3 collective-permute-done.43
  485.6 6.1 %fusion.17 = f32[512,2048]{1,0:T(8,128)} fusion(bf16[2,256,2048]{2,1,0:T(8,128)(2,1)S(1)} %copy-done.38, bf16[512,2048]{1,0:T(8,128)(2,1)} %copy-done.39, f32[512,2048]{1,0:T(8,128)} %get-tuple-element.298, f32[512]{0:T(512)S(1)} %broadcast_multiply_fusion, f32[2048]{0:T(1024)S(1)} %copy-done.62, f32[512]{0:T(512)S(1)} %bitcast.221), kind=kLoop, calls=%fused_computation.23 | loop fusion | flops 8388608 | bytes 12595200 | tf_op jit(solution)/shard_map/add | solution.py:952
  491.7 9.7 %reduce-scatter.5.cloned.1.call-done = f32[1,4,512,128]{3,2,1,0:T(8,128)} async-done(((f32[4,4,512,128]{3,2,1,0:T(8,128)}), f32[1,4,512,128]{3,2,1,0:T(8,128)}) %reduce-scatter.5.cloned.1.call-update) | async-done | bytes 1048592 | tf_op jit(solution)/shard_map/reduce_scatter | solution.py:604
  502.5 13.5 %collective-permute-done.41 = f32[1024,128]{1,0:T(8,128)} collective-permute-done((f32[1024,128]{1,0:T(8,128)}, f32[1024,128]{1,0:T(8,128)}, u32[]{:S(2)}, u32[]{:S(2)}) %collective-permute-start.41) | collective-permute-done | bytes 524320 | tf_op jit(solution)/shard_map/ppermute | solution.py:463
  516.0 10.4 %collective-permute-start.47 = (f32[15712]{0:T(1024)S(1)}, f32[15712]{0:T(1024)S(1)}, u32[]{:S(2)}, u32[]{:S(2)}) collective-permute-start(f32[15712]{0:T(1024)S(1)} %add.334), channel_id=1, source_target_pairs={{0,8},{8,0},{16,24},{24,16},{1,9},{9,1},{17,25},{25,17},{2,10},{10... | collective-permute-start | bytes 188552 | tf_op jit(solution)/shard_map/ppermute | solution.py:463
  533.8 2.9 collective-permute-start.48
  537.8 6.0 %collective-permute-done.48 = f32[15712]{0:T(1024)S(1)} collective-permute-done((f32[15712]{0:T(1024)S(1)}, f32[15712]{0:T(1024)S(1)}, u32[]{:S(2)}, u32[]{:S(2)}) %collective-permute-start.48) | collective-permute-done | bytes 62880 | tf_op jit(solution)/shard_map/ppermute | solution.py:463
  (353 shorter events, 134.6 us)
Async XLA Ops:
  7.2 365.7 %reduce-scatter.3.cloned.1.call-start = ((), (), s32[]{:S(2)}) async-start(), calls=%async_computation.2 | async-start | bytes 5242880 | tf_op jit(solution)/shard_map/reduce_scatter | solution.py:604
  34.3 13.4 %collective-permute-start = (f32[2,8,2304]{2,1,0:T(8,128)S(1)}, f32[2,8,2304]{2,1,0:T(8,128)S(1)}, u32[]{:S(2)}, u32[]{:S(2)}) collective-permute-start(f32[2,8,2304]{2,1,0:T(8,128)S(1)} %pad_maximum_fusion.5), channel_id=1, source_target_pairs={{0,2},{2,4},{4,6},{1,3},{3,5},{5,7},{8,10},{10,12},{12,14},{9,11},... | collective-permute-start | bytes 442376 | tf_op jit(solution)/shard_map/ppermute | solution.py:469
  41.0 25.8 %collective-permute-start.1 = (f32[512,512]{1,0:T(8,128)}, f32[512,512]{1,0:T(8,128)}, u32[]{:S(2)}, u32[]{:S(2)}) collective-permute-start(f32[512,512]{1,0:T(8,128)} %get-tuple-element.168), channel_id=1, source_target_pairs={{0,2},{2,0},{4,6},{6,4},{1,3},{3,1},{5,7},{7,5},{8,10},{10,8},{12,... | collective-permute-start | bytes 3145736 | tf_op jit(solution)/shard_map/ppermute | solution.py:463
  42.5 24.6 %collective-permute-start.2 = (f32[512,512]{1,0:T(8,128)}, f32[512,512]{1,0:T(8,128)}, u32[]{:S(2)}, u32[]{:S(2)}) collective-permute-start(f32[512,512]{1,0:T(8,128)} %get-tuple-element.170), channel_id=1, source_target_pairs={{0,4},{2,6},{4,0},{6,2},{1,5},{3,7},{5,1},{7,3},{8,12},{10,14},{12... | collective-permute-start | bytes 3145736 | tf_op jit(solution)/shard_map/ppermute | solution.py:463
  45.9 72.9 %collective-permute-start.9 = (f32[512,1024]{1,0:T(8,128)}, f32[512,1024]{1,0:T(8,128)S(1)}, u32[]{:S(2)}, u32[]{:S(2)}) collective-permute-start(f32[512,1024]{1,0:T(8,128)} %dynamic-slice_convert_fusion), channel_id=1, source_target_pairs={{0,8},{8,0},{16,24},{24,16},{1,9},{9,1},{17,25},{25,17},{2,10},{10... | collective-permute-start | bytes 6291464 | tf_op jit(solution)/shard_map/ppermute | solution.py:463
  67.5 15.6 %collective-permute-start.3 = (f32[2,136,512]{2,1,0:T(8,128)S(1)}, f32[2,136,512]{2,1,0:T(8,128)S(1)}, u32[]{:S(2)}, u32[]{:S(2)}) collective-permute-start(f32[2,136,512]{2,1,0:T(8,128)S(1)} %get-tuple-element.315), channel_id=1, source_target_pairs={{0,2},{2,0},{4,6},{6,4},{1,3},{3,1},{5,7},{7,5},{8,10},{10,8},{12,... | collective-permute-start | bytes 1671176 | tf_op jit(solution)/shard_map/ppermute | solution.py:463
  68.1 15.0 %collective-permute-start.4 = (f32[2,136,512]{2,1,0:T(8,128)S(1)}, f32[2,136,512]{2,1,0:T(8,128)S(1)}, u32[]{:S(2)}, u32[]{:S(2)}) collective-permute-start(f32[2,136,512]{2,1,0:T(8,128)S(1)} %get-tuple-element.314), channel_id=1, source_target_pairs={{0,4},{2,6},{4,0},{6,2},{1,5},{3,7},{5,1},{7,3},{8,12},{10,14},{12... | collective-permute-start | bytes 1671176 | tf_op jit(solution)/shard_map/ppermute | solution.py:463
  69.6 24.3 %collective-permute-start.5 = (f32[2,136,512]{2,1,0:T(8,128)S(1)}, f32[2,136,512]{2,1,0:T(8,128)S(1)}, u32[]{:S(2)}, u32[]{:S(2)}) collective-permute-start(f32[2,136,512]{2,1,0:T(8,128)S(1)} %get-tuple-element.313), channel_id=1, source_target_pairs={{0,6},{2,4},{4,2},{6,0},{1,7},{3,5},{5,3},{7,1},{8,14},{10,12},{12... | collective-permute-start | bytes 1671176 | tf_op jit(solution)/shard_map/ppermute | solution.py:463
  94.7 14.9 %collective-permute-start.6 = (f32[2,128,512]{2,1,0:T(8,128)S(1)}, f32[2,128,512]{2,1,0:T(8,128)S(1)}, u32[]{:S(2)}, u32[]{:S(2)}) collective-permute-start(f32[2,128,512]{2,1,0:T(8,128)S(1)} %get-tuple-element.344), channel_id=1, source_target_pairs={{0,2},{2,0},{4,6},{6,4},{1,3},{3,1},{5,7},{7,5},{8,10},{10,8},{12,... | collective-permute-start | bytes 1572872 | tf_op jit(solution)/shard_map/ppermute | solution.py:463
  95.6 22.8 %collective-permute-start.7 = (f32[2,128,512]{2,1,0:T(8,128)S(1)}, f32[2,128,512]{2,1,0:T(8,128)S(1)}, u32[]{:S(2)}, u32[]{:S(2)}) collective-permute-start(f32[2,128,512]{2,1,0:T(8,128)S(1)} %get-tuple-element.343), channel_id=1, source_target_pairs={{0,4},{2,6},{4,0},{6,2},{1,5},{3,7},{5,1},{7,3},{8,12},{10,14},{12... | collective-permute-start | bytes 1572872 | tf_op jit(solution)/shard_map/ppermute | solution.py:463
  97.1 21.2 %collective-permute-start.8 = (f32[2,128,512]{2,1,0:T(8,128)S(1)}, f32[2,128,512]{2,1,0:T(8,128)S(1)}, u32[]{:S(2)}, u32[]{:S(2)}) collective-permute-start(f32[2,128,512]{2,1,0:T(8,128)S(1)} %get-tuple-element.299), channel_id=1, source_target_pairs={{0,6},{2,4},{4,2},{6,0},{1,7},{3,5},{5,3},{7,1},{8,14},{10,12},{12... | collective-permute-start | bytes 1572872 | tf_op jit(solution)/shard_map/ppermute | solution.py:463
  122.6 73.0 %collective-permute-start.14 = (f32[2,512,512]{2,1,0:T(8,128)}, f32[2,512,512]{2,1,0:T(8,128)}, u32[]{:S(2)}, u32[]{:S(2)}) collective-permute-start(f32[2,512,512]{2,1,0:T(8,128)} %pad_maximum_fusion.1), channel_id=1, source_target_pairs={{0,4},{2,6},{4,0},{6,2},{1,5},{3,7},{5,1},{7,3},{8,12},{10,14},{12... | collective-permute-start | bytes 6291464 | tf_op jit(solution)/shard_map/ppermute | solution.py:463
  127.0 68.5 %collective-permute-start.15 = (f32[2,512,512]{2,1,0:T(8,128)}, f32[2,512,512]{2,1,0:T(8,128)S(1)}, u32[]{:S(2)}, u32[]{:S(2)}) collective-permute-start(f32[2,512,512]{2,1,0:T(8,128)} %pad_maximum_fusion.2), channel_id=1, source_target_pairs={{0,2},{2,0},{4,6},{6,4},{1,3},{3,1},{5,7},{7,5},{8,10},{10,8},{12,... | collective-permute-start | bytes 6291464 | tf_op jit(solution)/shard_map/ppermute | solution.py:463
  156.5 31.2 %collective-permute-start.11 = (f32[2,136,512]{2,1,0:T(8,128)}, f32[2,136,512]{2,1,0:T(8,128)S(1)}, u32[]{:S(2)}, u32[]{:S(2)}) collective-permute-start(f32[2,136,512]{2,1,0:T(8,128)} %get-tuple-element.308), channel_id=1, source_target_pairs={{0,2},{2,0},{4,6},{6,4},{1,3},{3,1},{5,7},{7,5},{8,10},{10,8},{12,... | collective-permute-start | bytes 1671176 | tf_op jit(solution)/shard_map/ppermute | solution.py:463
  158.0 29.8 %collective-permute-start.12 = (f32[2,136,512]{2,1,0:T(8,128)}, f32[2,136,512]{2,1,0:T(8,128)S(1)}, u32[]{:S(2)}, u32[]{:S(2)}) collective-permute-start(f32[2,136,512]{2,1,0:T(8,128)} %get-tuple-element.307), channel_id=1, source_target_pairs={{0,4},{2,6},{4,0},{6,2},{1,5},{3,7},{5,1},{7,3},{8,12},{10,14},{12... | collective-permute-start | bytes 1671176 | tf_op jit(solution)/shard_map/ppermute | solution.py:463
  158.6 37.0 %collective-permute-start.13 = (f32[2,136,512]{2,1,0:T(8,128)}, f32[2,136,512]{2,1,0:T(8,128)S(1)}, u32[]{:S(2)}, u32[]{:S(2)}) collective-permute-start(f32[2,136,512]{2,1,0:T(8,128)} %get-tuple-element.306), channel_id=1, source_target_pairs={{0,6},{2,4},{4,2},{6,0},{1,7},{3,5},{5,3},{7,1},{8,14},{10,12},{12... | collective-permute-start | bytes 1671176 | tf_op jit(solution)/shard_map/ppermute | solution.py:463
  200.6 15.6 %collective-permute-start.19 = (f32[3,512,1024]{2,1,0:T(8,128)}, f32[3,512,1024]{2,1,0:T(8,128)}, u32[]{:S(2)}, u32[]{:S(2)}) collective-permute-start(f32[3,512,1024]{2,1,0:T(8,128)} %maximum_maximum_fusion.mine), channel_id=1, source_target_pairs={{0,1},{1,0},{2,3},{3,2},{4,5},{5,4},{6,7},{7,6},{8,9},{9,8},{10,11... | collective-permute-start | bytes 18874376 | tf_op jit(solution)/shard_map/ppermute | solution.py:463
  203.0 21.5 %collective-permute-start.16 = (f32[2,128,512]{2,1,0:T(8,128)S(1)}, f32[2,128,512]{2,1,0:T(8,128)S(1)}, u32[]{:S(2)}, u32[]{:S(2)}) collective-permute-start(f32[2,128,512]{2,1,0:T(8,128)S(1)} %get-tuple-element.342), channel_id=1, source_target_pairs={{0,2},{2,0},{4,6},{6,4},{1,3},{3,1},{5,7},{7,5},{8,10},{10,8},{12,... | collective-permute-start | bytes 1572872 | tf_op jit(solution)/shard_map/ppermute | solution.py:463
  203.5 24.6 %collective-permute-start.17 = (f32[2,128,512]{2,1,0:T(8,128)S(1)}, f32[2,128,512]{2,1,0:T(8,128)S(1)}, u32[]{:S(2)}, u32[]{:S(2)}) collective-permute-start(f32[2,128,512]{2,1,0:T(8,128)S(1)} %fusion.32), channel_id=1, source_target_pairs={{0,4},{2,6},{4,0},{6,2},{1,5},{3,7},{5,1},{7,3},{8,12},{10,14},{12... | collective-permute-start | bytes 1572872 | tf_op jit(solution)/shard_map/ppermute | solution.py:463
  205.3 24.4 %collective-permute-start.18 = (f32[2,128,512]{2,1,0:T(8,128)S(1)}, f32[2,128,512]{2,1,0:T(8,128)S(1)}, u32[]{:S(2)}, u32[]{:S(2)}) collective-permute-start(f32[2,128,512]{2,1,0:T(8,128)S(1)} %get-tuple-element.340), channel_id=1, source_target_pairs={{0,6},{2,4},{4,2},{6,0},{1,7},{3,5},{5,3},{7,1},{8,14},{10,12},{12... | collective-permute-start | bytes 1572872 | tf_op jit(solution)/shard_map/ppermute | solution.py:463
  231.9 52.1 %collective-permute-start.23 = (f32[512,1024]{1,0:T(8,128)S(1)}, f32[512,1024]{1,0:T(8,128)}, u32[]{:S(2)}, u32[]{:S(2)}) collective-permute-start(f32[512,1024]{1,0:T(8,128)S(1)} %dynamic-slice_convert_fusion.3), channel_id=1, source_target_pairs={{0,8},{8,0},{16,24},{24,16},{1,9},{9,1},{17,25},{25,17},{2,10},{10... | collective-permute-start | bytes 6291464 | tf_op jit(solution)/shard_map/ppermute | solution.py:463
  235.4 28.7 %collective-permute-start.20 = (f32[512,512]{1,0:T(8,128)}, f32[512,512]{1,0:T(8,128)S(1)}, u32[]{:S(2)}, u32[]{:S(2)}) collective-permute-start(f32[512,512]{1,0:T(8,128)} %get-tuple-element.326), channel_id=1, source_target_pairs={{0,2},{2,0},{4,6},{6,4},{1,3},{3,1},{5,7},{7,5},{8,10},{10,8},{12,... | collective-permute-start | bytes 3145736 | tf_op jit(solution)/shard_map/ppermute | solution.py:463
  236.3 44.8 %collective-permute-start.21 = (f32[512,512]{1,0:T(8,128)}, f32[512,512]{1,0:T(8,128)S(1)}, u32[]{:S(2)}, u32[]{:S(2)}) collective-permute-start(f32[512,512]{1,0:T(8,128)} %get-tuple-element.325), channel_id=1, source_target_pairs={{0,4},{2,6},{4,0},{6,2},{1,5},{3,7},{5,1},{7,3},{8,12},{10,14},{12... | collective-permute-start | bytes 3145736 | tf_op jit(solution)/shard_map/ppermute | solution.py:463
  238.0 46.0 %collective-permute-start.22 = (f32[512,512]{1,0:T(8,128)S(1)}, f32[512,512]{1,0:T(8,128)S(1)}, u32[]{:S(2)}, u32[]{:S(2)}) collective-permute-start(f32[512,512]{1,0:T(8,128)S(1)} %get-tuple-element.324), channel_id=1, source_target_pairs={{0,6},{2,4},{4,2},{6,0},{1,7},{3,5},{5,3},{7,1},{8,14},{10,12},{12... | collective-permute-start | bytes 3145736 | tf_op jit(solution)/shard_map/ppermute | solution.py:463
  262.8 30.2 %collective-permute-start.24 = (f32[2,8,2048]{2,1,0:T(8,128)S(1)}, f32[2,8,2048]{2,1,0:T(8,128)S(1)}, u32[]{:S(2)}, u32[]{:S(2)}) collective-permute-start(f32[2,8,2048]{2,1,0:T(8,128)S(1)} %get-tuple-element.193), channel_id=1, source_target_pairs={{2,0},{4,2},{6,4},{3,1},{5,3},{7,5},{10,8},{12,10},{14,12},{11,9},... | collective-permute-start | bytes 393224 | tf_op jit(solution)/shard_map/ppermute | solution.py:469
  293.1 208.3 %reduce-scatter.5.cloned.1.call-start = ((), (), s32[]{:S(2)}) async-start(), calls=%async_computation.3 | async-start | bytes 5242880 | tf_op jit(solution)/shard_map/reduce_scatter | solution.py:604
  293.1 16.0 %collective-permute-start.28 = (f32[1,512,1024]{2,1,0:T(8,128)S(1)}, f32[1,512,1024]{2,1,0:T(8,128)}, u32[]{:S(2)}, u32[]{:S(2)}) collective-permute-start(f32[1,512,1024]{2,1,0:T(8,128)S(1)} %bitcast.178), channel_id=1, source_target_pairs={{0,1},{1,0},{2,3},{3,2},{4,5},{5,4},{6,7},{7,6},{8,9},{9,8},{10,11... | collective-permute-start | bytes 6291464 | tf_op jit(solution)/shard_map/ppermute | solution.py:463
  302.0 26.3 %collective-permute-start.25 = (f32[512,512]{1,0:T(8,128)}, f32[512,512]{1,0:T(8,128)}, u32[]{:S(2)}, u32[]{:S(2)}) collective-permute-start(f32[512,512]{1,0:T(8,128)} %get-tuple-element.208), channel_id=1, source_target_pairs={{0,2},{2,0},{4,6},{6,4},{1,3},{3,1},{5,7},{7,5},{8,10},{10,8},{12,... | collective-permute-start | bytes 3145736 | tf_op jit(solution)/shard_map/ppermute | solution.py:463
  303.8 47.5 %collective-permute-start.26 = (f32[512,512]{1,0:T(8,128)}, f32[512,512]{1,0:T(8,128)}, u32[]{:S(2)}, u32[]{:S(2)}) collective-permute-start(f32[512,512]{1,0:T(8,128)} %get-tuple-element.209), channel_id=1, source_target_pairs={{0,4},{2,6},{4,0},{6,2},{1,5},{3,7},{5,1},{7,3},{8,12},{10,14},{12... | collective-permute-start | bytes 3145736 | tf_op jit(solution)/shard_map/ppermute | solution.py:463
  303.8 47.5 %collective-permute-start.27 = (f32[512,512]{1,0:T(8,128)}, f32[512,512]{1,0:T(8,128)}, u32[]{:S(2)}, u32[]{:S(2)}) collective-permute-start(f32[512,512]{1,0:T(8,128)} %get-tuple-element.210), channel_id=1, source_target_pairs={{0,6},{2,4},{4,2},{6,0},{1,7},{3,5},{5,3},{7,1},{8,14},{10,12},{12... | collective-permute-start | bytes 3145736 | tf_op jit(solution)/shard_map/ppermute | solution.py:463
  306.4 17.4 %collective-permute-start.29 = (f32[2,256,256]{2,1,0:T(8,128)}, f32[2,256,256]{2,1,0:T(8,128)}, u32[]{:S(2)}, u32[]{:S(2)}) collective-permute-start(f32[2,256,256]{2,1,0:T(8,128)} %pad_add_fusion), channel_id=1, source_target_pairs={{0,1},{1,0},{2,3},{3,2},{4,5},{5,4},{6,7},{7,6},{8,9},{9,8},{10,11... | collective-permute-start | bytes 1572872 | tf_op jit(solution)/shard_map/ppermute | solution.py:463
  351.3 54.2 %collective-permute-start.30 = (f32[2,2,1024,128]{3,2,1,0:T(8,128)}, f32[2,2,1024,128]{3,2,1,0:T(8,128)}, u32[]{:S(2)}, u32[]{:S(2)}) collective-permute-start(f32[2,2,1024,128]{3,2,1,0:T(8,128)} %get-tuple-element.220), channel_id=1, source_target_pairs={{0,2},{2,0},{4,6},{6,4},{1,3},{3,1},{5,7},{7,5},{8,10},{10,8},{12,... | collective-permute-start | bytes 6291464 | tf_op jit(solution)/shard_map/ppermute | solution.py:463
  351.6 55.8 %collective-permute-start.31 = (f32[2,2,1024,128]{3,2,1,0:T(8,128)}, f32[2,2,1024,128]{3,2,1,0:T(8,128)}, u32[]{:S(2)}, u32[]{:S(2)}) collective-permute-start(f32[2,2,1024,128]{3,2,1,0:T(8,128)} %get-tuple-element.222), channel_id=1, source_target_pairs={{0,4},{2,6},{4,0},{6,2},{1,5},{3,7},{5,1},{7,3},{8,12},{10,14},{12... | collective-permute-start | bytes 6291464 | tf_op jit(solution)/shard_map/ppermute | solution.py:463
  371.6 28.8 %collective-permute-start.35 = (f32[2,8,256]{2,1,0:T(8,128)S(1)}, f32[2,8,256]{2,1,0:T(8,128)S(1)}, u32[]{:S(2)}, u32[]{:S(2)}) collective-permute-start(f32[2,8,256]{2,1,0:T(8,128)S(1)} %get-tuple-element.232), channel_id=1, source_target_pairs={{2,0},{4,2},{6,4},{3,1},{5,3},{7,5},{10,8},{12,10},{14,12},{11,9},... | collective-permute-start | bytes 49160 | tf_op jit(solution)/shard_map/ppermute | solution.py:469
  375.0 35.1 %collective-permute-start.32 = (f32[512,128]{1,0:T(8,128)}, f32[512,128]{1,0:T(8,128)S(1)}, u32[]{:S(2)}, u32[]{:S(2)}) collective-permute-start(f32[512,128]{1,0:T(8,128)} %get-tuple-element.352), channel_id=1, source_target_pairs={{0,2},{2,0},{4,6},{6,4},{1,3},{3,1},{5,7},{7,5},{8,10},{10,8},{12,... | collective-permute-start | bytes 786440 | tf_op jit(solution)/shard_map/ppermute | solution.py:463
  377.6 32.5 %collective-permute-start.33 = (f32[512,128]{1,0:T(8,128)}, f32[512,128]{1,0:T(8,128)S(1)}, u32[]{:S(2)}, u32[]{:S(2)}) collective-permute-start(f32[512,128]{1,0:T(8,128)} %get-tuple-element.351), channel_id=1, source_target_pairs={{0,4},{2,6},{4,0},{6,2},{1,5},{3,7},{5,1},{7,3},{8,12},{10,14},{12... | collective-permute-start | bytes 786440 | tf_op jit(solution)/shard_map/ppermute | solution.py:463
  411.2 39.7 %collective-permute-start.36 = (f32[2,1024,128]{2,1,0:T(8,128)}, f32[2,1024,128]{2,1,0:T(8,128)}, u32[]{:S(2)}, u32[]{:S(2)}) collective-permute-start(f32[2,1024,128]{2,1,0:T(8,128)} %slice_bitcast_fusion.1), channel_id=1, source_target_pairs={{0,4},{2,6},{4,0},{6,2},{1,5},{3,7},{5,1},{7,3},{8,12},{10,14},{12... | collective-permute-start | bytes 3145736 | tf_op jit(solution)/shard_map/ppermute | solution.py:463
  415.0 37.5 %collective-permute-start.37 = (f32[2,1024,128]{2,1,0:T(8,128)}, f32[2,1024,128]{2,1,0:T(8,128)}, u32[]{:S(2)}, u32[]{:S(2)}) collective-permute-start(f32[2,1024,128]{2,1,0:T(8,128)} %slice_bitcast_fusion), channel_id=1, source_target_pairs={{0,2},{2,0},{4,6},{6,4},{1,3},{3,1},{5,7},{7,5},{8,10},{10,8},{12,... | collective-permute-start | bytes 3145736 | tf_op jit(solution)/shard_map/ppermute | solution.py:463
  419.3 30.4 %collective-permute-start.38 = (f32[2,2,2,160,128]{4,3,0,2,1:T(8,128)S(1)}, f32[2,2,2,160,128]{4,3,0,2,1:T(8,128)}, u32[]{:S(2)}, u32[]{:S(2)}) collective-permute-start(f32[2,2,2,160,128]{4,3,0,2,1:T(8,128)S(1)} %dynamic-slice_bitcast_fusion), channel_id=1, source_target_pairs={{0,2},{2,0},{4,6},{6,4},{1,3},{3,1},{5,7},{7,5},{8,10},{10,8},{12,... | collective-permute-start | bytes 1966088 | tf_op jit(solution)/shard_map/ppermute | solution.py:463
  454.9 15.6 %collective-permute-start.42 = (f32[512,2048]{1,0:T(8,128)}, f32[512,2048]{1,0:T(8,128)}, u32[]{:S(2)}, u32[]{:S(2)}) collective-permute-start(f32[512,2048]{1,0:T(8,128)} %bitcast_add_fusion), channel_id=1, source_target_pairs={{0,1},{1,0},{2,3},{3,2},{4,5},{5,4},{6,7},{7,6},{8,9},{9,8},{10,11... | collective-permute-start | bytes 12582920 | tf_op jit(solution)/shard_map/ppermute | solution.py:463
  454.9 15.6 %collective-permute-start.46 = (f32[512,2048]{1,0:T(8,128)}, f32[512,2048]{1,0:T(8,128)}, u32[]{:S(2)}, u32[]{:S(2)}) collective-permute-start(f32[512,2048]{1,0:T(8,128)} %fusion.47), channel_id=1, source_target_pairs={{0,1},{1,0},{2,3},{3,2},{4,5},{5,4},{6,7},{7,6},{8,9},{9,8},{10,11... | collective-permute-start | bytes 12582920 | tf_op jit(solution)/shard_map/ppermute | solution.py:463
  459.0 43.4 %collective-permute-start.39 = (f32[1024,128]{1,0:T(8,128)}, f32[1024,128]{1,0:T(8,128)}, u32[]{:S(2)}, u32[]{:S(2)}) collective-permute-start(f32[1024,128]{1,0:T(8,128)} %get-tuple-element.322), channel_id=1, source_target_pairs={{0,8},{8,0},{16,24},{24,16},{1,9},{9,1},{17,25},{25,17},{2,10},{10... | collective-permute-start | bytes 1572872 | tf_op jit(solution)/shard_map/ppermute | solution.py:463
  460.6 41.9 %collective-permute-start.40 = (f32[1024,128]{1,0:T(8,128)}, f32[1024,128]{1,0:T(8,128)}, u32[]{:S(2)}, u32[]{:S(2)}) collective-permute-start(f32[1024,128]{1,0:T(8,128)} %get-tuple-element.321), channel_id=1, source_target_pairs={{0,16},{8,24},{16,0},{24,8},{1,17},{9,25},{17,1},{25,9},{2,18},{10... | collective-permute-start | bytes 1572872 | tf_op jit(solution)/shard_map/ppermute | solution.py:463
  466.0 50.0 %collective-permute-start.41 = (f32[1024,128]{1,0:T(8,128)}, f32[1024,128]{1,0:T(8,128)}, u32[]{:S(2)}, u32[]{:S(2)}) collective-permute-start(f32[1024,128]{1,0:T(8,128)} %get-tuple-element.320), channel_id=1, source_target_pairs={{0,24},{8,16},{16,8},{24,0},{1,25},{9,17},{17,9},{25,1},{2,26},{10... | collective-permute-start | bytes 1572872 | tf_op jit(solution)/shard_map/ppermute | solution.py:463
  516.0 17.8 %collective-permute-start.47 = (f32[15712]{0:T(1024)S(1)}, f32[15712]{0:T(1024)S(1)}, u32[]{:S(2)}, u32[]{:S(2)}) collective-permute-start(f32[15712]{0:T(1024)S(1)} %add.334), channel_id=1, source_target_pairs={{0,8},{8,0},{16,24},{24,16},{1,9},{9,1},{17,25},{25,17},{2,10},{10... | collective-permute-start | bytes 188552 | tf_op jit(solution)/shard_map/ppermute | solution.py:463
  528.5 20.6 %collective-permute-start.49 = (f32[512,128]{1,0:T(8,128)}, f32[512,128]{1,0:T(8,128)S(1)}, u32[]{:S(2)}, u32[]{:S(2)}) collective-permute-start(f32[512,128]{1,0:T(8,128)} %get-tuple-element.348), channel_id=1, source_target_pairs={{0,2},{2,0},{4,6},{6,4},{1,3},{3,1},{5,7},{7,5},{8,10},{10,8},{12,... | collective-permute-start | bytes 786440 | tf_op jit(solution)/shard_map/ppermute | solution.py:463
  529.9 19.1 %collective-permute-start.50 = (f32[512,128]{1,0:T(8,128)}, f32[512,128]{1,0:T(8,128)S(1)}, u32[]{:S(2)}, u32[]{:S(2)}) collective-permute-start(f32[512,128]{1,0:T(8,128)} %get-tuple-element.347), channel_id=1, source_target_pairs={{0,4},{2,6},{4,0},{6,2},{1,5},{3,7},{5,1},{7,3},{8,12},{10,14},{12... | collective-permute-start | bytes 786440 | tf_op jit(solution)/shard_map/ppermute | solution.py:463
  531.4 17.7 %collective-permute-start.51 = (f32[512,128]{1,0:T(8,128)S(1)}, f32[512,128]{1,0:T(8,128)S(1)}, u32[]{:S(2)}, u32[]{:S(2)}) collective-permute-start(f32[512,128]{1,0:T(8,128)S(1)} %get-tuple-element.346), channel_id=1, source_target_pairs={{0,6},{2,4},{4,2},{6,0},{1,7},{3,5},{5,3},{7,1},{8,14},{10,12},{12... | collective-permute-start | bytes 786440 | tf_op jit(solution)/shard_map/ppermute | solution.py:463
  (81 other events, 844.1 us)
Sparse Core Ops, SparseCore 0:
  293.2 77.2 reduce-scatter.2
  402.7 98.6 reduce-scatter.4

commit v4 on v3

--- a/solution.py
+++ b/solution.py
@@ -124,7 +124,7 @@
 
 
 def call(kernel, inputs, in_specs, out_specs, out_shape, grid, name, micros, scratch=(), index=None):
-    scalars = () if index is None else (index.reshape(1),)
+    scalars = () if index is None else (index.reshape(-1),)
     return pl.pallas_call(
         kernel,
         grid_spec=pltpu.PrefetchScalarGridSpec(
@@ -145,7 +145,7 @@
 
 def state_kernel(
     heads, pre_x, edge_x, taps_x, pre_bc, edge_bc, taps_bc, dtraw, params,
-    local_state, total_decay, u_out, b_out, c_out, steps_out, b_turned,
+    state_out, u_out, b_out, c_out, steps_out, b_turned,
 ):
     slots, lanes = pre_x.shape[1:]
     state = b_out.shape[2]
@@ -169,10 +169,10 @@
     cumul = exact(rate, triangle(slots, BF16), ((1,), (1,)))
     steps_out[0, 0] = jnp.concatenate([step, cumul], axis=0)
     last = cumul[:, slots - 1 : slots]
-    total_decay[0] = widen(jnp.broadcast_to(jnp.exp(last), (heads, 8)), lanes)
+    state_out[0, state:] = widen(jnp.broadcast_to(jnp.exp(last), (heads, 8)), lanes)
     xd = (widen(step, lanes) * x).astype(BF16)
     tail = (widen(jnp.exp(last - cumul), lanes) * xd.astype(F32)).astype(BF16)
-    local_state[0] = mm(b_turned[...], tail)
+    state_out[0, :state] = mm(b_turned[...], tail)
 
 
 def inside_kernel(heads, width, u, steps, params, b_act, c_act, local_out, scores):
@@ -225,7 +225,7 @@
 
 
 def gate_back_kernel(
-    heads, inner_all, y, z, grad_out, gain, sums, c_act, steps,
+    heads, inner_all, y, z, grad_out, gain, sums, c_act, steps, decay,
     gated_out, grad_y, grad_z, gain_grad, leaving, c_turned,
 ):
     lanes = z.shape[-1]
@@ -252,7 +252,9 @@
     grad_y[0] = dy
     grad_z[0] = (dg * yv * slope(zv, sig)).astype(BF16)
     growth = widen(jnp.exp(steps[0, 0][heads:]), lanes)
-    leaving[0] = mm(c_turned[...], (growth * dy).astype(BF16))
+    state = c_turned.shape[0]
+    leaving[0, :state] = mm(c_turned[...], (growth * dy).astype(BF16))
+    leaving[0, state:] = decay[0]
 
 
 def inside_back_kernel(
@@ -475,12 +477,11 @@
     return lax.psum(value, "head")
 
 
-def gathered_pass(decay, part, reverse):
+def gathered_pass(both, rows, reverse):
     count = lax.axis_size("seq")
     place = lax.axis_index("seq")
-    gathered = lax.all_gather(jnp.concatenate([part, decay], axis=1), "seq")
-    rows = part.shape[1]
-    state = jnp.zeros_like(part)
+    gathered = lax.all_gather(both, "seq")
+    state = jnp.zeros_like(both[:, :rows])
     for turn in range(count - 1):
         source = count - 1 - turn if reverse else turn
         ahead = source > place if reverse else source < place
@@ -504,13 +505,11 @@
     return lax.optimization_barrier(values)
 
 
-def passed_on(decay, part, reverse, first, second):
+def passed_on(both, rows, reverse, first, second):
     if lax.axis_size("seq") != 4:
         beside_first = first()
-        return gathered_pass(decay, part, reverse), beside_first, second(beside_first)
+        return gathered_pass(both, rows, reverse), beside_first, second(beside_first)
     place = lax.axis_index("seq")
-    rows = part.shape[1]
-    both = jnp.concatenate([part, decay], axis=1)
     got = [quarter(both, 2, place)] + [swapped(quarter(both, 2, place ^ d), "seq", d) for d in (1, 2, 3)]
     got, beside_first = tied(got, first())
     order = (3, 2, 1, 0) if reverse else (0, 1, 2, 3)
@@ -679,19 +678,24 @@
     small = small.reshape(-1, 2, 2, 2, 2, small.shape[1] // 16).transpose(4, 3, 1, 2, 0, 5)
     a = a[0] + swapped(a[1], "seq", 2)
     b = b[0] + swapped(b[1], "seq", 1)
-    return a, b, small_step(small, "seq", 1, lax.axis_index("seq") % 2)
-
-
-def out_weight(pieces):
+    small = small_step(small, "seq", 1, lax.axis_index("seq") % 2)
+    small = small_step(small, "seq", 2, lax.axis_index("seq") // 2)
+    small = small.reshape((4,) + small.shape[2:])
+    return jnp.concatenate([jnp.concatenate([a, b], axis=0), small], axis=1)
+
+
+def out_weight(pieces, small):
     even, odd = pieces[0] + pieces[2], pieces[1] + pieces[3]
+    size = even.shape[0] - small
     parity = lax.axis_index("batch") % 2
-    return jnp.concatenate([jnp.where(parity == 0, even, odd), jnp.where(parity == 0, odd, even)], axis=0)
+    low = jnp.where(parity == 0, even[:size], odd[:size])
+    high = jnp.where(parity == 0, odd[:size], even[:size])
+    return jnp.concatenate([low, high], axis=0), even[size:] + odd[size:]
 
 
 def added_over(values, axis):
-    for bit in (1, 2):
-        values = values + swapped(values, axis, bit)
-    return values
+    far = [swapped(values, axis, d) for d in (1, 2, 3)]
+    return (values + far[0]) + (far[1] + far[2])
 
 
 def per_device(
@@ -733,15 +737,15 @@
     proj = mm(normed, jnp.concatenate([w_bc, w_dt], axis=1))
     pre_bc = proj[:, : 2 * state].reshape(seqs, slots, 2 * state)
     projected = jnp.einsum("tg,gjn->tjn", normed, gate_input_weight, preferred_element_type=F32)
-    gate_z = projected[:, 0].reshape(seqs, slots, inner)
-    pre_x = projected[:, 1].reshape(seqs, slots, inner)
-    edges = jnp.concatenate([pre_x[:, slots - EDGE :], pre_bc[:, slots - EDGE :]], axis=2)
+    projected = projected.transpose(1, 0, 2).reshape(2, seqs, slots, inner)
+    edges = jnp.concatenate([projected[1, :, slots - EDGE :], pre_bc[:, slots - EDGE :]], axis=2)
     edges = shifted(edges, "seq", 1)
     edge_x, edge_bc = edges[..., :inner], edges[..., inner:]
     dtraw = proj[:, 2 * state :].reshape(seqs, slots, groups, heads).transpose(0, 2, 3, 1)
     params = head_params.reshape(3, groups, heads).transpose(1, 2, 0)
     gain = gate_gain.reshape(1, inner)
 
+    part_of = lambda j: pl.BlockSpec((None, 1, slots, LANES), lambda b, g: (j, b, 0, g))
     grid = (seqs, groups)
     S = jax.ShapeDtypeStruct
     wide = pl.BlockSpec((1, slots, LANES), lambda b, g: (b, 0, g))
@@ -756,20 +760,22 @@
     par_spec = pl.BlockSpec((1, heads, 3), lambda b, g: (g, 0, 0))
     wide_s = S((seqs, slots, inner), F32)
     wide_b = S((seqs, slots, inner), BF16)
-    state_s = S((seqs, state, inner), F32)
+    decay_s = S((seqs, state + EDGE, inner), F32)
+    with_decay = pl.BlockSpec((1, state + EDGE, LANES), lambda b, g: (b, 0, g))
+    decay_spec = pl.BlockSpec((1, EDGE, LANES), lambda b, g: (b, state // EDGE, g))
     bc_b = S((seqs, slots, state), F32)
     settings = pltpu.CompilerParams(vmem_limit_bytes=VMEM_LIMIT)
 
-    local_state, total_decay, u, b_act, c_act, steps = call(
+    local_state, u, b_act, c_act, steps = call(
         functools.partial(state_kernel, heads),
-        [pre_x, edge_x, conv_x, pre_bc, edge_bc, conv_bc, dtraw, params],
+        [projected, edge_x, conv_x, pre_bc, edge_bc, conv_bc, dtraw, params],
         [
-            wide, edge, taps, per_seq(slots, 2 * state), per_seq(EDGE, 2 * state),
+            part_of(1), edge, taps, per_seq(slots, 2 * state), per_seq(EDGE, 2 * state),
             fixed(CONV + 1, 2 * state), by_head(heads), par_spec,
         ],
-        [states, edge, wide, per_seq(slots, state), per_seq(slots, state), by_head(2 * heads)],
+        [with_decay, wide, per_seq(slots, state), per_seq(slots, state), by_head(2 * heads)],
         [
-            state_s, S((seqs, EDGE, inner), F32), wide_s, bc_b, bc_b,
+            decay_s, wide_s, bc_b, bc_b,
             S((seqs, groups, 2 * heads, slots), F32),
         ],
         grid,
@@ -796,15 +802,15 @@
             scratch=[pltpu.VMEM((slots, slots), F32)],
         )
 
-    entering, grad_out, local_out = passed_on(total_decay, local_state, False, mix_back, scan_inside)
+    entering, grad_out, local_out = passed_on(local_state, state, False, mix_back, scan_inside)
     if paired:
         entering, mix_far, seq_first = tied(entering, mix_far, seq_first)
         seq_second = rows_of_seq_second(*seq_first)
 
     y, sums = call(
         functools.partial(gate_kernel, heads),
-        [local_out, entering, c_act, steps, gate_z, grad_out, gain],
-        [wide, states, per_seq(slots, state), by_head(2 * heads), wide, wide, gain_spec],
+        [local_out, entering, c_act, steps, projected, grad_out, gain],
+        [wide, states, per_seq(slots, state), by_head(2 * heads), part_of(0), wide, gain_spec],
         [wide, per_seq(8, slots)],
         [wide_s, S((seqs, 8, slots), F32)],
         grid,
@@ -815,10 +821,13 @@
 
     gated, grad_y, grad_z, gain_grad, leaving = call(
         functools.partial(gate_back_kernel, heads, inner_all),
-        [y, gate_z, grad_out, gain, sums, c_act, steps],
-        [wide, wide, wide, gain_spec, per_seq(8, slots), per_seq(slots, state), by_head(2 * heads)],
-        [wide, wide, wide, line, states],
-        [wide_b, wide_s, wide_b, S((seqs, 1, inner), F32), state_s],
+        [y, projected, grad_out, gain, sums, c_act, steps, local_state],
+        [
+            wide, part_of(0), wide, gain_spec, per_seq(8, slots), per_seq(slots, state), by_head(2 * heads),
+            decay_spec,
+        ],
+        [wide, wide, wide, line, with_decay],
+        [wide_b, wide_s, wide_b, S((seqs, 1, inner), F32), decay_s],
         grid,
         "gate_back",
         17,
@@ -848,7 +857,7 @@
             return ()
         return assembled(rows_of_seq_third(*beside[2])), mm(gated, w_out)
 
-    coming, beside, ready = passed_on(total_decay, leaving, True, scan_inside_back, rows_ready)
+    coming, beside, ready = passed_on(leaving, state, True, scan_inside_back, rows_ready)
     inside, grad_bc = beside[:2]
     if paired:
         coming, grad_z_sent, gated_sent, ready = tied(coming, grad_z, gated, ready)
@@ -861,9 +870,9 @@
         mixed = mm(gated, w_out)
     grad_pre, tail_x, first_x, taps_grad_x, grad_dt, params_grad, grad_b = call(
         functools.partial(scan_back_kernel, heads),
-        [u, pre_x, edge_x, conv_x, dtraw, params, steps, b_act, y, grad_y, inside, entering, coming],
+        [u, projected, edge_x, conv_x, dtraw, params, steps, b_act, y, grad_y, inside, entering, coming],
         [
-            wide, wide, edge, taps, by_head(heads), par_spec, by_head(2 * heads), per_seq(slots, state),
+            wide, part_of(1), edge, taps, by_head(heads), par_spec, by_head(2 * heads), per_seq(slots, state),
             wide, wide, wide, states, states,
         ],
         [
@@ -938,10 +947,10 @@
     portion = jnp.einsum("tjn,gjn->tg", grad_zx, gate_input_weight, preferred_element_type=F32)
     portion = portion + mm(grad_dtr, w_dt, ((1,), (1,)))
     if paired:
-        a, b, small = second_transfers(a, b, small)
-        a, b, small, portion, mixed = tied(a, b, small, portion, mixed)
-        out_pieces = sent_back(jnp.concatenate([a, b], axis=0), "batch")
-        small = small_step(small, "seq", 2, lax.axis_index("seq") // 2)
+        small_rows = small.shape[0]
+        out_sum, portion, mixed, sum_x = tied(second_transfers(a, b, small), portion, mixed, sum_x)
+        out_pieces = sent_back(out_sum, "batch")
+        x_pieces = sent_back(sum_x, "seq")
     mixed = head_sum(mixed)
     mixed_out = (mask * (hidden_f + mixed)).astype(BF16).reshape(seqs, slots, model)
     grad_normed = head_sum(portion) + mm(grad_pre_bc, w_bc, ((1,), (1,)))
@@ -958,16 +967,10 @@
     flat = jnp.concatenate([piece.reshape(-1) for piece in pieces])
     if paired:
         flat = added_over(flat, "seq")
-        out_pieces, sum_x, flat, small, grad_hidden, mixed_out = tied(
-            out_pieces, sum_x, flat, small, grad_hidden, mixed_out
-        )
-        batch_place = lax.axis_index("batch")
-        x_pieces = sent_back(sum_x, "seq")
-        small = small_step(small, "batch", 2, batch_place // 2)
-        done_small = small_step(small, "batch", 1, batch_place % 2)
+        out_pieces, x_pieces, flat, grad_hidden, mixed_out = tied(out_pieces, x_pieces, flat, grad_hidden, mixed_out)
         flat = added_over(flat, "batch")
         grad_weight = finished(z_pieces, x_pieces)
-        grad_w_out = out_weight(out_pieces)
+        grad_w_out, done_small = out_weight(out_pieces, small_rows)
         bc_mine = done_small[:state]
         bc_other = swapped(bc_mine, "head", 1)
         grad_w_bc = jnp.concatenate(

time: 567 us -> 560 us (0.988)
  waiting for transfers between devices: 162 us -> 155 us
    reduce_scatter x2, waiting for transfers between devices: 9.75 us -> 0.02 us  [over_batch(): return lax.psum_scatter(part, 'batch', scatter_dimension=0, tiled=True)[0]]
    ppermute x3, waiting for transfers between devices: 22.3 us -> 32 us  [shifted(): lax.ppermute(value, axis, [(source, source + steps) for source in range(i...]
    ppermute x52, waiting for transfers between devices: 130 us -> 123 us  [swapped(): return lax.ppermute(value, axis, [(i, i ^ bit) for i in range(count)])]
    unnamed x155 -> x148, local copies, waits for them, and re-layouts: 19.5 us -> 22.6 us
  transfers between devices with their start and end apart: 57 -> 57, of which waited for: 24 -> 24; matrix products, arithmetic and copies ran while one was open for 22% -> 21% of each run, Pallas kernels for 24% -> 25%
where the time goes in v4:
time: 560 us; the launch traced here: 553 us
  waiting for transfers between devices  155 us (28%)
  Pallas kernels  136 us (24%)
  starting transfers between devices  73.9 us (13%)
  matrix products  71.3 us (13%)
  local copies, waits for them, and re-layouts  50.8 us (9%)
  other arithmetic  50 us (9%)
  between operations  15.5 us (3%)
    pallas_call x14, Pallas kernels, call(): pl.pallas_call(kernel, grid_spec=pltpu.PrefetchScalarGridSpec(num_scalar_...  136 us
    ppermute x52, waiting for transfers between devices, swapped(): return lax.ppermute(value, axis, [(i, i ^ bit) for i in range(count)])  123 us
    ppermute x52, starting transfers between devices, swapped(): return lax.ppermute(value, axis, [(i, i ^ bit) for i in range(count)])  66.5 us
    dot_general x6, matrix products, mm(): lax.dot_general(a, b, (dims, ((), ())), precision=precision, preferred_el...  33.8 us
    ppermute x3, waiting for transfers between devices, shifted(): lax.ppermute(value, axis, [(source, source + steps) for source in range(i...  32 us
    dot_general x1, matrix products, per_device(): jnp.einsum('tjn,gjn->tg', grad_zx, gate_input_weight, preferred_element_t...  23.6 us
    unnamed x148, local copies, waits for them, and re-layouts  22.6 us
    dot_general x1, matrix products, per_device(): jnp.einsum('tg,gjn->tjn', normed, gate_input_weight, preferred_element_ty...  13.9 us
  transfers between devices with their start and end apart: 57, of which 24 were waited for; matrix products, arithmetic and copies ran while one was open for 21% of the time, Pallas kernels for 25%

profile of v4, /device:TPU:0, one launch (start us, length us, event | category | flops | bytes accessed | tf_op | source)
XLA Modules:
  0.0 553.1 jit_solution(16434272800376043345)
XLA Ops:
  7.2 2.2 fusion.18
  11.3 13.9 %fusion.2 = f32[512,2,2048]{2,0,1:T(8,128)S(1)} fusion(bf16[2048,2,2048]{2,1,0:T(2,128)(2,1)} %param.14, bf16[512,2048]{1,0:T(8,128)(2,1)S(1)} %fusion.12.own_rows), kind=kOutput, calls=%fused_computation.2 | convolution fusion | flops 8589934592 | bytes 27262976 | tf_op jit(solution)/shard_map/tg,gjn->tjn/dot_general | solution.py:739
  25.3 3.3 copy-done.35
  32.1 4.9 collective-permute-start
  47.7 11.4 %scan_state.1 = (f32[2,136,2048]{2,1,0:T(8,128)S(1)}, f32[2,256,2048]{2,1,0:T(8,128)}, f32[2,256,128]{2,1,0:T(8,128)S(1)}, f32[2,256,128]{2,1,0:T(8,128)S(1)}, f32[2,4,16,256]{3,2,1,0:T(8,128)S(1)}) custom-call(f32[2,2,256,2048]{3,2,1,0:T(8,128)} %bitcast.193, f32[2,8,2048]{2,1,0:T(8,128)S(1)} %slice.196.edge_x, f32[5,2048]{1,0:T(8,128)S(1)} %copy-done.29, ...), custom_call_target="tpu_custom_call" | custom-call | flops 4674999808 | bytes 8500000 | tf_op jit(solution)/shard_map/scan_state/pallas_call | solution.py:128
  59.1 5.3 collective-permute-done.1
  68.9 9.5 %fusion.45 = f32[512,2048]{1,0:T(8,128)} fusion(bf16[512,2048]{1,0:T(8,128)(2,1)S(1)} %copy-done.39, bf16[2048,2048]{1,0:T(8,128)(2,1)} %param.21), kind=kOutput, calls=%fused_computation.152 | convolution fusion | flops 4294967296 | bytes 14680064 | tf_op jit(solution)/shard_map/dot_general | solution.py:22
  78.4 2.6 collective-permute-done.3
  81.0 10.6 %collective-permute-done.5 = f32[2,136,512]{2,1,0:T(8,128)S(1)} collective-permute-done((f32[2,136,512]{2,1,0:T(8,128)S(1)}, f32[2,136,512]{2,1,0:T(8,128)S(1)}, u32[]{:S(2)}, u32[]{:S(2)}) %collective-permute-start.5) | collective-permute-done | bytes 557088 | tf_op jit(solution)/shard_map/ppermute | solution.py:465
  96.2 9.4 %scan_inside.1.local_out = f32[2,256,2048]{2,1,0:T(8,128)S(1)} custom-call(f32[2,256,2048]{2,1,0:T(8,128)} %get-tuple-element.137.u, f32[2,4,16,256]{3,2,1,0:T(8,128)S(1)} %get-tuple-element.140.steps, f32[4,8,3]{2,1,0:T(8,128)S(1)} %bitcast.189, f32[2,256,128]{2,1,0:T(8,128)S(1)} %get-tuple-element.141.b_act, f32[2,256,128]{2,1,0:T(8,128)S(1)} %get-tuple-element.148.c_act), custom_call_target="tpu_custom_call" | custom-call | flops 4950000128 | bytes 9000000 | tf_op jit(solution)/shard_map/scan_inside/pallas_call | solution.py:128
  107.7 9.0 %collective-permute-done.8 = f32[2,128,512]{2,1,0:T(8,128)S(1)} collective-permute-done((f32[2,128,512]{2,1,0:T(8,128)S(1)}, f32[2,128,512]{2,1,0:T(8,128)S(1)}, u32[]{:S(2)}, u32[]{:S(2)}) %collective-permute-start.8) | collective-permute-done | bytes 524320 | tf_op jit(solution)/shard_map/ppermute | solution.py:465
  120.4 2.7 pad_maximum_fusion.2
  124.3 11.3 %gate.1 = (f32[2,256,2048]{2,1,0:T(8,128)}, f32[2,8,256]{2,1,0:T(8,128)S(1)}) custom-call(f32[2,256,2048]{2,1,0:T(8,128)} %copy-done.2, f32[2,128,2048]{2,1,0:T(8,128)S(1)} %pad_maximum_fusion.1.entering, f32[2,256,128]{2,1,0:T(8,128)S(1)} %get-tuple-element.148.c_act, f32[2,4,16,256]{3,2,1,0:T(8,128)S(1)} %get-tuple-element.140.steps, ...), custom_call_target="tpu_custom_call" | custom-call | flops 4124999936 | bytes 7500000 | tf_op jit(solution)/shard_map/gate/pallas_call | solution.py:128
  136.7 11.8 %gate_back.1 = (bf16[2,256,2048]{2,1,0:T(8,128)(2,1)S(1)}, f32[2,256,2048]{2,1,0:T(8,128)}, bf16[2,256,2048]{2,1,0:T(8,128)(2,1)S(1)}, f32[2,1,2048]{2,1,0:T(1,128)S(1)}, f32[2,136,2048]{2,1,0:T(8,128)}) custom-call(f32[2,256,2048]{2,1,0:T(8,128)} %get-tuple-element.160.y, f32[2,2,256,2048]{3,2,1,0:T(8,128)} %bitcast.195, f32[2,256,2048]{2,1,0:T(8,128)} %bitcast.198, ...), custom_call_target="tpu_custom_call" | custom-call | flops 4674999808 | bytes 8500000 | tf_op jit(solution)/shard_map/gate_back/pallas_call | solution.py:128
  148.5 4.3 constant_dynamic-slice_fusion.1
  156.3 20.3 %scan_inside_back.1 = (f32[2,256,2048]{2,1,0:T(8,128)}, f32[2,256,256]{2,1,0:T(8,128)S(1)}) custom-call(f32[2,256,2048]{2,1,0:T(8,128)} %get-tuple-element.137.u, f32[2,4,16,256]{3,2,1,0:T(8,128)S(1)} %get-tuple-element.140.steps, f32[2,256,128]{2,1,0:T(8,128)S(1)} %get-tuple-element.141.b_act, f32[2,256,128]{2,1,0:T(8,128)S(1)} %get-tuple-element.148.c_act, ...), custom_call_target="tpu_custom_call" | custom-call | flops 7150000128 | bytes 13000000 | tf_op jit(solution)/shard_map/scan_inside_back/pallas_call | solution.py:128
  176.7 3.1 collective-permute-done.11
  179.7 11.4 %collective-permute-done.12 = f32[2,136,512]{2,1,0:T(8,128)S(1)} collective-permute-done((f32[2,136,512]{2,1,0:T(8,128)}, f32[2,136,512]{2,1,0:T(8,128)S(1)}, u32[]{:S(2)}, u32[]{:S(2)}) %collective-permute-start.12) | collective-permute-done | bytes 557088 | tf_op jit(solution)/shard_map/ppermute | solution.py:465
  192.3 4.6 maximum_maximum_fusion.mine
  203.1 9.4 %fusion.46 = f32[512,2048]{1,0:T(8,128)} fusion(bf16[512,2048]{1,0:T(8,128)(2,1)S(1)} %bitcast.176, bf16[2048,2048]{1,0:T(8,128)(2,1)} %param.21), kind=kOutput, calls=%fused_computation.153 | convolution fusion | flops 4294967296 | bytes 14680064 | tf_op jit(solution)/shard_map/dot_general | solution.py:22
  212.5 8.2 %assemble.2.far_rows = bf16[3,512,2048]{2,1,0:T(8,128)(2,1)} custom-call(f32[3,512,1024]{2,1,0:T(8,128)} %maximum_maximum_fusion.mine, f32[3,512,1024]{2,1,0:T(8,128)} %collective-permute-done.19.theirs, s32[1]{0:T(128)} %bitcast.21.side), custom_call_target="tpu_custom_call" | custom-call | flops 825000000 | bytes 1500000 | tf_op jit(solution)/shard_map/assemble/pallas_call | solution.py:128
  220.7 5.7 %collective-permute-done.18 = f32[2,128,512]{2,1,0:T(8,128)S(1)} collective-permute-done((f32[2,128,512]{2,1,0:T(8,128)S(1)}, f32[2,128,512]{2,1,0:T(8,128)S(1)}, u32[]{:S(2)}, u32[]{:S(2)}) %collective-permute-start.18) | collective-permute-done | bytes 524320 | tf_op jit(solution)/shard_map/ppermute | solution.py:465
  235.4 21.3 %scan_back.1 = (bf16[2,256,2048]{2,1,0:T(8,128)(2,1)S(1)}, f32[2,8,2048]{2,1,0:T(8,128)S(1)}, f32[2,8,2048]{2,1,0:T(8,128)S(1)}, f32[2,8,2048]{2,1,0:T(8,128)S(1...) custom-call(f32[2,256,2048]{2,1,0:T(8,128)} %get-tuple-element.137.u, ...), custom_call_target="tpu_custom_call" | custom-call | flops 9349999616 | bytes 17000000 | tf_op jit(solution)/shard_map/scan_back/pallas_call | solution.py:128
  260.6 18.8 %collective-permute-done.21.refs_2_ = f32[512,512]{1,0:T(8,128)S(1)} collective-permute-done((f32[512,512]{1,0:T(8,128)}, f32[512,512]{1,0:T(8,128)S(1)}, u32[]{:S(2)}, u32[]{:S(2)}) %collective-permute-start.21) | collective-permute-done | bytes 1048608 | tf_op jit(solution)/shard_map/ppermute | solution.py:465
  281.7 9.1 %weight_part.2 = f32[4,4,512,128]{3,2,1,0:T(8,128)} custom-call(bf16[512,2048]{1,0:T(8,128)(2,1)} %copy-done.34, bf16[3,512,2048]{2,1,0:T(8,128)(2,1)} %assemble.2.far_rows, f32[512,512]{1,0:T(8,128)S(1)} %get-tuple-element.194.refs_0_, f32[512,512]{1,0:T(8,128)S(1)} %collective-permute-done.20.refs_1_, f32[512,512]{1,0:T(8,128)S(1)} %collective-permute-done.21.refs_2_, ...), custom_call_target="tpu_custom_call" | custom-call | flops 275000000 | bytes 500000 | tf_op jit(solution)/shard_map/weight_part/pallas_call | solution.py:128
  294.1 5.8 %mend.1 = (bf16[2,256,2048]{2,1,0:T(8,128)(2,1)}, f32[512,512]{1,0:T(8,128)S(1)}, f32[512,512]{1,0:T(8,128)}, f32[512,512]{1,0:T(8,128)}, f32[512,512]{1,0:T(8,128)}) custom-call(s32[1]{0:T(128)} %bitcast.place, bf16[2,256,2048]{2,1,0:T(8,128)(2,1)} %copy-done.31, f32[2,8,2048]{2,1,0:T(8,128)S(1)} %copy-done.33, f32[2,8,2048]{2,1,0:T(8,128)S(1)} %copy-done.28, ...), custom_call_target="tpu_custom_call" | custom-call | flops 1100000000 | bytes 2000000 | tf_op jit(solution)/shard_map/mend/pallas_call | solution.py:128
  305.8 2.7 assemble.3
  309.8 11.0 %pair_part.1 = (f32[2,2,1024,128]{3,2,1,0:T(8,128)S(1)}, f32[2,2,1024,128]{3,2,1,0:T(8,128)S(1)}, f32[2,2,1024,128]{3,2,1,0:T(8,128)}, f32[2,2,1024,128]{3,2,1,0:T(8,128)}) custom-call(s32[1]{0:T(128)} %bitcast.place, bf16[512,2048]{1,0:T(8,128)(2,1)} %copy-done.38, bf16[512,2048]{1,0:T(8,128)(2,1)} %bitcast.173, ...), custom_call_target="tpu_custom_call" | custom-call | flops 275000000 | bytes 500000 | tf_op jit(solution)/shard_map/pair_part/pallas_call | solution.py:128
  324.2 2.1 collective-permute-done.25.refs_1_
  326.3 22.9 %collective-permute-done.26.refs_2_ = f32[512,512]{1,0:T(8,128)} collective-permute-done((f32[512,512]{1,0:T(8,128)}, f32[512,512]{1,0:T(8,128)}, u32[]{:S(2)}, u32[]{:S(2)}) %collective-permute-start.26) | collective-permute-done | bytes 1048608 | tf_op jit(solution)/shard_map/ppermute | solution.py:465
  349.2 10.1 %weight_part.3 = f32[4,4,512,128]{3,2,1,0:T(8,128)} custom-call(bf16[512,2048]{1,0:T(8,128)(2,1)} %copy-done.34, bf16[3,512,2048]{2,1,0:T(8,128)(2,1)} %assemble.2.far_rows, f32[512,512]{1,0:T(8,128)S(1)} %get-tuple-element.223.refs_0_, f32[512,512]{1,0:T(8,128)} %collective-permute-done.25.refs_1_, f32[512,512]{1,0:T(8,128)} %collective-permute-done.26.refs_2_, ...), custom_call_target="tpu_custom_call" | custom-call | flops 275000000 | bytes 500000 | tf_op jit(solution)/shard_map/weight_part/pallas_call | solution.py:128
  361.1 3.9 copy.57
  373.5 2.7 collective-permute-start.32
  376.8 32.0 %collective-permute-done.35 = f32[2,8,256]{2,1,0:T(8,128)S(1)} collective-permute-done((f32[2,8,256]{2,1,0:T(8,128)}, f32[2,8,256]{2,1,0:T(8,128)S(1)}, u32[]{:S(2)}, u32[]{:S(2)}) %collective-permute-start.35) | collective-permute-done | bytes 16416 | tf_op jit(solution)/shard_map/ppermute | solution.py:471
  415.8 2.6 add.296
  419.5 2.2 collective-permute-start.36
  428.4 23.6 %fusion = f32[512,2048,1]{1,0,2:T(8,128)S(1)} fusion(bf16[2048,2,2048]{2,1,0:T(2,128)(2,1)} %param.14, bf16[512,1,2048]{2,0,1:T(8,128)(2,1)} %bitcast.226, bf16[512,1,2048]{2,0,1:T(8,128)(2,1)S(1)} %bitcast.175), kind=kOutput, calls=%fused_computation | convolution fusion | flops 8592031744 | bytes 25165824 | tf_op jit(solution)/shard_map/tjn,gjn->tg/dot_general | solution.py:947
  452.0 5.9 %collective-permute-done.38 = f32[2,2,2,160,128]{4,3,0,2,1:T(8,128)} collective-permute-done((f32[2,2,2,160,128]{4,3,0,2,1:T(8,128)S(1)}, f32[2,2,2,160,128]{4,3,0,2,1:T(8,128)}, u32[]{:S(2)}, u32[]{:S(2)}) %collective-permute-start.38) | collective-permute-done | bytes 655392 | tf_op jit(solution)/shard_map/ppermute | solution.py:465
  460.0 2.7 bitcast_add_fusion
  462.8 3.6 collective-permute-done.39
  471.7 3.0 dynamic-slice_bitcast_fusion.1
  476.2 2.7 collective-permute-start.41
  484.3 8.4 %fusion.14 = (f32[512]{0:T(512)S(1)}, f32[2048]{0:T(1024)S(1)}, f32[512,2048]{1,0:T(8,128)}, bf16[512,2048]{1,0:T(8,128)(2,1)}) fusion(bf16[2,256,2048]{2,1,0:T(8,128)(2,1)S(1)} %copy-done.37, f32[2048]{0:T(1024)S(1)} %copy-done.58, f32[512]{0:T(512)S(1)} %bitcast.219, f32[512,2048]{1,0:T(8,128)S(1)} %copy-done.40, ...), kind=kOutput, calls=%fused_computation.20 | convolution fusion | flops 550499840 | bytes 26499072 | tf_op jit(solution)/shard_map/dot_general | solution.py:22
  494.8 2.3 collective-permute-done.47
  498.5 6.8 %fusion.17 = f32[512,2048]{1,0:T(8,128)} fusion(bf16[2,256,2048]{2,1,0:T(8,128)(2,1)} %param.12, bf16[512,2048]{1,0:T(8,128)(2,1)} %copy-done.38, f32[512,2048]{1,0:T(8,128)} %get-tuple-element.298, f32[512]{0:T(512)S(1)} %broadcast_multiply_fusion, f32[2048]{0:T(1024)S(1)} %copy-done.58, f32[512]{0:T(512)S(1)} %bitcast.220), kind=kLoop, calls=%fused_computation.23 | loop fusion | flops 8388608 | bytes 12595200 | tf_op jit(solution)/shard_map/add | solution.py:961
  507.6 10.6 %collective-permute-done.44.refs_6_ = f32[512,128]{1,0:T(8,128)S(1)} collective-permute-done((f32[512,128]{1,0:T(8,128)S(1)}, f32[512,128]{1,0:T(8,128)S(1)}, u32[]{:S(2)}, u32[]{:S(2)}) %collective-permute-start.44) | collective-permute-done | bytes 262176 | tf_op jit(solution)/shard_map/ppermute | solution.py:465
  523.1 12.4 %collective-permute-start.51 = (f32[15712]{0:T(1024)S(1)}, f32[15712]{0:T(1024)S(1)}, u32[]{:S(2)}, u32[]{:S(2)}) collective-permute-start(f32[15712]{0:T(1024)S(1)} %add_add_fusion.2), channel_id=1, source_target_pairs={{0,8},{8,0},{16,24},{24,16},{1,9},{9,1},{17,25},{25,17},{2,10},{10... | collective-permute-start | bytes 188552 | tf_op jit(solution)/shard_map/ppermute | solution.py:465
  539.1 2.3 finish.1
  (340 shorter events, 131.2 us)
Async XLA Ops:
  7.2 364.8 %reduce-scatter.3.cloned.1.call-start = ((), (), s32[]{:S(2)}) async-start(), calls=%async_computation.2 | async-start | bytes 5242880 | tf_op jit(solution)/shard_map/reduce_scatter | solution.py:603
  32.1 15.5 %collective-permute-start = (f32[2,8,2304]{2,1,0:T(8,128)S(1)}, f32[2,8,2304]{2,1,0:T(8,128)S(1)}, u32[]{:S(2)}, u32[]{:S(2)}) collective-permute-start(f32[2,8,2304]{2,1,0:T(8,128)S(1)} %pad_maximum_fusion.6), channel_id=1, source_target_pairs={{0,2},{2,4},{4,6},{1,3},{3,5},{5,7},{8,10},{10,12},{12,14},{9,11},... | collective-permute-start | bytes 442376 | tf_op jit(solution)/shard_map/ppermute | solution.py:471
  38.8 25.6 %collective-permute-start.1 = (f32[512,512]{1,0:T(8,128)}, f32[512,512]{1,0:T(8,128)S(1)}, u32[]{:S(2)}, u32[]{:S(2)}) collective-permute-start(f32[512,512]{1,0:T(8,128)} %get-tuple-element.167), channel_id=1, source_target_pairs={{0,2},{2,0},{4,6},{6,4},{1,3},{3,1},{5,7},{7,5},{8,10},{10,8},{12,... | collective-permute-start | bytes 3145736 | tf_op jit(solution)/shard_map/ppermute | solution.py:465
  40.3 24.6 %collective-permute-start.2 = (f32[512,512]{1,0:T(8,128)}, f32[512,512]{1,0:T(8,128)}, u32[]{:S(2)}, u32[]{:S(2)}) collective-permute-start(f32[512,512]{1,0:T(8,128)} %get-tuple-element.169), channel_id=1, source_target_pairs={{0,4},{2,6},{4,0},{6,2},{1,5},{3,7},{5,1},{7,3},{8,12},{10,14},{12... | collective-permute-start | bytes 3145736 | tf_op jit(solution)/shard_map/ppermute | solution.py:465
  45.9 71.4 %collective-permute-start.9 = (f32[512,1024]{1,0:T(8,128)}, f32[512,1024]{1,0:T(8,128)}, u32[]{:S(2)}, u32[]{:S(2)}) collective-permute-start(f32[512,1024]{1,0:T(8,128)} %dynamic-slice_convert_fusion), channel_id=1, source_target_pairs={{0,8},{8,0},{16,24},{24,16},{1,9},{9,1},{17,25},{25,17},{2,10},{10... | collective-permute-start | bytes 6291464 | tf_op jit(solution)/shard_map/ppermute | solution.py:465
  65.5 15.6 %collective-permute-start.3 = (f32[2,136,512]{2,1,0:T(8,128)S(1)}, f32[2,136,512]{2,1,0:T(8,128)S(1)}, u32[]{:S(2)}, u32[]{:S(2)}) collective-permute-start(f32[2,136,512]{2,1,0:T(8,128)S(1)} %get-tuple-element.317), channel_id=1, source_target_pairs={{0,2},{2,0},{4,6},{6,4},{1,3},{3,1},{5,7},{7,5},{8,10},{10,8},{12,... | collective-permute-start | bytes 1671176 | tf_op jit(solution)/shard_map/ppermute | solution.py:465
  66.1 14.9 %collective-permute-start.4 = (f32[2,136,512]{2,1,0:T(8,128)S(1)}, f32[2,136,512]{2,1,0:T(8,128)S(1)}, u32[]{:S(2)}, u32[]{:S(2)}) collective-permute-start(f32[2,136,512]{2,1,0:T(8,128)S(1)} %get-tuple-element.316), channel_id=1, source_target_pairs={{0,4},{2,6},{4,0},{6,2},{1,5},{3,7},{5,1},{7,3},{8,12},{10,14},{12... | collective-permute-start | bytes 1671176 | tf_op jit(solution)/shard_map/ppermute | solution.py:465
  67.5 24.1 %collective-permute-start.5 = (f32[2,136,512]{2,1,0:T(8,128)S(1)}, f32[2,136,512]{2,1,0:T(8,128)S(1)}, u32[]{:S(2)}, u32[]{:S(2)}) collective-permute-start(f32[2,136,512]{2,1,0:T(8,128)S(1)} %get-tuple-element.315), channel_id=1, source_target_pairs={{0,6},{2,4},{4,2},{6,0},{1,7},{3,5},{5,3},{7,1},{8,14},{10,12},{12... | collective-permute-start | bytes 1671176 | tf_op jit(solution)/shard_map/ppermute | solution.py:465
  92.6 14.9 %collective-permute-start.6 = (f32[2,128,512]{2,1,0:T(8,128)S(1)}, f32[2,128,512]{2,1,0:T(8,128)S(1)}, u32[]{:S(2)}, u32[]{:S(2)}) collective-permute-start(f32[2,128,512]{2,1,0:T(8,128)S(1)} %get-tuple-element.340), channel_id=1, source_target_pairs={{0,2},{2,0},{4,6},{6,4},{1,3},{3,1},{5,7},{7,5},{8,10},{10,8},{12,... | collective-permute-start | bytes 1572872 | tf_op jit(solution)/shard_map/ppermute | solution.py:465
  94.1 13.6 %collective-permute-start.7 = (f32[2,128,512]{2,1,0:T(8,128)S(1)}, f32[2,128,512]{2,1,0:T(8,128)S(1)}, u32[]{:S(2)}, u32[]{:S(2)}) collective-permute-start(f32[2,128,512]{2,1,0:T(8,128)S(1)} %get-tuple-element.339), channel_id=1, source_target_pairs={{0,4},{2,6},{4,0},{6,2},{1,5},{3,7},{5,1},{7,3},{8,12},{10,14},{12... | collective-permute-start | bytes 1572872 | tf_op jit(solution)/shard_map/ppermute | solution.py:465
  95.0 21.8 %collective-permute-start.8 = (f32[2,128,512]{2,1,0:T(8,128)S(1)}, f32[2,128,512]{2,1,0:T(8,128)S(1)}, u32[]{:S(2)}, u32[]{:S(2)}) collective-permute-start(f32[2,128,512]{2,1,0:T(8,128)S(1)} %get-tuple-element.299), channel_id=1, source_target_pairs={{0,6},{2,4},{4,2},{6,0},{1,7},{3,5},{5,3},{7,1},{8,14},{10,12},{12... | collective-permute-start | bytes 1572872 | tf_op jit(solution)/shard_map/ppermute | solution.py:465
  119.2 71.9 %collective-permute-start.15 = (f32[2,512,512]{2,1,0:T(8,128)S(1)}, f32[2,512,512]{2,1,0:T(8,128)S(1)}, u32[]{:S(2)}, u32[]{:S(2)}) collective-permute-start(f32[2,512,512]{2,1,0:T(8,128)S(1)} %pad_maximum_fusion.3), channel_id=1, source_target_pairs={{0,2},{2,0},{4,6},{6,4},{1,3},{3,1},{5,7},{7,5},{8,10},{10,8},{12,... | collective-permute-start | bytes 6291464 | tf_op jit(solution)/shard_map/ppermute | solution.py:465
  123.1 68.0 %collective-permute-start.14 = (f32[2,512,512]{2,1,0:T(8,128)}, f32[2,512,512]{2,1,0:T(8,128)}, u32[]{:S(2)}, u32[]{:S(2)}) collective-permute-start(f32[2,512,512]{2,1,0:T(8,128)} %pad_maximum_fusion.2), channel_id=1, source_target_pairs={{0,4},{2,6},{4,0},{6,2},{1,5},{3,7},{5,1},{7,3},{8,12},{10,14},{12... | collective-permute-start | bytes 6291464 | tf_op jit(solution)/shard_map/ppermute | solution.py:465
  152.9 26.9 %collective-permute-start.11 = (f32[2,136,512]{2,1,0:T(8,128)}, f32[2,136,512]{2,1,0:T(8,128)S(1)}, u32[]{:S(2)}, u32[]{:S(2)}) collective-permute-start(f32[2,136,512]{2,1,0:T(8,128)} %get-tuple-element.310), channel_id=1, source_target_pairs={{0,2},{2,0},{4,6},{6,4},{1,3},{3,1},{5,7},{7,5},{8,10},{10,8},{12,... | collective-permute-start | bytes 1671176 | tf_op jit(solution)/shard_map/ppermute | solution.py:465
  153.4 37.7 %collective-permute-start.12 = (f32[2,136,512]{2,1,0:T(8,128)}, f32[2,136,512]{2,1,0:T(8,128)S(1)}, u32[]{:S(2)}, u32[]{:S(2)}) collective-permute-start(f32[2,136,512]{2,1,0:T(8,128)} %get-tuple-element.309), channel_id=1, source_target_pairs={{0,4},{2,6},{4,0},{6,2},{1,5},{3,7},{5,1},{7,3},{8,12},{10,14},{12... | collective-permute-start | bytes 1671176 | tf_op jit(solution)/shard_map/ppermute | solution.py:465
  154.6 36.5 %collective-permute-start.13 = (f32[2,136,512]{2,1,0:T(8,128)S(1)}, f32[2,136,512]{2,1,0:T(8,128)S(1)}, u32[]{:S(2)}, u32[]{:S(2)}) collective-permute-start(f32[2,136,512]{2,1,0:T(8,128)S(1)} %get-tuple-element.308), channel_id=1, source_target_pairs={{0,6},{2,4},{4,2},{6,0},{1,7},{3,5},{5,3},{7,1},{8,14},{10,12},{12... | collective-permute-start | bytes 1671176 | tf_op jit(solution)/shard_map/ppermute | solution.py:465
  196.9 15.5 %collective-permute-start.19 = (f32[3,512,1024]{2,1,0:T(8,128)}, f32[3,512,1024]{2,1,0:T(8,128)}, u32[]{:S(2)}, u32[]{:S(2)}) collective-permute-start(f32[3,512,1024]{2,1,0:T(8,128)} %maximum_maximum_fusion.mine), channel_id=1, source_target_pairs={{0,1},{1,0},{2,3},{3,2},{4,5},{5,4},{6,7},{7,6},{8,9},{9,8},{10,11... | collective-permute-start | bytes 18874376 | tf_op jit(solution)/shard_map/ppermute | solution.py:465
  199.2 21.4 %collective-permute-start.17 = (f32[2,128,512]{2,1,0:T(8,128)S(1)}, f32[2,128,512]{2,1,0:T(8,128)S(1)}, u32[]{:S(2)}, u32[]{:S(2)}) collective-permute-start(f32[2,128,512]{2,1,0:T(8,128)S(1)} %fusion.32), channel_id=1, source_target_pairs={{0,4},{2,6},{4,0},{6,2},{1,5},{3,7},{5,1},{7,3},{8,12},{10,14},{12... | collective-permute-start | bytes 1572872 | tf_op jit(solution)/shard_map/ppermute | solution.py:465
  200.4 20.3 %collective-permute-start.16 = (f32[2,128,512]{2,1,0:T(8,128)S(1)}, f32[2,128,512]{2,1,0:T(8,128)S(1)}, u32[]{:S(2)}, u32[]{:S(2)}) collective-permute-start(f32[2,128,512]{2,1,0:T(8,128)S(1)} %get-tuple-element.338), channel_id=1, source_target_pairs={{0,2},{2,0},{4,6},{6,4},{1,3},{3,1},{5,7},{7,5},{8,10},{10,8},{12,... | collective-permute-start | bytes 1572872 | tf_op jit(solution)/shard_map/ppermute | solution.py:465
  202.1 24.2 %collective-permute-start.18 = (f32[2,128,512]{2,1,0:T(8,128)S(1)}, f32[2,128,512]{2,1,0:T(8,128)S(1)}, u32[]{:S(2)}, u32[]{:S(2)}) collective-permute-start(f32[2,128,512]{2,1,0:T(8,128)S(1)} %get-tuple-element.336), channel_id=1, source_target_pairs={{0,6},{2,4},{4,2},{6,0},{1,7},{3,5},{5,3},{7,1},{8,14},{10,12},{12... | collective-permute-start | bytes 1572872 | tf_op jit(solution)/shard_map/ppermute | solution.py:465
  228.4 52.1 %collective-permute-start.23 = (f32[512,1024]{1,0:T(8,128)S(1)}, f32[512,1024]{1,0:T(8,128)S(1)}, u32[]{:S(2)}, u32[]{:S(2)}) collective-permute-start(f32[512,1024]{1,0:T(8,128)S(1)} %dynamic-slice_convert_fusion.3), channel_id=1, source_target_pairs={{0,8},{8,0},{16,24},{24,16},{1,9},{9,1},{17,25},{25,17},{2,10},{10... | collective-permute-start | bytes 6291464 | tf_op jit(solution)/shard_map/ppermute | solution.py:465
  231.9 28.7 %collective-permute-start.20 = (f32[512,512]{1,0:T(8,128)}, f32[512,512]{1,0:T(8,128)S(1)}, u32[]{:S(2)}, u32[]{:S(2)}) collective-permute-start(f32[512,512]{1,0:T(8,128)} %get-tuple-element.322), channel_id=1, source_target_pairs={{0,2},{2,0},{4,6},{6,4},{1,3},{3,1},{5,7},{7,5},{8,10},{10,8},{12,... | collective-permute-start | bytes 3145736 | tf_op jit(solution)/shard_map/ppermute | solution.py:465
  233.6 45.8 %collective-permute-start.21 = (f32[512,512]{1,0:T(8,128)}, f32[512,512]{1,0:T(8,128)S(1)}, u32[]{:S(2)}, u32[]{:S(2)}) collective-permute-start(f32[512,512]{1,0:T(8,128)} %get-tuple-element.321), channel_id=1, source_target_pairs={{0,4},{2,6},{4,0},{6,2},{1,5},{3,7},{5,1},{7,3},{8,12},{10,14},{12... | collective-permute-start | bytes 3145736 | tf_op jit(solution)/shard_map/ppermute | solution.py:465
  234.4 46.0 %collective-permute-start.22 = (f32[512,512]{1,0:T(8,128)}, f32[512,512]{1,0:T(8,128)S(1)}, u32[]{:S(2)}, u32[]{:S(2)}) collective-permute-start(f32[512,512]{1,0:T(8,128)} %get-tuple-element.320), channel_id=1, source_target_pairs={{0,6},{2,4},{4,2},{6,0},{1,7},{3,5},{5,3},{7,1},{8,14},{10,12},{12... | collective-permute-start | bytes 3145736 | tf_op jit(solution)/shard_map/ppermute | solution.py:465
  259.3 31.5 %collective-permute-start.24 = (f32[2,8,2048]{2,1,0:T(8,128)S(1)}, f32[2,8,2048]{2,1,0:T(8,128)S(1)}, u32[]{:S(2)}, u32[]{:S(2)}) collective-permute-start(f32[2,8,2048]{2,1,0:T(8,128)S(1)} %get-tuple-element.192), channel_id=1, source_target_pairs={{2,0},{4,2},{6,4},{3,1},{5,3},{7,5},{10,8},{12,10},{14,12},{11,9},... | collective-permute-start | bytes 393224 | tf_op jit(solution)/shard_map/ppermute | solution.py:471
  290.8 179.9 %reduce-scatter.5.cloned.1.call-start = ((), (), s32[]{:S(2)}) async-start(), calls=%async_computation.3 | async-start | bytes 5242880 | tf_op jit(solution)/shard_map/reduce_scatter | solution.py:603
  290.9 14.9 %collective-permute-start.28 = (f32[1,512,1024]{2,1,0:T(8,128)}, f32[1,512,1024]{2,1,0:T(8,128)}, u32[]{:S(2)}, u32[]{:S(2)}) collective-permute-start(f32[1,512,1024]{2,1,0:T(8,128)} %bitcast.24.mine), channel_id=1, source_target_pairs={{0,1},{1,0},{2,3},{3,2},{4,5},{5,4},{6,7},{7,6},{8,9},{9,8},{10,11... | collective-permute-start | bytes 6291464 | tf_op jit(solution)/shard_map/ppermute | solution.py:465
  299.9 26.3 %collective-permute-start.25 = (f32[512,512]{1,0:T(8,128)}, f32[512,512]{1,0:T(8,128)}, u32[]{:S(2)}, u32[]{:S(2)}) collective-permute-start(f32[512,512]{1,0:T(8,128)} %get-tuple-element.207), channel_id=1, source_target_pairs={{0,2},{2,0},{4,6},{6,4},{1,3},{3,1},{5,7},{7,5},{8,10},{10,8},{12,... | collective-permute-start | bytes 3145736 | tf_op jit(solution)/shard_map/ppermute | solution.py:465
  301.7 47.5 %collective-permute-start.26 = (f32[512,512]{1,0:T(8,128)}, f32[512,512]{1,0:T(8,128)}, u32[]{:S(2)}, u32[]{:S(2)}) collective-permute-start(f32[512,512]{1,0:T(8,128)} %get-tuple-element.208), channel_id=1, source_target_pairs={{0,4},{2,6},{4,0},{6,2},{1,5},{3,7},{5,1},{7,3},{8,12},{10,14},{12... | collective-permute-start | bytes 3145736 | tf_op jit(solution)/shard_map/ppermute | solution.py:465
  301.7 47.5 %collective-permute-start.27 = (f32[512,512]{1,0:T(8,128)}, f32[512,512]{1,0:T(8,128)}, u32[]{:S(2)}, u32[]{:S(2)}) collective-permute-start(f32[512,512]{1,0:T(8,128)} %get-tuple-element.209), channel_id=1, source_target_pairs={{0,6},{2,4},{4,2},{6,0},{1,7},{3,5},{5,3},{7,1},{8,14},{10,12},{12... | collective-permute-start | bytes 3145736 | tf_op jit(solution)/shard_map/ppermute | solution.py:465
  304.3 17.9 %collective-permute-start.29 = (f32[2,256,256]{2,1,0:T(8,128)}, f32[2,256,256]{2,1,0:T(8,128)}, u32[]{:S(2)}, u32[]{:S(2)}) collective-permute-start(f32[2,256,256]{2,1,0:T(8,128)} %pad_add_fusion), channel_id=1, source_target_pairs={{0,1},{1,0},{2,3},{3,2},{4,5},{5,4},{6,7},{7,6},{8,9},{9,8},{10,11... | collective-permute-start | bytes 1572872 | tf_op jit(solution)/shard_map/ppermute | solution.py:465
  359.3 54.5 %collective-permute-start.31 = (f32[2,2,1024,128]{3,2,1,0:T(8,128)}, f32[2,2,1024,128]{3,2,1,0:T(8,128)}, u32[]{:S(2)}, u32[]{:S(2)}) collective-permute-start(f32[2,2,1024,128]{3,2,1,0:T(8,128)} %get-tuple-element.221), channel_id=1, source_target_pairs={{0,4},{2,6},{4,0},{6,2},{1,5},{3,7},{5,1},{7,3},{8,12},{10,14},{12... | collective-permute-start | bytes 6291464 | tf_op jit(solution)/shard_map/ppermute | solution.py:465
  359.7 56.1 %collective-permute-start.30 = (f32[2,2,1024,128]{3,2,1,0:T(8,128)}, f32[2,2,1024,128]{3,2,1,0:T(8,128)}, u32[]{:S(2)}, u32[]{:S(2)}) collective-permute-start(f32[2,2,1024,128]{3,2,1,0:T(8,128)} %copy-done.26), channel_id=1, source_target_pairs={{0,2},{2,0},{4,6},{6,4},{1,3},{3,1},{5,7},{7,5},{8,10},{10,8},{12,... | collective-permute-start | bytes 6291464 | tf_op jit(solution)/shard_map/ppermute | solution.py:465
  370.7 38.1 %collective-permute-start.35 = (f32[2,8,256]{2,1,0:T(8,128)}, f32[2,8,256]{2,1,0:T(8,128)S(1)}, u32[]{:S(2)}, u32[]{:S(2)}) collective-permute-start(f32[2,8,256]{2,1,0:T(8,128)} %get-tuple-element.231), channel_id=1, source_target_pairs={{2,0},{4,2},{6,4},{3,1},{5,3},{7,5},{10,8},{12,10},{14,12},{11,9},... | collective-permute-start | bytes 49160 | tf_op jit(solution)/shard_map/ppermute | solution.py:471
  373.5 45.0 %collective-permute-start.32 = (f32[512,128]{1,0:T(8,128)S(1)}, f32[512,128]{1,0:T(8,128)S(1)}, u32[]{:S(2)}, u32[]{:S(2)}) collective-permute-start(f32[512,128]{1,0:T(8,128)S(1)} %get-tuple-element.350), channel_id=1, source_target_pairs={{0,2},{2,0},{4,6},{6,4},{1,3},{3,1},{5,7},{7,5},{8,10},{10,8},{12,... | collective-permute-start | bytes 786440 | tf_op jit(solution)/shard_map/ppermute | solution.py:465
  376.2 42.3 %collective-permute-start.33 = (f32[512,128]{1,0:T(8,128)S(1)}, f32[512,128]{1,0:T(8,128)S(1)}, u32[]{:S(2)}, u32[]{:S(2)}) collective-permute-start(f32[512,128]{1,0:T(8,128)S(1)} %get-tuple-element.349), channel_id=1, source_target_pairs={{0,4},{2,6},{4,0},{6,2},{1,5},{3,7},{5,1},{7,3},{8,12},{10,14},{12... | collective-permute-start | bytes 786440 | tf_op jit(solution)/shard_map/ppermute | solution.py:465
  419.5 46.9 %collective-permute-start.36 = (f32[2,1024,128]{2,1,0:T(8,128)}, f32[2,1024,128]{2,1,0:T(8,128)}, u32[]{:S(2)}, u32[]{:S(2)}) collective-permute-start(f32[2,1024,128]{2,1,0:T(8,128)} %slice_bitcast_fusion.1), channel_id=1, source_target_pairs={{0,4},{2,6},{4,0},{6,2},{1,5},{3,7},{5,1},{7,3},{8,12},{10,14},{12... | collective-permute-start | bytes 3145736 | tf_op jit(solution)/shard_map/ppermute | solution.py:465
  422.8 45.0 %collective-permute-start.37 = (f32[2,1024,128]{2,1,0:T(8,128)}, f32[2,1024,128]{2,1,0:T(8,128)}, u32[]{:S(2)}, u32[]{:S(2)}) collective-permute-start(f32[2,1024,128]{2,1,0:T(8,128)} %slice_bitcast_fusion), channel_id=1, source_target_pairs={{0,2},{2,0},{4,6},{6,4},{1,3},{3,1},{5,7},{7,5},{8,10},{10,8},{12,... | collective-permute-start | bytes 3145736 | tf_op jit(solution)/shard_map/ppermute | solution.py:465
  426.8 31.2 %collective-permute-start.38 = (f32[2,2,2,160,128]{4,3,0,2,1:T(8,128)S(1)}, f32[2,2,2,160,128]{4,3,0,2,1:T(8,128)}, u32[]{:S(2)}, u32[]{:S(2)}) collective-permute-start(f32[2,2,2,160,128]{4,3,0,2,1:T(8,128)S(1)} %dynamic-slice_bitcast_fusion), channel_id=1, source_target_pairs={{0,2},{2,0},{4,6},{6,4},{1,3},{3,1},{5,7},{7,5},{8,10},{10,8},{12,... | collective-permute-start | bytes 1966088 | tf_op jit(solution)/shard_map/ppermute | solution.py:465
  470.8 13.5 %collective-permute-start.50 = (f32[512,2048]{1,0:T(8,128)}, f32[512,2048]{1,0:T(8,128)}, u32[]{:S(2)}, u32[]{:S(2)}) collective-permute-start(f32[512,2048]{1,0:T(8,128)} %fusion.46), channel_id=1, source_target_pairs={{0,1},{1,0},{2,3},{3,2},{4,5},{5,4},{6,7},{7,6},{8,9},{9,8},{10,11... | collective-permute-start | bytes 12582920 | tf_op jit(solution)/shard_map/ppermute | solution.py:465
  474.7 43.5 %collective-permute-start.40 = (f32[1184,128]{1,0:T(8,128)}, f32[1184,128]{1,0:T(8,128)}, u32[]{:S(2)}, u32[]{:S(2)}) collective-permute-start(f32[1184,128]{1,0:T(8,128)} %get-tuple-element.303), channel_id=1, source_target_pairs={{0,8},{8,0},{16,24},{24,16},{1,9},{9,1},{17,25},{25,17},{2,10},{10... | collective-permute-start | bytes 1818632 | tf_op jit(solution)/shard_map/ppermute | solution.py:465
  476.2 43.8 %collective-permute-start.41 = (f32[1184,128]{1,0:T(8,128)}, f32[1184,128]{1,0:T(8,128)}, u32[]{:S(2)}, u32[]{:S(2)}) collective-permute-start(f32[1184,128]{1,0:T(8,128)} %get-tuple-element.302), channel_id=1, source_target_pairs={{0,16},{8,24},{16,0},{24,8},{1,17},{9,25},{17,1},{25,9},{2,18},{10... | collective-permute-start | bytes 1818632 | tf_op jit(solution)/shard_map/ppermute | solution.py:465
  478.9 41.1 %collective-permute-start.42 = (f32[1184,128]{1,0:T(8,128)S(1)}, f32[1184,128]{1,0:T(8,128)}, u32[]{:S(2)}, u32[]{:S(2)}) collective-permute-start(f32[1184,128]{1,0:T(8,128)S(1)} %get-tuple-element.301), channel_id=1, source_target_pairs={{0,24},{8,16},{16,8},{24,0},{1,25},{9,17},{17,9},{25,1},{2,26},{10... | collective-permute-start | bytes 1818632 | tf_op jit(solution)/shard_map/ppermute | solution.py:465
  481.1 13.4 %collective-permute-start.43 = (f32[512,128]{1,0:T(8,128)}, f32[512,128]{1,0:T(8,128)S(1)}, u32[]{:S(2)}, u32[]{:S(2)}) collective-permute-start(f32[512,128]{1,0:T(8,128)} %get-tuple-element.346), channel_id=1, source_target_pairs={{0,2},{2,0},{4,6},{6,4},{1,3},{3,1},{5,7},{7,5},{8,10},{10,8},{12,... | collective-permute-start | bytes 786440 | tf_op jit(solution)/shard_map/ppermute | solution.py:465
  494.5 10.8 %collective-permute-start.48 = (f32[15712]{0:T(1024)S(1)}, f32[15712]{0:T(1024)S(1)}, u32[]{:S(2)}, u32[]{:S(2)}) collective-permute-start(f32[15712]{0:T(1024)S(1)} %concatenate.49), channel_id=1, source_target_pairs={{0,4},{2,6},{4,0},{6,2},{1,5},{3,7},{5,1},{7,3},{8,12},{10,14},{12... | collective-permute-start | bytes 188552 | tf_op jit(solution)/shard_map/ppermute | solution.py:465
  505.3 12.9 %collective-permute-start.44 = (f32[512,128]{1,0:T(8,128)S(1)}, f32[512,128]{1,0:T(8,128)S(1)}, u32[]{:S(2)}, u32[]{:S(2)}) collective-permute-start(f32[512,128]{1,0:T(8,128)S(1)} %copy-done.57), channel_id=1, source_target_pairs={{0,4},{2,6},{4,0},{6,2},{1,5},{3,7},{5,1},{7,3},{8,12},{10,14},{12... | collective-permute-start | bytes 786440 | tf_op jit(solution)/shard_map/ppermute | solution.py:465
  507.0 11.2 %collective-permute-start.45 = (f32[512,128]{1,0:T(8,128)S(1)}, f32[512,128]{1,0:T(8,128)S(1)}, u32[]{:S(2)}, u32[]{:S(2)}) collective-permute-start(f32[512,128]{1,0:T(8,128)S(1)} %get-tuple-element.344), channel_id=1, source_target_pairs={{0,6},{2,4},{4,2},{6,0},{1,7},{3,5},{5,3},{7,1},{8,14},{10,12},{12... | collective-permute-start | bytes 786440 | tf_op jit(solution)/shard_map/ppermute | solution.py:465
  523.1 18.3 %collective-permute-start.51 = (f32[15712]{0:T(1024)S(1)}, f32[15712]{0:T(1024)S(1)}, u32[]{:S(2)}, u32[]{:S(2)}) collective-permute-start(f32[15712]{0:T(1024)S(1)} %add_add_fusion.2), channel_id=1, source_target_pairs={{0,8},{8,0},{16,24},{24,16},{1,9},{9,1},{17,25},{25,17},{2,10},{10... | collective-permute-start | bytes 188552 | tf_op jit(solution)/shard_map/ppermute | solution.py:465
  (79 other events, 642.6 us)
Sparse Core Ops, SparseCore 0:
  291.0 77.2 reduce-scatter.2
  370.6 77.2 reduce-scatter.4

commit v5 on v4

--- a/solution.py
+++ b/solution.py
@@ -439,15 +439,15 @@
             ahead = CONV - 1 - tap
             moved = pltpu.roll(later[seq], EDGE - ahead, 0)
             end = end + jnp.where(row >= EDGE - ahead, moved, 0.0) * taps[tap : tap + 1]
-        mended[seq] = jnp.concatenate([value[seq, : slots - 16], value[seq, slots - 16 :]], axis=0)
         last = jnp.concatenate([value[seq, slots - 16 :][: 16 - EDGE].astype(F32), end], axis=0).astype(BF16)
+        mended[seq, : slots - 16] = value[seq, : slots - 16]
         mended[seq, slots - 16 :] = last
-    for index, piece in enumerate(pieces):
-
-        @pl.when(pl.program_id(0) == index)
-        def _():
-            for seq in range(seqs):
-                piece[seq * slots : (seq + 1) * slots] = mended[seq].astype(F32)
+        for index, piece in enumerate(pieces):
+
+            @pl.when(pl.program_id(0) == index)
+            def _():
+                piece[seq * slots : (seq + 1) * slots - 16] = value[seq, : slots - 16].astype(F32)
+                piece[(seq + 1) * slots - 16 : (seq + 1) * slots] = last.astype(F32)
 
 
 def finish_kernel(place, *refs):

time: 560 us -> 560 us (level)
  no operation moved by 1% of the time
where the time goes in v5:
time: 560 us; the launch traced here: 553 us
  waiting for transfers between devices  156 us (28%)
  Pallas kernels  136 us (24%)
  starting transfers between devices  73.5 us (13%)
  matrix products  71.3 us (13%)
  local copies, waits for them, and re-layouts  50.7 us (9%)
  other arithmetic  50 us (9%)
  between operations  15.5 us (3%)
    pallas_call x14, Pallas kernels, call(): pl.pallas_call(kernel, grid_spec=pltpu.PrefetchScalarGridSpec(num_scalar_...  136 us
    ppermute x52, waiting for transfers between devices, swapped(): return lax.ppermute(value, axis, [(i, i ^ bit) for i in range(count)])  124 us
    ppermute x52, starting transfers between devices, swapped(): return lax.ppermute(value, axis, [(i, i ^ bit) for i in range(count)])  66 us
    dot_general x6, matrix products, mm(): lax.dot_general(a, b, (dims, ((), ())), precision=precision, preferred_el...  33.8 us
    ppermute x3, waiting for transfers between devices, shifted(): lax.ppermute(value, axis, [(source, source + steps) for source in range(i...  32 us
    dot_general x1, matrix products, per_device(): jnp.einsum('tjn,gjn->tg', grad_zx, gate_input_weight, preferred_element_t...  23.6 us
    unnamed x148, local copies, waits for them, and re-layouts  22.6 us
    dot_general x1, matrix products, per_device(): jnp.einsum('tg,gjn->tjn', normed, gate_input_weight, preferred_element_ty...  13.9 us
  transfers between devices with their start and end apart: 57, of which 24 were waited for; matrix products, arithmetic and copies ran while one was open for 21% of the time, Pallas kernels for 25%

profile of v5, /device:TPU:0, one launch (start us, length us, event | category | flops | bytes accessed | tf_op | source)
XLA Modules:
  0.0 553.1 jit_solution(11979837773551884197)
XLA Ops:
  7.2 2.2 fusion.18
  11.3 13.9 %fusion.2 = f32[512,2,2048]{2,0,1:T(8,128)S(1)} fusion(bf16[2048,2,2048]{2,1,0:T(2,128)(2,1)} %param.14, bf16[512,2048]{1,0:T(8,128)(2,1)S(1)} %fusion.12.own_rows), kind=kOutput, calls=%fused_computation.2 | convolution fusion | flops 8589934592 | bytes 27262976 | tf_op jit(solution)/shard_map/tg,gjn->tjn/dot_general | solution.py:739
  25.3 3.3 copy-done.35
  32.1 4.9 collective-permute-start
  47.7 11.4 %scan_state.1 = (f32[2,136,2048]{2,1,0:T(8,128)S(1)}, f32[2,256,2048]{2,1,0:T(8,128)}, f32[2,256,128]{2,1,0:T(8,128)S(1)}, f32[2,256,128]{2,1,0:T(8,128)S(1)}, f32[2,4,16,256]{3,2,1,0:T(8,128)S(1)}) custom-call(f32[2,2,256,2048]{3,2,1,0:T(8,128)} %bitcast.193, f32[2,8,2048]{2,1,0:T(8,128)S(1)} %slice.196.edge_x, f32[5,2048]{1,0:T(8,128)S(1)} %copy-done.29, ...), custom_call_target="tpu_custom_call" | custom-call | flops 4674999808 | bytes 8500000 | tf_op jit(solution)/shard_map/scan_state/pallas_call | solution.py:128
  59.1 5.3 collective-permute-done.1
  68.9 9.5 %fusion.45 = f32[512,2048]{1,0:T(8,128)} fusion(bf16[512,2048]{1,0:T(8,128)(2,1)S(1)} %copy-done.39, bf16[2048,2048]{1,0:T(8,128)(2,1)} %param.21), kind=kOutput, calls=%fused_computation.152 | convolution fusion | flops 4294967296 | bytes 14680064 | tf_op jit(solution)/shard_map/dot_general | solution.py:22
  78.4 2.6 collective-permute-done.3
  81.0 10.6 %collective-permute-done.5 = f32[2,136,512]{2,1,0:T(8,128)S(1)} collective-permute-done((f32[2,136,512]{2,1,0:T(8,128)S(1)}, f32[2,136,512]{2,1,0:T(8,128)S(1)}, u32[]{:S(2)}, u32[]{:S(2)}) %collective-permute-start.5) | collective-permute-done | bytes 557088 | tf_op jit(solution)/shard_map/ppermute | solution.py:465
  96.2 9.4 %scan_inside.1.local_out = f32[2,256,2048]{2,1,0:T(8,128)S(1)} custom-call(f32[2,256,2048]{2,1,0:T(8,128)} %get-tuple-element.137.u, f32[2,4,16,256]{3,2,1,0:T(8,128)S(1)} %get-tuple-element.140.steps, f32[4,8,3]{2,1,0:T(8,128)S(1)} %bitcast.189, f32[2,256,128]{2,1,0:T(8,128)S(1)} %get-tuple-element.141.b_act, f32[2,256,128]{2,1,0:T(8,128)S(1)} %get-tuple-element.148.c_act), custom_call_target="tpu_custom_call" | custom-call | flops 4950000128 | bytes 9000000 | tf_op jit(solution)/shard_map/scan_inside/pallas_call | solution.py:128
  107.7 9.0 %collective-permute-done.8 = f32[2,128,512]{2,1,0:T(8,128)S(1)} collective-permute-done((f32[2,128,512]{2,1,0:T(8,128)S(1)}, f32[2,128,512]{2,1,0:T(8,128)S(1)}, u32[]{:S(2)}, u32[]{:S(2)}) %collective-permute-start.8) | collective-permute-done | bytes 524320 | tf_op jit(solution)/shard_map/ppermute | solution.py:465
  120.4 2.7 pad_maximum_fusion.2
  124.3 11.3 %gate.1 = (f32[2,256,2048]{2,1,0:T(8,128)}, f32[2,8,256]{2,1,0:T(8,128)S(1)}) custom-call(f32[2,256,2048]{2,1,0:T(8,128)} %copy-done.2, f32[2,128,2048]{2,1,0:T(8,128)S(1)} %pad_maximum_fusion.1.entering, f32[2,256,128]{2,1,0:T(8,128)S(1)} %get-tuple-element.148.c_act, f32[2,4,16,256]{3,2,1,0:T(8,128)S(1)} %get-tuple-element.140.steps, ...), custom_call_target="tpu_custom_call" | custom-call | flops 4124999936 | bytes 7500000 | tf_op jit(solution)/shard_map/gate/pallas_call | solution.py:128
  136.7 11.8 %gate_back.1 = (bf16[2,256,2048]{2,1,0:T(8,128)(2,1)S(1)}, f32[2,256,2048]{2,1,0:T(8,128)}, bf16[2,256,2048]{2,1,0:T(8,128)(2,1)S(1)}, f32[2,1,2048]{2,1,0:T(1,128)S(1)}, f32[2,136,2048]{2,1,0:T(8,128)}) custom-call(f32[2,256,2048]{2,1,0:T(8,128)} %get-tuple-element.160.y, f32[2,2,256,2048]{3,2,1,0:T(8,128)} %bitcast.195, f32[2,256,2048]{2,1,0:T(8,128)} %bitcast.198, ...), custom_call_target="tpu_custom_call" | custom-call | flops 4674999808 | bytes 8500000 | tf_op jit(solution)/shard_map/gate_back/pallas_call | solution.py:128
  148.5 4.3 constant_dynamic-slice_fusion.1
  156.3 20.3 %scan_inside_back.1 = (f32[2,256,2048]{2,1,0:T(8,128)}, f32[2,256,256]{2,1,0:T(8,128)S(1)}) custom-call(f32[2,256,2048]{2,1,0:T(8,128)} %get-tuple-element.137.u, f32[2,4,16,256]{3,2,1,0:T(8,128)S(1)} %get-tuple-element.140.steps, f32[2,256,128]{2,1,0:T(8,128)S(1)} %get-tuple-element.141.b_act, f32[2,256,128]{2,1,0:T(8,128)S(1)} %get-tuple-element.148.c_act, ...), custom_call_target="tpu_custom_call" | custom-call | flops 7150000128 | bytes 13000000 | tf_op jit(solution)/shard_map/scan_inside_back/pallas_call | solution.py:128
  176.7 3.1 collective-permute-done.11
  179.7 11.4 %collective-permute-done.12 = f32[2,136,512]{2,1,0:T(8,128)S(1)} collective-permute-done((f32[2,136,512]{2,1,0:T(8,128)}, f32[2,136,512]{2,1,0:T(8,128)S(1)}, u32[]{:S(2)}, u32[]{:S(2)}) %collective-permute-start.12) | collective-permute-done | bytes 557088 | tf_op jit(solution)/shard_map/ppermute | solution.py:465
  192.3 4.6 maximum_maximum_fusion.mine
  203.1 9.4 %fusion.46 = f32[512,2048]{1,0:T(8,128)} fusion(bf16[512,2048]{1,0:T(8,128)(2,1)S(1)} %bitcast.176, bf16[2048,2048]{1,0:T(8,128)(2,1)} %param.21), kind=kOutput, calls=%fused_computation.153 | convolution fusion | flops 4294967296 | bytes 14680064 | tf_op jit(solution)/shard_map/dot_general | solution.py:22
  212.5 8.2 %assemble.2.far_rows = bf16[3,512,2048]{2,1,0:T(8,128)(2,1)} custom-call(f32[3,512,1024]{2,1,0:T(8,128)} %maximum_maximum_fusion.mine, f32[3,512,1024]{2,1,0:T(8,128)} %collective-permute-done.19.theirs, s32[1]{0:T(128)} %bitcast.21.side), custom_call_target="tpu_custom_call" | custom-call | flops 825000000 | bytes 1500000 | tf_op jit(solution)/shard_map/assemble/pallas_call | solution.py:128
  220.7 5.7 %collective-permute-done.18 = f32[2,128,512]{2,1,0:T(8,128)S(1)} collective-permute-done((f32[2,128,512]{2,1,0:T(8,128)S(1)}, f32[2,128,512]{2,1,0:T(8,128)S(1)}, u32[]{:S(2)}, u32[]{:S(2)}) %collective-permute-start.18) | collective-permute-done | bytes 524320 | tf_op jit(solution)/shard_map/ppermute | solution.py:465
  235.4 21.3 %scan_back.1 = (bf16[2,256,2048]{2,1,0:T(8,128)(2,1)S(1)}, f32[2,8,2048]{2,1,0:T(8,128)S(1)}, f32[2,8,2048]{2,1,0:T(8,128)S(1)}, f32[2,8,2048]{2,1,0:T(8,128)S(1...) custom-call(f32[2,256,2048]{2,1,0:T(8,128)} %get-tuple-element.137.u, ...), custom_call_target="tpu_custom_call" | custom-call | flops 9349999616 | bytes 17000000 | tf_op jit(solution)/shard_map/scan_back/pallas_call | solution.py:128
  260.6 18.8 %collective-permute-done.21.refs_2_ = f32[512,512]{1,0:T(8,128)S(1)} collective-permute-done((f32[512,512]{1,0:T(8,128)}, f32[512,512]{1,0:T(8,128)S(1)}, u32[]{:S(2)}, u32[]{:S(2)}) %collective-permute-start.21) | collective-permute-done | bytes 1048608 | tf_op jit(solution)/shard_map/ppermute | solution.py:465
  281.7 9.1 %weight_part.2 = f32[4,4,512,128]{3,2,1,0:T(8,128)} custom-call(bf16[512,2048]{1,0:T(8,128)(2,1)} %copy-done.34, bf16[3,512,2048]{2,1,0:T(8,128)(2,1)} %assemble.2.far_rows, f32[512,512]{1,0:T(8,128)S(1)} %get-tuple-element.194.refs_0_, f32[512,512]{1,0:T(8,128)S(1)} %collective-permute-done.20.refs_1_, f32[512,512]{1,0:T(8,128)S(1)} %collective-permute-done.21.refs_2_, ...), custom_call_target="tpu_custom_call" | custom-call | flops 275000000 | bytes 500000 | tf_op jit(solution)/shard_map/weight_part/pallas_call | solution.py:128
  294.1 5.9 %mend.1 = (bf16[2,256,2048]{2,1,0:T(8,128)(2,1)}, f32[512,512]{1,0:T(8,128)S(1)}, f32[512,512]{1,0:T(8,128)}, f32[512,512]{1,0:T(8,128)}, f32[512,512]{1,0:T(8,128)}) custom-call(s32[1]{0:T(128)} %bitcast.place, bf16[2,256,2048]{2,1,0:T(8,128)(2,1)} %copy-done.31, f32[2,8,2048]{2,1,0:T(8,128)S(1)} %copy-done.33, f32[2,8,2048]{2,1,0:T(8,128)S(1)} %copy-done.28, ...), custom_call_target="tpu_custom_call" | custom-call | flops 1100000000 | bytes 2000000 | tf_op jit(solution)/shard_map/mend/pallas_call | solution.py:128
  305.9 2.7 assemble.3
  309.9 11.0 %pair_part.1 = (f32[2,2,1024,128]{3,2,1,0:T(8,128)S(1)}, f32[2,2,1024,128]{3,2,1,0:T(8,128)S(1)}, f32[2,2,1024,128]{3,2,1,0:T(8,128)}, f32[2,2,1024,128]{3,2,1,0:T(8,128)}) custom-call(s32[1]{0:T(128)} %bitcast.place, bf16[512,2048]{1,0:T(8,128)(2,1)} %copy-done.38, bf16[512,2048]{1,0:T(8,128)(2,1)} %bitcast.173, ...), custom_call_target="tpu_custom_call" | custom-call | flops 275000000 | bytes 500000 | tf_op jit(solution)/shard_map/pair_part/pallas_call | solution.py:128
  324.2 2.1 collective-permute-done.25.refs_1_
  326.3 22.9 %collective-permute-done.26.refs_2_ = f32[512,512]{1,0:T(8,128)} collective-permute-done((f32[512,512]{1,0:T(8,128)}, f32[512,512]{1,0:T(8,128)}, u32[]{:S(2)}, u32[]{:S(2)}) %collective-permute-start.26) | collective-permute-done | bytes 1048608 | tf_op jit(solution)/shard_map/ppermute | solution.py:465
  349.2 10.1 %weight_part.3 = f32[4,4,512,128]{3,2,1,0:T(8,128)} custom-call(bf16[512,2048]{1,0:T(8,128)(2,1)} %copy-done.34, bf16[3,512,2048]{2,1,0:T(8,128)(2,1)} %assemble.2.far_rows, f32[512,512]{1,0:T(8,128)S(1)} %get-tuple-element.223.refs_0_, f32[512,512]{1,0:T(8,128)} %collective-permute-done.25.refs_1_, f32[512,512]{1,0:T(8,128)} %collective-permute-done.26.refs_2_, ...), custom_call_target="tpu_custom_call" | custom-call | flops 275000000 | bytes 500000 | tf_op jit(solution)/shard_map/weight_part/pallas_call | solution.py:128
  361.1 3.9 copy.57
  373.5 2.7 collective-permute-start.32
  376.8 32.0 %collective-permute-done.35 = f32[2,8,256]{2,1,0:T(8,128)S(1)} collective-permute-done((f32[2,8,256]{2,1,0:T(8,128)}, f32[2,8,256]{2,1,0:T(8,128)S(1)}, u32[]{:S(2)}, u32[]{:S(2)}) %collective-permute-start.35) | collective-permute-done | bytes 16416 | tf_op jit(solution)/shard_map/ppermute | solution.py:471
  415.8 2.6 add.296
  419.5 2.2 collective-permute-start.36
  428.5 23.6 %fusion = f32[512,2048,1]{1,0,2:T(8,128)S(1)} fusion(bf16[2048,2,2048]{2,1,0:T(2,128)(2,1)} %param.14, bf16[512,1,2048]{2,0,1:T(8,128)(2,1)} %bitcast.226, bf16[512,1,2048]{2,0,1:T(8,128)(2,1)S(1)} %bitcast.175), kind=kOutput, calls=%fused_computation | convolution fusion | flops 8592031744 | bytes 25165824 | tf_op jit(solution)/shard_map/tjn,gjn->tg/dot_general | solution.py:947
  452.1 6.0 %collective-permute-done.38 = f32[2,2,2,160,128]{4,3,0,2,1:T(8,128)} collective-permute-done((f32[2,2,2,160,128]{4,3,0,2,1:T(8,128)S(1)}, f32[2,2,2,160,128]{4,3,0,2,1:T(8,128)}, u32[]{:S(2)}, u32[]{:S(2)}) %collective-permute-start.38) | collective-permute-done | bytes 655392 | tf_op jit(solution)/shard_map/ppermute | solution.py:465
  460.0 2.7 bitcast_add_fusion
  462.8 3.7 collective-permute-done.39
  471.8 3.0 dynamic-slice_bitcast_fusion.1
  476.3 2.7 collective-permute-start.41
  484.5 8.4 %fusion.14 = (f32[512]{0:T(512)S(1)}, f32[2048]{0:T(1024)S(1)}, f32[512,2048]{1,0:T(8,128)}, bf16[512,2048]{1,0:T(8,128)(2,1)}) fusion(bf16[2,256,2048]{2,1,0:T(8,128)(2,1)S(1)} %copy-done.37, f32[2048]{0:T(1024)S(1)} %copy-done.58, f32[512]{0:T(512)S(1)} %bitcast.219, f32[512,2048]{1,0:T(8,128)S(1)} %copy-done.40, ...), kind=kOutput, calls=%fused_computation.20 | convolution fusion | flops 550499840 | bytes 26499072 | tf_op jit(solution)/shard_map/dot_general | solution.py:22
  494.9 2.4 collective-permute-done.47
  498.6 6.8 %fusion.17 = f32[512,2048]{1,0:T(8,128)} fusion(bf16[2,256,2048]{2,1,0:T(8,128)(2,1)} %param.12, bf16[512,2048]{1,0:T(8,128)(2,1)} %copy-done.38, f32[512,2048]{1,0:T(8,128)} %get-tuple-element.298, f32[512]{0:T(512)S(1)} %broadcast_multiply_fusion, f32[2048]{0:T(1024)S(1)} %copy-done.58, f32[512]{0:T(512)S(1)} %bitcast.220), kind=kLoop, calls=%fused_computation.23 | loop fusion | flops 8388608 | bytes 12595200 | tf_op jit(solution)/shard_map/add | solution.py:961
  507.6 10.7 %collective-permute-done.44.refs_6_ = f32[512,128]{1,0:T(8,128)S(1)} collective-permute-done((f32[512,128]{1,0:T(8,128)S(1)}, f32[512,128]{1,0:T(8,128)S(1)}, u32[]{:S(2)}, u32[]{:S(2)}) %collective-permute-start.44) | collective-permute-done | bytes 262176 | tf_op jit(solution)/shard_map/ppermute | solution.py:465
  523.1 12.4 %collective-permute-start.51 = (f32[15712]{0:T(1024)S(1)}, f32[15712]{0:T(1024)S(1)}, u32[]{:S(2)}, u32[]{:S(2)}) collective-permute-start(f32[15712]{0:T(1024)S(1)} %add_add_fusion.2), channel_id=1, source_target_pairs={{0,8},{8,0},{16,24},{24,16},{1,9},{9,1},{17,25},{25,17},{2,10},{10... | collective-permute-start | bytes 188552 | tf_op jit(solution)/shard_map/ppermute | solution.py:465
  539.1 2.3 finish.1
  (340 shorter events, 130.8 us)
Async XLA Ops:
  7.2 364.8 %reduce-scatter.3.cloned.1.call-start = ((), (), s32[]{:S(2)}) async-start(), calls=%async_computation.2 | async-start | bytes 5242880 | tf_op jit(solution)/shard_map/reduce_scatter | solution.py:603
  32.1 15.5 %collective-permute-start = (f32[2,8,2304]{2,1,0:T(8,128)S(1)}, f32[2,8,2304]{2,1,0:T(8,128)S(1)}, u32[]{:S(2)}, u32[]{:S(2)}) collective-permute-start(f32[2,8,2304]{2,1,0:T(8,128)S(1)} %pad_maximum_fusion.6), channel_id=1, source_target_pairs={{0,2},{2,4},{4,6},{1,3},{3,5},{5,7},{8,10},{10,12},{12,14},{9,11},... | collective-permute-start | bytes 442376 | tf_op jit(solution)/shard_map/ppermute | solution.py:471
  38.8 25.6 %collective-permute-start.1 = (f32[512,512]{1,0:T(8,128)}, f32[512,512]{1,0:T(8,128)S(1)}, u32[]{:S(2)}, u32[]{:S(2)}) collective-permute-start(f32[512,512]{1,0:T(8,128)} %get-tuple-element.167), channel_id=1, source_target_pairs={{0,2},{2,0},{4,6},{6,4},{1,3},{3,1},{5,7},{7,5},{8,10},{10,8},{12,... | collective-permute-start | bytes 3145736 | tf_op jit(solution)/shard_map/ppermute | solution.py:465
  40.3 24.6 %collective-permute-start.2 = (f32[512,512]{1,0:T(8,128)}, f32[512,512]{1,0:T(8,128)}, u32[]{:S(2)}, u32[]{:S(2)}) collective-permute-start(f32[512,512]{1,0:T(8,128)} %get-tuple-element.169), channel_id=1, source_target_pairs={{0,4},{2,6},{4,0},{6,2},{1,5},{3,7},{5,1},{7,3},{8,12},{10,14},{12... | collective-permute-start | bytes 3145736 | tf_op jit(solution)/shard_map/ppermute | solution.py:465
  45.9 71.4 %collective-permute-start.9 = (f32[512,1024]{1,0:T(8,128)}, f32[512,1024]{1,0:T(8,128)}, u32[]{:S(2)}, u32[]{:S(2)}) collective-permute-start(f32[512,1024]{1,0:T(8,128)} %dynamic-slice_convert_fusion), channel_id=1, source_target_pairs={{0,8},{8,0},{16,24},{24,16},{1,9},{9,1},{17,25},{25,17},{2,10},{10... | collective-permute-start | bytes 6291464 | tf_op jit(solution)/shard_map/ppermute | solution.py:465
  65.5 15.6 %collective-permute-start.3 = (f32[2,136,512]{2,1,0:T(8,128)S(1)}, f32[2,136,512]{2,1,0:T(8,128)S(1)}, u32[]{:S(2)}, u32[]{:S(2)}) collective-permute-start(f32[2,136,512]{2,1,0:T(8,128)S(1)} %get-tuple-element.317), channel_id=1, source_target_pairs={{0,2},{2,0},{4,6},{6,4},{1,3},{3,1},{5,7},{7,5},{8,10},{10,8},{12,... | collective-permute-start | bytes 1671176 | tf_op jit(solution)/shard_map/ppermute | solution.py:465
  66.1 14.9 %collective-permute-start.4 = (f32[2,136,512]{2,1,0:T(8,128)S(1)}, f32[2,136,512]{2,1,0:T(8,128)S(1)}, u32[]{:S(2)}, u32[]{:S(2)}) collective-permute-start(f32[2,136,512]{2,1,0:T(8,128)S(1)} %get-tuple-element.316), channel_id=1, source_target_pairs={{0,4},{2,6},{4,0},{6,2},{1,5},{3,7},{5,1},{7,3},{8,12},{10,14},{12... | collective-permute-start | bytes 1671176 | tf_op jit(solution)/shard_map/ppermute | solution.py:465
  67.5 24.1 %collective-permute-start.5 = (f32[2,136,512]{2,1,0:T(8,128)S(1)}, f32[2,136,512]{2,1,0:T(8,128)S(1)}, u32[]{:S(2)}, u32[]{:S(2)}) collective-permute-start(f32[2,136,512]{2,1,0:T(8,128)S(1)} %get-tuple-element.315), channel_id=1, source_target_pairs={{0,6},{2,4},{4,2},{6,0},{1,7},{3,5},{5,3},{7,1},{8,14},{10,12},{12... | collective-permute-start | bytes 1671176 | tf_op jit(solution)/shard_map/ppermute | solution.py:465
  92.6 14.9 %collective-permute-start.6 = (f32[2,128,512]{2,1,0:T(8,128)S(1)}, f32[2,128,512]{2,1,0:T(8,128)S(1)}, u32[]{:S(2)}, u32[]{:S(2)}) collective-permute-start(f32[2,128,512]{2,1,0:T(8,128)S(1)} %get-tuple-element.340), channel_id=1, source_target_pairs={{0,2},{2,0},{4,6},{6,4},{1,3},{3,1},{5,7},{7,5},{8,10},{10,8},{12,... | collective-permute-start | bytes 1572872 | tf_op jit(solution)/shard_map/ppermute | solution.py:465
  94.1 13.6 %collective-permute-start.7 = (f32[2,128,512]{2,1,0:T(8,128)S(1)}, f32[2,128,512]{2,1,0:T(8,128)S(1)}, u32[]{:S(2)}, u32[]{:S(2)}) collective-permute-start(f32[2,128,512]{2,1,0:T(8,128)S(1)} %get-tuple-element.339), channel_id=1, source_target_pairs={{0,4},{2,6},{4,0},{6,2},{1,5},{3,7},{5,1},{7,3},{8,12},{10,14},{12... | collective-permute-start | bytes 1572872 | tf_op jit(solution)/shard_map/ppermute | solution.py:465
  95.0 21.8 %collective-permute-start.8 = (f32[2,128,512]{2,1,0:T(8,128)S(1)}, f32[2,128,512]{2,1,0:T(8,128)S(1)}, u32[]{:S(2)}, u32[]{:S(2)}) collective-permute-start(f32[2,128,512]{2,1,0:T(8,128)S(1)} %get-tuple-element.299), channel_id=1, source_target_pairs={{0,6},{2,4},{4,2},{6,0},{1,7},{3,5},{5,3},{7,1},{8,14},{10,12},{12... | collective-permute-start | bytes 1572872 | tf_op jit(solution)/shard_map/ppermute | solution.py:465
  119.2 71.9 %collective-permute-start.15 = (f32[2,512,512]{2,1,0:T(8,128)S(1)}, f32[2,512,512]{2,1,0:T(8,128)S(1)}, u32[]{:S(2)}, u32[]{:S(2)}) collective-permute-start(f32[2,512,512]{2,1,0:T(8,128)S(1)} %pad_maximum_fusion.3), channel_id=1, source_target_pairs={{0,2},{2,0},{4,6},{6,4},{1,3},{3,1},{5,7},{7,5},{8,10},{10,8},{12,... | collective-permute-start | bytes 6291464 | tf_op jit(solution)/shard_map/ppermute | solution.py:465
  123.1 68.0 %collective-permute-start.14 = (f32[2,512,512]{2,1,0:T(8,128)}, f32[2,512,512]{2,1,0:T(8,128)}, u32[]{:S(2)}, u32[]{:S(2)}) collective-permute-start(f32[2,512,512]{2,1,0:T(8,128)} %pad_maximum_fusion.2), channel_id=1, source_target_pairs={{0,4},{2,6},{4,0},{6,2},{1,5},{3,7},{5,1},{7,3},{8,12},{10,14},{12... | collective-permute-start | bytes 6291464 | tf_op jit(solution)/shard_map/ppermute | solution.py:465
  152.9 26.9 %collective-permute-start.11 = (f32[2,136,512]{2,1,0:T(8,128)}, f32[2,136,512]{2,1,0:T(8,128)S(1)}, u32[]{:S(2)}, u32[]{:S(2)}) collective-permute-start(f32[2,136,512]{2,1,0:T(8,128)} %get-tuple-element.310), channel_id=1, source_target_pairs={{0,2},{2,0},{4,6},{6,4},{1,3},{3,1},{5,7},{7,5},{8,10},{10,8},{12,... | collective-permute-start | bytes 1671176 | tf_op jit(solution)/shard_map/ppermute | solution.py:465
  153.4 37.7 %collective-permute-start.12 = (f32[2,136,512]{2,1,0:T(8,128)}, f32[2,136,512]{2,1,0:T(8,128)S(1)}, u32[]{:S(2)}, u32[]{:S(2)}) collective-permute-start(f32[2,136,512]{2,1,0:T(8,128)} %get-tuple-element.309), channel_id=1, source_target_pairs={{0,4},{2,6},{4,0},{6,2},{1,5},{3,7},{5,1},{7,3},{8,12},{10,14},{12... | collective-permute-start | bytes 1671176 | tf_op jit(solution)/shard_map/ppermute | solution.py:465
  154.6 36.5 %collective-permute-start.13 = (f32[2,136,512]{2,1,0:T(8,128)S(1)}, f32[2,136,512]{2,1,0:T(8,128)S(1)}, u32[]{:S(2)}, u32[]{:S(2)}) collective-permute-start(f32[2,136,512]{2,1,0:T(8,128)S(1)} %get-tuple-element.308), channel_id=1, source_target_pairs={{0,6},{2,4},{4,2},{6,0},{1,7},{3,5},{5,3},{7,1},{8,14},{10,12},{12... | collective-permute-start | bytes 1671176 | tf_op jit(solution)/shard_map/ppermute | solution.py:465
  196.9 15.5 %collective-permute-start.19 = (f32[3,512,1024]{2,1,0:T(8,128)}, f32[3,512,1024]{2,1,0:T(8,128)}, u32[]{:S(2)}, u32[]{:S(2)}) collective-permute-start(f32[3,512,1024]{2,1,0:T(8,128)} %maximum_maximum_fusion.mine), channel_id=1, source_target_pairs={{0,1},{1,0},{2,3},{3,2},{4,5},{5,4},{6,7},{7,6},{8,9},{9,8},{10,11... | collective-permute-start | bytes 18874376 | tf_op jit(solution)/shard_map/ppermute | solution.py:465
  199.2 21.4 %collective-permute-start.17 = (f32[2,128,512]{2,1,0:T(8,128)S(1)}, f32[2,128,512]{2,1,0:T(8,128)S(1)}, u32[]{:S(2)}, u32[]{:S(2)}) collective-permute-start(f32[2,128,512]{2,1,0:T(8,128)S(1)} %fusion.32), channel_id=1, source_target_pairs={{0,4},{2,6},{4,0},{6,2},{1,5},{3,7},{5,1},{7,3},{8,12},{10,14},{12... | collective-permute-start | bytes 1572872 | tf_op jit(solution)/shard_map/ppermute | solution.py:465
  200.4 20.3 %collective-permute-start.16 = (f32[2,128,512]{2,1,0:T(8,128)S(1)}, f32[2,128,512]{2,1,0:T(8,128)S(1)}, u32[]{:S(2)}, u32[]{:S(2)}) collective-permute-start(f32[2,128,512]{2,1,0:T(8,128)S(1)} %get-tuple-element.338), channel_id=1, source_target_pairs={{0,2},{2,0},{4,6},{6,4},{1,3},{3,1},{5,7},{7,5},{8,10},{10,8},{12,... | collective-permute-start | bytes 1572872 | tf_op jit(solution)/shard_map/ppermute | solution.py:465
  202.1 24.2 %collective-permute-start.18 = (f32[2,128,512]{2,1,0:T(8,128)S(1)}, f32[2,128,512]{2,1,0:T(8,128)S(1)}, u32[]{:S(2)}, u32[]{:S(2)}) collective-permute-start(f32[2,128,512]{2,1,0:T(8,128)S(1)} %get-tuple-element.336), channel_id=1, source_target_pairs={{0,6},{2,4},{4,2},{6,0},{1,7},{3,5},{5,3},{7,1},{8,14},{10,12},{12... | collective-permute-start | bytes 1572872 | tf_op jit(solution)/shard_map/ppermute | solution.py:465
  228.4 52.1 %collective-permute-start.23 = (f32[512,1024]{1,0:T(8,128)S(1)}, f32[512,1024]{1,0:T(8,128)S(1)}, u32[]{:S(2)}, u32[]{:S(2)}) collective-permute-start(f32[512,1024]{1,0:T(8,128)S(1)} %dynamic-slice_convert_fusion.3), channel_id=1, source_target_pairs={{0,8},{8,0},{16,24},{24,16},{1,9},{9,1},{17,25},{25,17},{2,10},{10... | collective-permute-start | bytes 6291464 | tf_op jit(solution)/shard_map/ppermute | solution.py:465
  231.9 28.7 %collective-permute-start.20 = (f32[512,512]{1,0:T(8,128)}, f32[512,512]{1,0:T(8,128)S(1)}, u32[]{:S(2)}, u32[]{:S(2)}) collective-permute-start(f32[512,512]{1,0:T(8,128)} %get-tuple-element.322), channel_id=1, source_target_pairs={{0,2},{2,0},{4,6},{6,4},{1,3},{3,1},{5,7},{7,5},{8,10},{10,8},{12,... | collective-permute-start | bytes 3145736 | tf_op jit(solution)/shard_map/ppermute | solution.py:465
  233.6 45.8 %collective-permute-start.21 = (f32[512,512]{1,0:T(8,128)}, f32[512,512]{1,0:T(8,128)S(1)}, u32[]{:S(2)}, u32[]{:S(2)}) collective-permute-start(f32[512,512]{1,0:T(8,128)} %get-tuple-element.321), channel_id=1, source_target_pairs={{0,4},{2,6},{4,0},{6,2},{1,5},{3,7},{5,1},{7,3},{8,12},{10,14},{12... | collective-permute-start | bytes 3145736 | tf_op jit(solution)/shard_map/ppermute | solution.py:465
  234.4 46.0 %collective-permute-start.22 = (f32[512,512]{1,0:T(8,128)}, f32[512,512]{1,0:T(8,128)S(1)}, u32[]{:S(2)}, u32[]{:S(2)}) collective-permute-start(f32[512,512]{1,0:T(8,128)} %get-tuple-element.320), channel_id=1, source_target_pairs={{0,6},{2,4},{4,2},{6,0},{1,7},{3,5},{5,3},{7,1},{8,14},{10,12},{12... | collective-permute-start | bytes 3145736 | tf_op jit(solution)/shard_map/ppermute | solution.py:465
  259.3 31.5 %collective-permute-start.24 = (f32[2,8,2048]{2,1,0:T(8,128)S(1)}, f32[2,8,2048]{2,1,0:T(8,128)S(1)}, u32[]{:S(2)}, u32[]{:S(2)}) collective-permute-start(f32[2,8,2048]{2,1,0:T(8,128)S(1)} %get-tuple-element.192), channel_id=1, source_target_pairs={{2,0},{4,2},{6,4},{3,1},{5,3},{7,5},{10,8},{12,10},{14,12},{11,9},... | collective-permute-start | bytes 393224 | tf_op jit(solution)/shard_map/ppermute | solution.py:471
  290.8 180.1 %reduce-scatter.5.cloned.1.call-start = ((), (), s32[]{:S(2)}) async-start(), calls=%async_computation.3 | async-start | bytes 5242880 | tf_op jit(solution)/shard_map/reduce_scatter | solution.py:603
  290.9 15.0 %collective-permute-start.28 = (f32[1,512,1024]{2,1,0:T(8,128)}, f32[1,512,1024]{2,1,0:T(8,128)}, u32[]{:S(2)}, u32[]{:S(2)}) collective-permute-start(f32[1,512,1024]{2,1,0:T(8,128)} %bitcast.24.mine), channel_id=1, source_target_pairs={{0,1},{1,0},{2,3},{3,2},{4,5},{5,4},{6,7},{7,6},{8,9},{9,8},{10,11... | collective-permute-start | bytes 6291464 | tf_op jit(solution)/shard_map/ppermute | solution.py:465
  300.0 26.3 %collective-permute-start.25 = (f32[512,512]{1,0:T(8,128)}, f32[512,512]{1,0:T(8,128)}, u32[]{:S(2)}, u32[]{:S(2)}) collective-permute-start(f32[512,512]{1,0:T(8,128)} %get-tuple-element.207), channel_id=1, source_target_pairs={{0,2},{2,0},{4,6},{6,4},{1,3},{3,1},{5,7},{7,5},{8,10},{10,8},{12,... | collective-permute-start | bytes 3145736 | tf_op jit(solution)/shard_map/ppermute | solution.py:465
  301.7 47.5 %collective-permute-start.26 = (f32[512,512]{1,0:T(8,128)}, f32[512,512]{1,0:T(8,128)}, u32[]{:S(2)}, u32[]{:S(2)}) collective-permute-start(f32[512,512]{1,0:T(8,128)} %get-tuple-element.208), channel_id=1, source_target_pairs={{0,4},{2,6},{4,0},{6,2},{1,5},{3,7},{5,1},{7,3},{8,12},{10,14},{12... | collective-permute-start | bytes 3145736 | tf_op jit(solution)/shard_map/ppermute | solution.py:465
  301.7 47.5 %collective-permute-start.27 = (f32[512,512]{1,0:T(8,128)}, f32[512,512]{1,0:T(8,128)}, u32[]{:S(2)}, u32[]{:S(2)}) collective-permute-start(f32[512,512]{1,0:T(8,128)} %get-tuple-element.209), channel_id=1, source_target_pairs={{0,6},{2,4},{4,2},{6,0},{1,7},{3,5},{5,3},{7,1},{8,14},{10,12},{12... | collective-permute-start | bytes 3145736 | tf_op jit(solution)/shard_map/ppermute | solution.py:465
  304.3 17.9 %collective-permute-start.29 = (f32[2,256,256]{2,1,0:T(8,128)}, f32[2,256,256]{2,1,0:T(8,128)}, u32[]{:S(2)}, u32[]{:S(2)}) collective-permute-start(f32[2,256,256]{2,1,0:T(8,128)} %pad_add_fusion), channel_id=1, source_target_pairs={{0,1},{1,0},{2,3},{3,2},{4,5},{5,4},{6,7},{7,6},{8,9},{9,8},{10,11... | collective-permute-start | bytes 1572872 | tf_op jit(solution)/shard_map/ppermute | solution.py:465
  359.4 54.5 %collective-permute-start.31 = (f32[2,2,1024,128]{3,2,1,0:T(8,128)}, f32[2,2,1024,128]{3,2,1,0:T(8,128)}, u32[]{:S(2)}, u32[]{:S(2)}) collective-permute-start(f32[2,2,1024,128]{3,2,1,0:T(8,128)} %get-tuple-element.221), channel_id=1, source_target_pairs={{0,4},{2,6},{4,0},{6,2},{1,5},{3,7},{5,1},{7,3},{8,12},{10,14},{12... | collective-permute-start | bytes 6291464 | tf_op jit(solution)/shard_map/ppermute | solution.py:465
  359.7 56.1 %collective-permute-start.30 = (f32[2,2,1024,128]{3,2,1,0:T(8,128)}, f32[2,2,1024,128]{3,2,1,0:T(8,128)}, u32[]{:S(2)}, u32[]{:S(2)}) collective-permute-start(f32[2,2,1024,128]{3,2,1,0:T(8,128)} %copy-done.26), channel_id=1, source_target_pairs={{0,2},{2,0},{4,6},{6,4},{1,3},{3,1},{5,7},{7,5},{8,10},{10,8},{12,... | collective-permute-start | bytes 6291464 | tf_op jit(solution)/shard_map/ppermute | solution.py:465
  370.7 38.2 %collective-permute-start.35 = (f32[2,8,256]{2,1,0:T(8,128)}, f32[2,8,256]{2,1,0:T(8,128)S(1)}, u32[]{:S(2)}, u32[]{:S(2)}) collective-permute-start(f32[2,8,256]{2,1,0:T(8,128)} %get-tuple-element.231), channel_id=1, source_target_pairs={{2,0},{4,2},{6,4},{3,1},{5,3},{7,5},{10,8},{12,10},{14,12},{11,9},... | collective-permute-start | bytes 49160 | tf_op jit(solution)/shard_map/ppermute | solution.py:471
  373.5 45.0 %collective-permute-start.32 = (f32[512,128]{1,0:T(8,128)S(1)}, f32[512,128]{1,0:T(8,128)S(1)}, u32[]{:S(2)}, u32[]{:S(2)}) collective-permute-start(f32[512,128]{1,0:T(8,128)S(1)} %get-tuple-element.350), channel_id=1, source_target_pairs={{0,2},{2,0},{4,6},{6,4},{1,3},{3,1},{5,7},{7,5},{8,10},{10,8},{12,... | collective-permute-start | bytes 786440 | tf_op jit(solution)/shard_map/ppermute | solution.py:465
  376.2 42.3 %collective-permute-start.33 = (f32[512,128]{1,0:T(8,128)S(1)}, f32[512,128]{1,0:T(8,128)S(1)}, u32[]{:S(2)}, u32[]{:S(2)}) collective-permute-start(f32[512,128]{1,0:T(8,128)S(1)} %get-tuple-element.349), channel_id=1, source_target_pairs={{0,4},{2,6},{4,0},{6,2},{1,5},{3,7},{5,1},{7,3},{8,12},{10,14},{12... | collective-permute-start | bytes 786440 | tf_op jit(solution)/shard_map/ppermute | solution.py:465
  419.5 47.0 %collective-permute-start.36 = (f32[2,1024,128]{2,1,0:T(8,128)}, f32[2,1024,128]{2,1,0:T(8,128)}, u32[]{:S(2)}, u32[]{:S(2)}) collective-permute-start(f32[2,1024,128]{2,1,0:T(8,128)} %slice_bitcast_fusion.1), channel_id=1, source_target_pairs={{0,4},{2,6},{4,0},{6,2},{1,5},{3,7},{5,1},{7,3},{8,12},{10,14},{12... | collective-permute-start | bytes 3145736 | tf_op jit(solution)/shard_map/ppermute | solution.py:465
  422.8 45.1 %collective-permute-start.37 = (f32[2,1024,128]{2,1,0:T(8,128)}, f32[2,1024,128]{2,1,0:T(8,128)}, u32[]{:S(2)}, u32[]{:S(2)}) collective-permute-start(f32[2,1024,128]{2,1,0:T(8,128)} %slice_bitcast_fusion), channel_id=1, source_target_pairs={{0,2},{2,0},{4,6},{6,4},{1,3},{3,1},{5,7},{7,5},{8,10},{10,8},{12,... | collective-permute-start | bytes 3145736 | tf_op jit(solution)/shard_map/ppermute | solution.py:465
  426.8 31.3 %collective-permute-start.38 = (f32[2,2,2,160,128]{4,3,0,2,1:T(8,128)S(1)}, f32[2,2,2,160,128]{4,3,0,2,1:T(8,128)}, u32[]{:S(2)}, u32[]{:S(2)}) collective-permute-start(f32[2,2,2,160,128]{4,3,0,2,1:T(8,128)S(1)} %dynamic-slice_bitcast_fusion), channel_id=1, source_target_pairs={{0,2},{2,0},{4,6},{6,4},{1,3},{3,1},{5,7},{7,5},{8,10},{10,8},{12,... | collective-permute-start | bytes 1966088 | tf_op jit(solution)/shard_map/ppermute | solution.py:465
  470.9 13.5 %collective-permute-start.50 = (f32[512,2048]{1,0:T(8,128)}, f32[512,2048]{1,0:T(8,128)}, u32[]{:S(2)}, u32[]{:S(2)}) collective-permute-start(f32[512,2048]{1,0:T(8,128)} %fusion.46), channel_id=1, source_target_pairs={{0,1},{1,0},{2,3},{3,2},{4,5},{5,4},{6,7},{7,6},{8,9},{9,8},{10,11... | collective-permute-start | bytes 12582920 | tf_op jit(solution)/shard_map/ppermute | solution.py:465
  474.8 43.4 %collective-permute-start.40 = (f32[1184,128]{1,0:T(8,128)}, f32[1184,128]{1,0:T(8,128)}, u32[]{:S(2)}, u32[]{:S(2)}) collective-permute-start(f32[1184,128]{1,0:T(8,128)} %get-tuple-element.303), channel_id=1, source_target_pairs={{0,8},{8,0},{16,24},{24,16},{1,9},{9,1},{17,25},{25,17},{2,10},{10... | collective-permute-start | bytes 1818632 | tf_op jit(solution)/shard_map/ppermute | solution.py:465
  476.3 43.8 %collective-permute-start.41 = (f32[1184,128]{1,0:T(8,128)}, f32[1184,128]{1,0:T(8,128)}, u32[]{:S(2)}, u32[]{:S(2)}) collective-permute-start(f32[1184,128]{1,0:T(8,128)} %get-tuple-element.302), channel_id=1, source_target_pairs={{0,16},{8,24},{16,0},{24,8},{1,17},{9,25},{17,1},{25,9},{2,18},{10... | collective-permute-start | bytes 1818632 | tf_op jit(solution)/shard_map/ppermute | solution.py:465
  478.9 41.1 %collective-permute-start.42 = (f32[1184,128]{1,0:T(8,128)S(1)}, f32[1184,128]{1,0:T(8,128)}, u32[]{:S(2)}, u32[]{:S(2)}) collective-permute-start(f32[1184,128]{1,0:T(8,128)S(1)} %get-tuple-element.301), channel_id=1, source_target_pairs={{0,24},{8,16},{16,8},{24,0},{1,25},{9,17},{17,9},{25,1},{2,26},{10... | collective-permute-start | bytes 1818632 | tf_op jit(solution)/shard_map/ppermute | solution.py:465
  481.3 13.3 %collective-permute-start.43 = (f32[512,128]{1,0:T(8,128)}, f32[512,128]{1,0:T(8,128)S(1)}, u32[]{:S(2)}, u32[]{:S(2)}) collective-permute-start(f32[512,128]{1,0:T(8,128)} %get-tuple-element.346), channel_id=1, source_target_pairs={{0,2},{2,0},{4,6},{6,4},{1,3},{3,1},{5,7},{7,5},{8,10},{10,8},{12,... | collective-permute-start | bytes 786440 | tf_op jit(solution)/shard_map/ppermute | solution.py:465
  494.5 10.8 %collective-permute-start.48 = (f32[15712]{0:T(1024)S(1)}, f32[15712]{0:T(1024)S(1)}, u32[]{:S(2)}, u32[]{:S(2)}) collective-permute-start(f32[15712]{0:T(1024)S(1)} %concatenate.49), channel_id=1, source_target_pairs={{0,4},{2,6},{4,0},{6,2},{1,5},{3,7},{5,1},{7,3},{8,12},{10,14},{12... | collective-permute-start | bytes 188552 | tf_op jit(solution)/shard_map/ppermute | solution.py:465
  505.3 12.9 %collective-permute-start.44 = (f32[512,128]{1,0:T(8,128)S(1)}, f32[512,128]{1,0:T(8,128)S(1)}, u32[]{:S(2)}, u32[]{:S(2)}) collective-permute-start(f32[512,128]{1,0:T(8,128)S(1)} %copy-done.57), channel_id=1, source_target_pairs={{0,4},{2,6},{4,0},{6,2},{1,5},{3,7},{5,1},{7,3},{8,12},{10,14},{12... | collective-permute-start | bytes 786440 | tf_op jit(solution)/shard_map/ppermute | solution.py:465
  507.0 11.2 %collective-permute-start.45 = (f32[512,128]{1,0:T(8,128)S(1)}, f32[512,128]{1,0:T(8,128)S(1)}, u32[]{:S(2)}, u32[]{:S(2)}) collective-permute-start(f32[512,128]{1,0:T(8,128)S(1)} %get-tuple-element.344), channel_id=1, source_target_pairs={{0,6},{2,4},{4,2},{6,0},{1,7},{3,5},{5,3},{7,1},{8,14},{10,12},{12... | collective-permute-start | bytes 786440 | tf_op jit(solution)/shard_map/ppermute | solution.py:465
  523.1 18.3 %collective-permute-start.51 = (f32[15712]{0:T(1024)S(1)}, f32[15712]{0:T(1024)S(1)}, u32[]{:S(2)}, u32[]{:S(2)}) collective-permute-start(f32[15712]{0:T(1024)S(1)} %add_add_fusion.2), channel_id=1, source_target_pairs={{0,8},{8,0},{16,24},{24,16},{1,9},{9,1},{17,25},{25,17},{2,10},{10... | collective-permute-start | bytes 188552 | tf_op jit(solution)/shard_map/ppermute | solution.py:465
  (79 other events, 642.7 us)
Sparse Core Ops, SparseCore 0:
  291.0 77.2 reduce-scatter.2
  370.6 77.2 reduce-scatter.4
